TPU v7x, 512 devices: a whole 4x8x8 slice. The times are simulated.
512 devices in a mesh: expert: 32 (over x, y), tensor: 16 (over z, core).
Axes of the slice: x: 4, y: 8, z: 8, core: 2. Of those that a mesh axis runs over, the one named last changes fastest.
Arguments:
- hidden: bfloat16 [160, 131072], P(None, ('expert', 'tensor')), may hold values from -6 to 6
- codes: bfloat16 [131072, 6144], P(('expert', 'tensor')), may hold values from -8 to 7, as said below
- scales: float32 [2048, 6144], P(('expert', 'tensor')), may hold values from 0.001 to 0.004
- signs: int32 [131072], P(('expert', 'tensor')), may hold values from 0 to 1
- lowrank_down_map: bfloat16 [131072, 64], P(('expert', 'tensor')), may hold values from -0.046875 to 0.046875
- lowrank_up_map: bfloat16 [8, 64, 6144], P(None, None, 'tensor'), may hold values from -0.75 to 0.75
- experts: int32 [512, 2], P('expert'), may hold values from 0 to 7, all different within a row; in each aligned block of 16 rows (0 to 15, 16 to 31, ...) at most 5 rows name the same one
- gates: float32 [512, 2], P('expert'), may hold values from 0.2 to 1
- output_gradient: bfloat16 [512, 6144], P('expert', 'tensor'), may hold values from -6 to 6
Outputs:
- mixed: bfloat16 [512, 6144], P('expert', 'tensor')
- hidden_gradient: bfloat16 [160, 131072], P(None, ('expert', 'tensor'))
- down_map_gradient: float32 [131072, 64], P(('expert', 'tensor'))
- up_map_gradient: float32 [8, 64, 6144], P(None, None, 'tensor')
- gates_gradient: float32 [512, 2], P('expert')
Inputs may be any that keep to these rules, and one draw needn't show every extreme that they name: The two experts of a token differ; among the 16 tokens of one index of the expert axis no expert is named more than 5 times, a bound that some block reaches. `codes`: whole numbers.
All inputs are finite; a program needn't handle non-finite values.
Results may differ from a plain program's by a relative error of at most 0.0056.
Values may be sent and summed in bfloat16 or wider, within the bound.
No kernel may reach another device: no remote copies, remote signals or barrier semaphores. Data moves between devices by JAX's collectives and lax.ppermute only.
A program may use at most 64 MiB of HBM per device.

v0:
```python
import math

import jax
import jax.numpy as jnp
import numpy as np
from jax import lax
from jax.sharding import PartitionSpec as P

HIDDEN_UNITS = 16384
EXPERT_COUNT = 8


LOWRANK_SCALE = 0.5
HIGH_ACCURACY = lax.Precision.HIGHEST


def from_partner(value, axis, distance):
    return lax.ppermute(value, axis, [(i, i ^ 1 << distance) for i in range(lax.axis_size(axis))])


def sylvester(count):
    table = np.ones((1, 1), np.float32)
    while table.shape[0] < count:
        table = np.kron(np.array([[1.0, 1.0], [1.0, -1.0]], np.float32), table)
    return jnp.asarray(table)


def spread(values):
    height, stride = values.shape
    result = jnp.dot(values, sylvester(stride), precision=HIGH_ACCURACY)
    position = lax.axis_index("tensor")
    for bit in range(lax.axis_size("tensor").bit_length() - 1):
        partner = from_partner(result, "tensor", bit)
        upper_half = position // (1 << bit) % 2 == 1
        result = jnp.where(upper_half, partner - result, result + partner)
    replicas = lax.axis_size("expert") // EXPERT_COUNT
    owner_position = lax.axis_index("expert")
    for bit in range(replicas.bit_length() - 1):
        partner = from_partner(result, "expert", bit)
        upper_half = owner_position // (1 << bit) % 2 == 1
        result = jnp.where(upper_half, partner - result, result + partner)
    return result


def body(
    hidden, codes, scales, signs, lowrank_down_map, lowrank_up_map, experts, gates, output_gradient
):
    slot_rows, stride = hidden.shape
    devices = lax.axis_size("expert")
    replicas = devices // EXPERT_COUNT
    owner = lax.axis_index("expert")
    expert_position = owner // replicas
    replica = owner % replicas
    capacity = slot_rows // devices
    tokens_here = experts.shape[0]
    columns = output_gradient.shape[1]
    scaling = 1.0 / math.sqrt(HIDDEN_UNITS)
    sign_values = (2 * signs - 1).astype(jnp.float32)
    rotated_hidden = (spread(hidden.astype(jnp.float32) * sign_values) * scaling).astype(
        jnp.bfloat16
    )
    group_size = codes.shape[0] // scales.shape[0]
    weights = (codes.astype(jnp.float32) * jnp.repeat(scales, group_size, axis=0)).astype(
        jnp.bfloat16
    )
    lowrank_local = lax.dynamic_index_in_dim(lowrank_up_map, expert_position, 0, keepdims=False)
    lowrank_input = lax.psum(
        jnp.dot(rotated_hidden, lowrank_down_map, preferred_element_type=jnp.float32), "tensor"
    )
    for bit in range(replicas.bit_length() - 1):
        lowrank_input = lowrank_input + from_partner(lowrank_input, "expert", bit)
    flat_ids = experts.reshape(tokens_here * 2)
    assigned = (flat_ids[:, None] == jnp.arange(EXPERT_COUNT, dtype=jnp.int32)[None, :]).astype(
        jnp.int32
    )
    earlier = jnp.cumsum(assigned, axis=0) - assigned
    slot_index = jnp.sum(earlier * assigned, axis=1)
    target = flat_ids * capacity + slot_index
    picker = (
        target[:, None] == jnp.arange(EXPERT_COUNT * capacity, dtype=jnp.int32)[None, :]
    ).astype(jnp.float32)
    partial_value = jnp.dot(rotated_hidden, weights, preferred_element_type=jnp.float32)
    frozen_output = lax.psum_scatter(partial_value, "tensor", scatter_dimension=1, tiled=True)
    adapter_out = LOWRANK_SCALE * jnp.dot(
        lowrank_input, lowrank_local.astype(jnp.float32), precision=HIGH_ACCURACY
    )
    slot_output = frozen_output + jnp.where(replica == 0, adapter_out, 0.0)
    arrived = lax.all_to_all(slot_output, "expert", split_axis=0, concat_axis=0, tiled=True)
    summed = (
        arrived.reshape(EXPERT_COUNT, replicas, capacity, columns)
        .sum(axis=1)
        .reshape(EXPERT_COUNT * capacity, columns)
    )
    row_values = jnp.dot(picker, summed, precision=HIGH_ACCURACY)
    pairs = row_values.reshape(tokens_here, 2, columns)
    mixed = jnp.sum(gates[:, :, None] * pairs, axis=1).astype(jnp.bfloat16)
    grad_values = output_gradient.astype(jnp.float32)
    gates_gradient = lax.psum(jnp.sum(grad_values[:, None, :] * pairs, axis=2), "tensor")
    weighted = (gates[:, :, None] * grad_values[:, None, :]).reshape(tokens_here * 2, columns)
    slot_gradient = lax.dot_general(
        picker, weighted, (((0,), (0,)), ((), ())), precision=HIGH_ACCURACY
    ).astype(jnp.bfloat16)
    outgoing = jnp.repeat(
        slot_gradient.reshape(EXPERT_COUNT, capacity, columns), replicas, axis=0
    ).reshape(devices * capacity, columns)
    d_rows = lax.all_to_all(outgoing, "expert", split_axis=0, concat_axis=0, tiled=True)
    lowrank_gradient = LOWRANK_SCALE * lax.psum(
        jnp.dot(d_rows, lowrank_local.T, preferred_element_type=jnp.float32), "tensor"
    )
    share = slot_rows // replicas
    share_in = lax.dynamic_slice_in_dim(lowrank_input, replica * share, share, 0)
    share_rows = lax.dynamic_slice_in_dim(d_rows, replica * share, share, 0).astype(jnp.float32)
    local_up_gradient = LOWRANK_SCALE * jnp.dot(share_in.T, share_rows, precision=HIGH_ACCURACY)
    expert_selection_mask = (jnp.arange(EXPERT_COUNT, dtype=jnp.int32) == expert_position).astype(
        jnp.float32
    )
    up_map_gradient = lax.psum(
        expert_selection_mask[:, None, None] * local_up_gradient[None], "expert"
    )
    rotated_gradient = lax.dot_general(
        lax.all_gather(d_rows, "tensor", axis=1, tiled=True),
        weights,
        (((1,), (1,)), ((), ())),
        preferred_element_type=jnp.float32,
    )
    rotated_gradient = rotated_gradient + jnp.dot(
        lowrank_gradient, lowrank_down_map.astype(jnp.float32).T, precision=HIGH_ACCURACY
    )
    down_map_gradient = jnp.dot(
        rotated_hidden.astype(jnp.float32).T, lowrank_gradient, precision=HIGH_ACCURACY
    )
    hidden_gradient = (spread(rotated_gradient) * scaling * sign_values).astype(jnp.bfloat16)
    return (mixed, hidden_gradient, down_map_gradient, up_map_gradient, gates_gradient)


def solution(mesh):
    placed = (
        P(None, ("expert", "tensor")),
        P(("expert", "tensor"), None),
        P(("expert", "tensor"), None),
        P(("expert", "tensor")),
        P(("expert", "tensor"), None),
        P(None, None, "tensor"),
        P("expert", None),
        P("expert", None),
        P("expert", "tensor"),
    )
    return jax.shard_map(
        body,
        mesh=mesh,
        in_specs=placed,
        out_specs=(
            P("expert", "tensor"),
            P(None, ("expert", "tensor")),
            P(("expert", "tensor"), None),
            P(None, None, "tensor"),
            P("expert", None),
        ),
        check_vma=False,
    )
```

profile of v0, /device:TPU:64, one launch (start us, length us, event | category | flops | bytes accessed | tf_op | source)
XLA Modules:
  0.0 446.9 jit_solution(7545466688250433095)
XLA Ops:
  13.4 6.9 %collective-permute-start.1 = (f32[160,256]{1,0:T(8,128)S(1)}, f32[160,256]{1,0:T(8,128)S(1)}, u32[]{:S(2)}, u32[]{:S(2)}) collective-permute-start(f32[160,256]{1,0:T(8,128)S(1)} %add_select_fusion.9), channel_id=1, source_target_pairs={{0,2},{1,3},{2,0},{3,1},{4,6},{5,7},{6,4},{7,5},{8,10},{9,11},{10,... | collective-permute-start | bytes 491528 | tf_op jit(solution)/shard_map/ppermute | solution.py:18
  20.4 4.5 collective-permute-done.1
  27.7 6.4 %collective-permute-done.2 = f32[160,256]{1,0:T(8,128)S(1)} collective-permute-done((f32[160,256]{1,0:T(8,128)S(1)}, f32[160,256]{1,0:T(8,128)S(1)}, u32[]{:S(2)}, u32[]{:S(2)}) %collective-permute-start.2) | collective-permute-done | bytes 163872 | tf_op jit(solution)/shard_map/ppermute | solution.py:18
  34.1 8.2 %collective-permute-start.3 = (f32[160,256]{1,0:T(8,128)S(1)}, f32[160,256]{1,0:T(8,128)S(1)}, u32[]{:S(2)}, u32[]{:S(2)}) collective-permute-start(f32[160,256]{1,0:T(8,128)S(1)} %add_select_fusion.7), channel_id=1, source_target_pairs={{0,8},{1,9},{2,10},{3,11},{4,12},{5,13},{6,14},{7,15},{8,0},{9,1},... | collective-permute-start | bytes 491528 | tf_op jit(solution)/shard_map/ppermute | solution.py:18
  42.4 6.8 %collective-permute-done.3 = f32[160,256]{1,0:T(8,128)S(1)} collective-permute-done((f32[160,256]{1,0:T(8,128)S(1)}, f32[160,256]{1,0:T(8,128)S(1)}, u32[]{:S(2)}, u32[]{:S(2)}) %collective-permute-start.3) | collective-permute-done | bytes 163872 | tf_op jit(solution)/shard_map/ppermute | solution.py:18
  52.8 3.7 collective-permute-done.4
  57.1 4.5 %collective-permute-start.5 = (f32[160,256]{1,0:T(8,128)}, f32[160,256]{1,0:T(8,128)}, u32[]{:S(2)}, u32[]{:S(2)}) collective-permute-start(f32[160,256]{1,0:T(8,128)} %add_select_fusion.5), channel_id=1, source_target_pairs={{0,32},{16,48},{32,0},{48,16},{64,96},{80,112},{96,64},{112,80},{1... | collective-permute-start | bytes 491528 | tf_op jit(solution)/shard_map/ppermute | solution.py:18
  85.7 20.4 %all_to_all.21 = bf16[32,5,384]{2,1,0:T(8,128)(2,1)} all-to-all(bf16[32,5,384]{2,1,0:T(8,128)(2,1)S(1)} %bitcast.31), channel_id=1, replica_groups=mesh['expert'=32,'tensor'=16] {'expert'}, dimensions={0} | all-to-all | bytes 245760 | tf_op jit(solution)/shard_map/all_to_all | solution.py:106
  109.5 46.9 %psum.28 = f32[160,64]{0,1:T(8,128)} all-reduce(f32[160,64]{0,1:T(8,128)} %fusion.34), channel_id=1, replica_groups=mesh['expert'=32,'tensor'=16] {'tensor'}, use_global_device_ids=true, to_apply=%region_3.4 | all-reduce | flops 10240 | bytes 81920 | tf_op jit(solution)/shard_map/psum | solution.py:67
  167.3 5.0 %collective-permute-done.7 = f32[160,64]{0,1:T(8,128)} collective-permute-done((f32[160,64]{0,1:T(8,128)}, f32[160,64]{0,1:T(8,128)}, u32[]{:S(2)}, u32[]{:S(2)}) %collective-permute-start.7) | collective-permute-done | bytes 40992 | tf_op jit(solution)/shard_map/ppermute | solution.py:18
  177.5 4.6 %all-to-all-start = ((f32[32,5,384]{2,1,0:T(8,128)}), f32[32,5,384]{2,1,0:T(8,128)}, u32[]{:S(2)}, u32[]{:S(2)}) async-start(f32[32,5,384]{2,1,0:T(8,128)} %all_to_all.14), calls=%async_computation.1 | async-start | bytes 786432 | tf_op jit(solution)/shard_map/all_to_all | solution.py:88
  185.3 8.2 %all-to-all-done = f32[32,5,384]{2,1,0:T(8,128)} async-done(((f32[32,5,384]{2,1,0:T(8,128)}), f32[32,5,384]{2,1,0:T(8,128)}, u32[]{:S(2)}, u32[]{:S(2)}) %all-to-all-start) | async-done | bytes 245792 | tf_op jit(solution)/shard_map/all_to_all | solution.py:88
  198.5 46.3 %all-reduce = (f32[160,64]{0,1:T(8,128)}, f32[16,2]{0,1:T(2,128)}) all-reduce(f32[160,64]{0,1:T(8,128)} %fusion.11, f32[16,2]{0,1:T(2,128)S(1)} %get-tuple-element.5), channel_id=1, replica_groups=mesh['expert'=32,'tensor'=16] {'tensor'}, use_global_device_ids=true, to_apply=%region_6.7 | all-reduce | flops 10272 | bytes 82176 | tf_op jit(solution)/shard_map/psum | solution.py:107
  253.1 6.0 %collective-permute-start.9 = (f32[160,256]{1,0:T(8,128)S(1)}, f32[160,256]{1,0:T(8,128)S(1)}, u32[]{:S(2)}, u32[]{:S(2)}) collective-permute-start(f32[160,256]{1,0:T(8,128)S(1)} %add_select_fusion.4), channel_id=1, source_target_pairs={{0,2},{1,3},{2,0},{3,1},{4,6},{5,7},{6,4},{7,5},{8,10},{9,11},{10,... | collective-permute-start | bytes 491528 | tf_op jit(solution)/shard_map/ppermute | solution.py:18
  259.1 4.5 %collective-permute-done.9 = f32[160,256]{1,0:T(8,128)S(1)} collective-permute-done((f32[160,256]{1,0:T(8,128)S(1)}, f32[160,256]{1,0:T(8,128)S(1)}, u32[]{:S(2)}, u32[]{:S(2)}) %collective-permute-start.9) | collective-permute-done | bytes 163872 | tf_op jit(solution)/shard_map/ppermute | solution.py:18
  263.6 4.1 collective-permute-start.10
  268.8 5.5 %collective-permute-done.10 = f32[160,256]{1,0:T(8,128)S(1)} collective-permute-done((f32[160,256]{1,0:T(8,128)S(1)}, f32[160,256]{1,0:T(8,128)S(1)}, u32[]{:S(2)}, u32[]{:S(2)}) %collective-permute-start.10) | collective-permute-done | bytes 163872 | tf_op jit(solution)/shard_map/ppermute | solution.py:18
  274.4 4.4 collective-permute-start.11
  279.8 6.6 %collective-permute-done.11 = f32[160,256]{1,0:T(8,128)S(1)} collective-permute-done((f32[160,256]{1,0:T(8,128)S(1)}, f32[160,256]{1,0:T(8,128)S(1)}, u32[]{:S(2)}, u32[]{:S(2)}) %collective-permute-start.11) | collective-permute-done | bytes 163872 | tf_op jit(solution)/shard_map/ppermute | solution.py:18
  286.5 4.4 collective-permute-start.12
  290.9 4.0 collective-permute-done.12
  295.0 4.3 collective-permute-start.13
  300.1 7.0 %collective-permute-done.13 = f32[160,256]{1,0:T(8,128)S(1)} collective-permute-done((f32[160,256]{1,0:T(8,128)S(1)}, f32[160,256]{1,0:T(8,128)S(1)}, u32[]{:S(2)}, u32[]{:S(2)}) %collective-permute-start.13) | collective-permute-done | bytes 163872 | tf_op jit(solution)/shard_map/ppermute | solution.py:18
  307.8 129.6 %all-reduce.3.cloned.1.call-done = f32[8,64,384]{2,1,0:T(8,128)} async-done(((f32[8,64,384]{2,1,0:T(8,128)}), f32[8,64,384]{2,1,0:T(8,128)}) %all-reduce.3.cloned.1.call-update) | async-done | bytes 786448 | tf_op jit(solution)/shard_map/psum | solution.py:117
  (92 shorter events, 78.0 us)
Async XLA Ops:
  8.0 165.8 %copy-start = (bf16[8,64,384]{2,1,0:T(8,128)(2,1)S(1)}, bf16[8,64,384]{2,1,0:T(8,128)(2,1)}, u32[]{:S(2)}) copy-start(bf16[8,64,384]{2,1,0:T(8,128)(2,1)} %param.16) | copy-start | bytes 1179652
  8.0 165.8 %reduce-scatter.2.cloned.1.call-start = ((), (), s32[]{:S(2)}) async-start(), calls=%async_computation.3 | async-start | bytes 4177920 | tf_op jit(solution)/shard_map/reduce_scatter | solution.py:83
  10.1 3.3 collective-permute-start
  13.4 11.4 %collective-permute-start.1 = (f32[160,256]{1,0:T(8,128)S(1)}, f32[160,256]{1,0:T(8,128)S(1)}, u32[]{:S(2)}, u32[]{:S(2)}) collective-permute-start(f32[160,256]{1,0:T(8,128)S(1)} %add_select_fusion.9), channel_id=1, source_target_pairs={{0,2},{1,3},{2,0},{3,1},{4,6},{5,7},{6,4},{7,5},{8,10},{9,11},{10,... | collective-permute-start | bytes 491528 | tf_op jit(solution)/shard_map/ppermute | solution.py:18
  24.9 9.2 %collective-permute-start.2 = (f32[160,256]{1,0:T(8,128)S(1)}, f32[160,256]{1,0:T(8,128)S(1)}, u32[]{:S(2)}, u32[]{:S(2)}) collective-permute-start(f32[160,256]{1,0:T(8,128)S(1)} %add_select_fusion.8), channel_id=1, source_target_pairs={{0,4},{1,5},{2,6},{3,7},{4,0},{5,1},{6,2},{7,3},{8,12},{9,13},{10,... | collective-permute-start | bytes 491528 | tf_op jit(solution)/shard_map/ppermute | solution.py:18
  34.1 15.1 %collective-permute-start.3 = (f32[160,256]{1,0:T(8,128)S(1)}, f32[160,256]{1,0:T(8,128)S(1)}, u32[]{:S(2)}, u32[]{:S(2)}) collective-permute-start(f32[160,256]{1,0:T(8,128)S(1)} %add_select_fusion.7), channel_id=1, source_target_pairs={{0,8},{1,9},{2,10},{3,11},{4,12},{5,13},{6,14},{7,15},{8,0},{9,1},... | collective-permute-start | bytes 491528 | tf_op jit(solution)/shard_map/ppermute | solution.py:18
  49.2 7.2 %collective-permute-start.4 = (f32[160,256]{1,0:T(8,128)S(1)}, f32[160,256]{1,0:T(8,128)S(1)}, u32[]{:S(2)}, u32[]{:S(2)}) collective-permute-start(f32[160,256]{1,0:T(8,128)S(1)} %add_select_fusion.6), channel_id=1, source_target_pairs={{0,16},{16,0},{32,48},{48,32},{64,80},{80,64},{96,112},{112,96},{1... | collective-permute-start | bytes 491528 | tf_op jit(solution)/shard_map/ppermute | solution.py:18
  57.1 10.2 %collective-permute-start.5 = (f32[160,256]{1,0:T(8,128)}, f32[160,256]{1,0:T(8,128)}, u32[]{:S(2)}, u32[]{:S(2)}) collective-permute-start(f32[160,256]{1,0:T(8,128)} %add_select_fusion.5), channel_id=1, source_target_pairs={{0,32},{16,48},{32,0},{48,16},{64,96},{80,112},{96,64},{112,80},{1... | collective-permute-start | bytes 491528 | tf_op jit(solution)/shard_map/ppermute | solution.py:18
  71.6 175.0 %all-gather.2.cloned.1.call-start = ((), (), s32[]{:S(2)}) async-start(), calls=%async_computation.4 | async-start | bytes 2088960 | tf_op jit(solution)/shard_map/all_gather | solution.py:121
  81.1 101.0 %copy-start.5 = (bf16[16,384]{1,0:T(8,128)(2,1)S(1)}, bf16[16,384]{1,0:T(8,128)(2,1)}, u32[]{:S(2)}) copy-start(bf16[16,384]{1,0:T(8,128)(2,1)} %param.19) | copy-start | bytes 36868
  81.1 102.5 %copy-start.8 = (s32[16,2]{0,1:T(2,128)S(1)}, s32[16,2]{0,1:T(2,128)}, u32[]{:S(2)}) copy-start(s32[16,2]{0,1:T(2,128)} %param.17) | copy-start | bytes 388
  156.4 6.4 %collective-permute-start.6 = (f32[160,64]{0,1:T(8,128)}, f32[160,64]{0,1:T(8,128)S(1)}, u32[]{:S(2)}, u32[]{:S(2)}) collective-permute-start(f32[160,64]{0,1:T(8,128)} %psum.28), channel_id=1, source_target_pairs={{0,16},{16,0},{32,48},{48,32},{64,80},{80,64},{96,112},{112,96},{1... | collective-permute-start | bytes 122888 | tf_op jit(solution)/shard_map/ppermute | solution.py:18
  164.2 8.1 %collective-permute-start.7 = (f32[160,64]{0,1:T(8,128)}, f32[160,64]{0,1:T(8,128)}, u32[]{:S(2)}, u32[]{:S(2)}) collective-permute-start(f32[160,64]{0,1:T(8,128)} %add.126), channel_id=1, source_target_pairs={{0,32},{16,48},{32,0},{48,16},{64,96},{80,112},{96,64},{112,80},{1... | collective-permute-start | bytes 122888 | tf_op jit(solution)/shard_map/ppermute | solution.py:18
  177.5 16.0 %all-to-all-start = ((f32[32,5,384]{2,1,0:T(8,128)}), f32[32,5,384]{2,1,0:T(8,128)}, u32[]{:S(2)}, u32[]{:S(2)}) async-start(f32[32,5,384]{2,1,0:T(8,128)} %all_to_all.14), calls=%async_computation.1 | async-start | bytes 786432 | tf_op jit(solution)/shard_map/all_to_all | solution.py:88
  182.1 255.2 %all-reduce.3.cloned.1.call-start = ((), (), s32[]{:S(2)}) async-start(), calls=%async_computation.5 | async-start | bytes 1572864 | tf_op jit(solution)/shard_map/psum | solution.py:117
  249.4 41.5 %copy-start.9 = (s32[256]{0:T(256)S(1)}, s32[256]{0:T(256)}, u32[]{:S(2)}) copy-start(s32[256]{0:T(256)} %param.14) | copy-start | bytes 3076
  249.4 49.9 %copy-start.2 = (bf16[160,256]{1,0:T(8,128)(2,1)S(1)}, bf16[160,256]{1,0:T(8,128)(2,1)}, u32[]{:S(2)}) copy-start(bf16[160,256]{1,0:T(8,128)(2,1)} %copy-done.1) | copy-start | bytes 245764
  249.4 49.9 %copy-start.4 = (f32[160,64]{0,1:T(8,128)S(1)}, f32[160,64]{0,1:T(8,128)}, u32[]{:S(2)}) copy-start(f32[160,64]{0,1:T(8,128)} %get-tuple-element.7) | copy-start | bytes 122884
  249.8 3.3 collective-permute-start.8
  253.1 10.5 %collective-permute-start.9 = (f32[160,256]{1,0:T(8,128)S(1)}, f32[160,256]{1,0:T(8,128)S(1)}, u32[]{:S(2)}, u32[]{:S(2)}) collective-permute-start(f32[160,256]{1,0:T(8,128)S(1)} %add_select_fusion.4), channel_id=1, source_target_pairs={{0,2},{1,3},{2,0},{3,1},{4,6},{5,7},{6,4},{7,5},{8,10},{9,11},{10,... | collective-permute-start | bytes 491528 | tf_op jit(solution)/shard_map/ppermute | solution.py:18
  263.6 10.7 %collective-permute-start.10 = (f32[160,256]{1,0:T(8,128)S(1)}, f32[160,256]{1,0:T(8,128)S(1)}, u32[]{:S(2)}, u32[]{:S(2)}) collective-permute-start(f32[160,256]{1,0:T(8,128)S(1)} %add_select_fusion.3), channel_id=1, source_target_pairs={{0,4},{1,5},{2,6},{3,7},{4,0},{5,1},{6,2},{7,3},{8,12},{9,13},{10,... | collective-permute-start | bytes 491528 | tf_op jit(solution)/shard_map/ppermute | solution.py:18
  274.4 12.1 %collective-permute-start.11 = (f32[160,256]{1,0:T(8,128)S(1)}, f32[160,256]{1,0:T(8,128)S(1)}, u32[]{:S(2)}, u32[]{:S(2)}) collective-permute-start(f32[160,256]{1,0:T(8,128)S(1)} %add_select_fusion.2), channel_id=1, source_target_pairs={{0,8},{1,9},{2,10},{3,11},{4,12},{5,13},{6,14},{7,15},{8,0},{9,1},... | collective-permute-start | bytes 491528 | tf_op jit(solution)/shard_map/ppermute | solution.py:18
  286.5 8.5 %collective-permute-start.12 = (f32[160,256]{1,0:T(8,128)S(1)}, f32[160,256]{1,0:T(8,128)S(1)}, u32[]{:S(2)}, u32[]{:S(2)}) collective-permute-start(f32[160,256]{1,0:T(8,128)S(1)} %add_select_fusion.1), channel_id=1, source_target_pairs={{0,16},{16,0},{32,48},{48,32},{64,80},{80,64},{96,112},{112,96},{1... | collective-permute-start | bytes 491528 | tf_op jit(solution)/shard_map/ppermute | solution.py:18
  295.0 12.2 %collective-permute-start.13 = (f32[160,256]{1,0:T(8,128)S(1)}, f32[160,256]{1,0:T(8,128)S(1)}, u32[]{:S(2)}, u32[]{:S(2)}) collective-permute-start(f32[160,256]{1,0:T(8,128)S(1)} %add_select_fusion), channel_id=1, source_target_pairs={{0,32},{16,48},{32,0},{48,16},{64,96},{80,112},{96,64},{112,80},{1... | collective-permute-start | bytes 491528 | tf_op jit(solution)/shard_map/ppermute | solution.py:18
  (5 other events, 5.1 us)
Sparse Core Ops, SparseCore 0:
  71.7 64.4 reduce-scatter.1
  138.5 42.9 all-gather.1
Sparse Core Ops, SparseCore 1:
  279.9 157.4 all-reduce.2
where the time goes:
time: 449 us; the launch traced here: 447 us
  waiting for transfers between devices  201 us (45%)
  blocking collectives  114 us (25%)
  starting transfers between devices  63.8 us (14%)
  matrix products  19.5 us (4%)
  local copies, waits for them, and re-layouts  17.9 us (4%)
  between operations  16 us (4%)
  other arithmetic  15.2 us (3%)
    psum x1, waiting for transfers between devices, body(): lax.psum(expert_selection_mask[:, None, None] * local_up_gradient[None],...  130 us
    ppermute x14, waiting for transfers between devices, from_partner(): lax.ppermute(value, axis, [(i, i ^ 1 << distance) for i in range(lax.axis...  63.1 us
    ppermute x14, starting transfers between devices, from_partner(): lax.ppermute(value, axis, [(i, i ^ 1 << distance) for i in range(lax.axis...  59.1 us
    psum x1, blocking collectives, body(): lax.psum(jnp.dot(rotated_hidden, lowrank_down_map, preferred_element_type...  46.9 us
    psum x1, blocking collectives, body(): lax.psum(jnp.dot(d_rows, lowrank_local.T, preferred_element_type=jnp.floa...  46.3 us
    all_to_all x1, blocking collectives, body(): lax.all_to_all(outgoing, 'expert', split_axis=0, concat_axis=0, tiled=True)  20.4 us
  transfers between devices with their start and end apart: 18, of which 16 were waited for; matrix products, arithmetic and copies ran while one was open for 8% of the time, Pallas kernels for 0%

commit v1 on v0

v1 whole, which is shorter than its diff:
```python
import math

import jax
import jax.numpy as jnp
import numpy as np
from jax import lax
from jax.sharding import Mesh
from jax.sharding import PartitionSpec as P

HIDDEN_UNITS = 16384
EXPERT_COUNT = 8
LOWRANK_SCALE = 0.5
HIGH_ACCURACY = lax.Precision.HIGHEST
BF = jnp.bfloat16
F32 = jnp.float32
EXPERT = ("e", "r")
TENSOR = ("z", "c")
SLAB = ("r", "z", "c")
LANES = 128


def sylvester(count):
    table = np.ones((1, 1), np.float32)
    while table.shape[0] < count:
        table = np.kron(np.array([[1.0, 1.0], [1.0, -1.0]], np.float32), table)
    return jnp.asarray(table, BF)


def exchange(value, axes):
    return lax.all_to_all(value, axes, split_axis=0, concat_axis=0, tiled=True)


def to_chunks(values, peers):
    height, stride = values.shape
    halves = stride // LANES
    blocks = peers // halves
    shaped = values.reshape(blocks, height // blocks, halves, LANES)
    return shaped.transpose(0, 2, 1, 3).reshape(peers, height // blocks, LANES)


def from_chunks(chunks, height, stride):
    halves = stride // LANES
    blocks = chunks.shape[0] // halves
    shaped = chunks.reshape(blocks, halves, height // blocks, LANES)
    return shaped.transpose(0, 2, 1, 3).reshape(height, stride)


def mix_blocks(chunks):
    peers, rows, lanes = chunks.shape
    mixed = jnp.dot(
        sylvester(peers), chunks.reshape(peers, rows * lanes), preferred_element_type=F32
    )
    return mixed.astype(BF).reshape(peers, rows, lanes)


def body(
    hidden, codes, scales, signs, lowrank_down_map, lowrank_up_map, experts, gates, output_gradient
):
    slot_rows, stride = hidden.shape
    replicas, depth, cores = lax.axis_size("r"), lax.axis_size("z"), lax.axis_size("c")
    devices = EXPERT_COUNT * replicas
    peers = replicas * depth * cores
    rank = lowrank_down_map.shape[1]
    expert_position = lax.axis_index("e")
    replica = lax.axis_index("r")
    core = lax.axis_index("c")
    capacity = slot_rows // devices
    tokens_here = experts.shape[0]
    columns = output_gradient.shape[1]
    scaling = 1.0 / math.sqrt(HIDDEN_UNITS)
    sign_values = (2 * signs - 1).astype(F32)
    group_size = codes.shape[0] // scales.shape[0]

    flat_ids = experts.reshape(tokens_here * 2)
    assigned = (flat_ids[:, None] == jnp.arange(EXPERT_COUNT, dtype=jnp.int32)[None, :]).astype(
        jnp.int32
    )
    earlier = jnp.cumsum(assigned, axis=0) - assigned
    slot_index = jnp.sum(earlier * assigned, axis=1)
    target = flat_ids * capacity + slot_index
    row = jnp.arange(devices * capacity, dtype=jnp.int32)
    row_slot = row // (replicas * capacity) * capacity + row % capacity
    copier = (row_slot[:, None] == target[None, :]).astype(BF)
    weighted = (
        (gates[:, :, None] * output_gradient.astype(F32)[:, None, :])
        .reshape(tokens_here * 2, columns)
        .astype(BF)
    )
    outgoing = jnp.dot(copier, weighted, preferred_element_type=F32).astype(BF)
    d_rows = exchange(outgoing, EXPERT)
    lowrank_local = lax.dynamic_index_in_dim(lowrank_up_map, expert_position, 0, keepdims=False)
    gathered = lax.all_gather(
        jnp.concatenate([d_rows, lowrank_local], axis=0), TENSOR, axis=1, tiled=True
    )

    signed = (hidden.astype(F32) * sign_values).astype(BF)
    mixed_blocks = mix_blocks(exchange(to_chunks(signed, peers), SLAB))
    unrotated = from_chunks(exchange(mixed_blocks, SLAB), slot_rows, stride)
    spread_local = sylvester(stride)
    rotated = (jnp.dot(unrotated, spread_local, preferred_element_type=F32) * scaling).astype(BF)

    weights = (codes.astype(F32) * jnp.repeat(scales, group_size, axis=0)).astype(BF)

    adapter_part = jnp.dot(rotated, lowrank_down_map, preferred_element_type=F32)
    adapter_column = exchange(adapter_part.T.astype(BF), SLAB)
    adapter_column = adapter_column.astype(F32).sum(axis=0)

    by_depth = weights.reshape(stride, depth, cores, columns)
    own = lax.dynamic_index_in_dim(by_depth, core, 2, keepdims=False).reshape(stride, depth * columns)
    other = lax.dynamic_index_in_dim(by_depth, 1 - core, 2, keepdims=False).reshape(
        stride, depth * columns
    )
    part_other = jnp.dot(rotated, other, preferred_element_type=F32).astype(BF)
    part_own = jnp.dot(rotated, own, preferred_element_type=F32)
    arrived = lax.ppermute(part_other, "c", [(0, 1), (1, 0)])
    pair = (part_own + arrived.astype(F32)).astype(BF)
    pair = pair.reshape(slot_rows, depth, columns).transpose(1, 0, 2)
    frozen = exchange(pair, "z").astype(F32).sum(axis=0)

    d_full = gathered[:slot_rows]
    lowrank_full = gathered[slot_rows:]
    adapter_grad = LOWRANK_SCALE * lax.dot_general(
        d_full, lowrank_full, (((1,), (1,)), ((), ())), preferred_element_type=F32
    )
    d_rotated = lax.dot_general(
        d_full, weights, (((1,), (1,)), ((), ())), preferred_element_type=F32
    ) + lax.dot_general(
        adapter_grad.astype(BF),
        lowrank_down_map,
        (((1,), (1,)), ((), ())),
        preferred_element_type=F32,
    )
    row_product = jnp.sum(rotated.astype(F32) * d_rotated, axis=1)
    down_map_gradient = lax.dot_general(
        rotated, adapter_grad.astype(BF), (((0,), (0,)), ((), ())), preferred_element_type=F32
    )
    d_local = jnp.dot(d_rotated.astype(BF), spread_local, preferred_element_type=F32)
    chunk_rows = slot_rows * stride // (peers * LANES)
    riders = jnp.concatenate(
        [adapter_column, row_product, jnp.zeros((3 * LANES - 2 * slot_rows,), F32)]
    ).astype(BF)
    riders = jnp.broadcast_to(riders.reshape(1, 3, LANES), (peers, 3, LANES))
    d_chunks = jnp.concatenate([to_chunks((d_local * scaling).astype(BF), peers), riders], axis=1)
    d_chunks = exchange(d_chunks, SLAB)
    d_mixed = exchange(mix_blocks(d_chunks[:, :chunk_rows]), SLAB)
    hidden_gradient = (
        from_chunks(d_mixed, slot_rows, stride).astype(F32) * sign_values
    ).astype(BF)
    riders = d_chunks[:, chunk_rows:].reshape(peers, 3 * LANES)
    adapter_in = riders[:, :slot_rows]
    row_total = riders[:, slot_rows : 2 * slot_rows].astype(F32).sum(axis=0)

    slot_output = frozen + (LOWRANK_SCALE / replicas) * lax.dot_general(
        adapter_in, lowrank_local, (((0,), (0,)), ((), ())), preferred_element_type=F32
    )
    share = rank // replicas
    adapter_share = lax.dynamic_slice_in_dim(adapter_in, replica * share, share, 0)
    up_share = LOWRANK_SCALE * jnp.dot(adapter_share, d_rows, preferred_element_type=F32)
    total_high = row_total.astype(BF)
    total_low = (row_total - total_high.astype(F32)).astype(BF)
    totals = jnp.concatenate(
        [total_high.reshape(devices, capacity), total_low.reshape(devices, capacity)], axis=1
    )
    totals = jnp.pad(totals, ((0, 0), (0, columns - 2 * capacity)))[:, None, :]
    parcel = jnp.concatenate(
        [
            slot_output.astype(BF).reshape(devices, capacity, columns),
            totals,
            jnp.broadcast_to(up_share.astype(BF)[None], (devices, share, columns)),
        ],
        axis=1,
    )
    parcel = exchange(parcel, EXPERT)
    up_map_gradient = (
        parcel[:, capacity + 1 :].astype(F32).reshape(EXPERT_COUNT, rank, columns)
    )
    summed = (
        parcel[:, :capacity]
        .astype(F32)
        .reshape(EXPERT_COUNT, replicas, capacity, columns)
        .sum(axis=1)
        .reshape(EXPERT_COUNT * capacity, columns)
    )
    totals = parcel.reshape(EXPERT_COUNT, replicas, capacity + 1 + share, columns)[:, 0, capacity]
    totals = totals[:, : 2 * capacity].astype(F32)
    totals = (totals[:, :capacity] + totals[:, capacity:]).reshape(EXPERT_COUNT * capacity)
    slot_id = jnp.arange(EXPERT_COUNT * capacity, dtype=jnp.int32)
    chosen = target[:, None] == slot_id[None, :]
    gates_gradient = jnp.sum(jnp.where(chosen, totals[None, :], 0.0), axis=1)
    gates_gradient = gates_gradient.reshape(tokens_here, 2) / gates
    chosen = chosen.reshape(tokens_here, 2, EXPERT_COUNT * capacity)
    mixer = jnp.sum(jnp.where(chosen, gates[:, :, None], 0.0), axis=1)
    mixed = jnp.dot(mixer, summed, precision=HIGH_ACCURACY).astype(BF)
    return (mixed, hidden_gradient, down_map_gradient, up_map_gradient, gates_gradient)


def solution(mesh):
    owners, tensor = mesh.devices.shape
    split = Mesh(
        mesh.devices.reshape(EXPERT_COUNT, owners // EXPERT_COUNT, tensor // 2, 2),
        ("e", "r", "z", "c"),
    )
    every = EXPERT + TENSOR
    placed = (
        P(None, every),
        P(every, None),
        P(every, None),
        P(every),
        P(every, None),
        P(None, None, TENSOR),
        P(EXPERT, None),
        P(EXPERT, None),
        P(EXPERT, TENSOR),
    )
    return jax.shard_map(
        body,
        mesh=split,
        in_specs=placed,
        out_specs=(
            P(EXPERT, TENSOR),
            P(None, every),
            P(every, None),
            P(None, None, TENSOR),
            P(EXPERT, None),
        ),
        check_vma=False,
    )
```

time: 449 us -> 199 us (0.44)
  the two profiles are of different devices: /device:TPU:64 before, /device:TPU:8 now
where the time goes in v1:
time: 199 us; the launch traced here: 198 us
  waiting for transfers between devices  78.5 us (39%)
  starting transfers between devices  59.4 us (30%)
  local copies, waits for them, and re-layouts  19.5 us (10%)
  matrix products  15.5 us (8%)
  between operations  14.7 us (7%)
  other arithmetic  10 us (5%)
    all_to_all x8, waiting for transfers between devices, exchange(): return lax.all_to_all(value, axes, split_axis=0, concat_axis=0, tiled=True)  78.5 us
    all_to_all x8, starting transfers between devices, exchange(): return lax.all_to_all(value, axes, split_axis=0, concat_axis=0, tiled=True)  57.3 us
  transfers between devices with their start and end apart: 10, of which 8 were waited for; matrix products, arithmetic and copies ran while one was open for 18% of the time, Pallas kernels for 0%

profile of v1, /device:TPU:8, one launch (start us, length us, event | category | flops | bytes accessed | tf_op | source)
XLA Modules:
  0.0 197.7 jit_solution(18093374348735652908)
XLA Ops:
  11.5 10.2 %all-to-all-start.3 = ((bf16[32,5,384]{2,1,0:T(8,128)(2,1)}), bf16[32,5,384]{2,1,0:T(8,128)(2,1)S(1)}, u32[]{:S(2)}, u32[]{:S(2)}) async-start(bf16[32,5,384]{2,1,0:T(8,128)(2,1)} %all_to_all.35), calls=%async_computation.3 | async-start | bytes 393216 | tf_op jit(solution)/shard_map/all_to_all | solution.py:30
  21.8 10.9 %all-to-all-done.3 = bf16[32,5,384]{2,1,0:T(8,128)(2,1)S(1)} async-done(((bf16[32,5,384]{2,1,0:T(8,128)(2,1)}), bf16[32,5,384]{2,1,0:T(8,128)(2,1)S(1)}, u32[]{:S(2)}, u32[]{:S(2)}) %all-to-all-start.3) | async-done | bytes 122912 | tf_op jit(solution)/shard_map/all_to_all | solution.py:30
  34.4 12.8 %all-to-all-start = ((bf16[64,5,128]{2,1,0:T(8,128)(2,1)}), bf16[64,5,128]{2,1,0:T(8,128)(2,1)}, u32[]{:S(2)}, u32[]{:S(2)}) async-start(bf16[64,5,128]{2,1,0:T(8,128)(2,1)} %copy.119), calls=%async_computation | async-start | bytes 262144 | tf_op jit(solution)/shard_map/all_to_all | solution.py:30
  47.2 2.6 %fusion = bf16[256,6144]{1,0:T(8,128)(2,1)S(1)} fusion(bf16[256,6144]{1,0:T(8,128)(2,1)} %param.13, f32[4,6144]{1,0:T(4,128)} %param.14), kind=kLoop, calls=%fused_computation.1 | loop fusion | flops 4718592 | bytes 6389760 | tf_op jit(solution)/shard_map/convert_element_type | solution.py:102
  49.8 2.8 %copy.121 = bf16[256,6144]{0,1:T(8,128)(2,1)} copy(bf16[256,6144]{1,0:T(8,128)(2,1)S(1)} %fusion) | data formatting | bytes 6291456 | tf_op jit(solution)/shard_map/convert_element_type | solution.py:102
  52.6 4.0 %all-to-all-done = bf16[64,5,128]{2,1,0:T(8,128)(2,1)} async-done(((bf16[64,5,128]{2,1,0:T(8,128)(2,1)}), bf16[64,5,128]{2,1,0:T(8,128)(2,1)}, u32[]{:S(2)}, u32[]{:S(2)}) %all-to-all-start) | async-done | bytes 81952 | tf_op jit(solution)/shard_map/all_to_all | solution.py:30
  60.0 6.9 %all-to-all-start.1 = ((bf16[64,5,128]{2,1,0:T(8,128)(2,1)}), bf16[64,5,128]{2,1,0:T(8,128)(2,1)}, u32[]{:S(2)}, u32[]{:S(2)}) async-start(bf16[64,5,128]{2,1,0:T(8,128)(2,1)} %reshape.167), calls=%async_computation.1 | async-start | bytes 262144 | tf_op jit(solution)/shard_map/all_to_all | solution.py:30
  66.9 3.9 %constant_dynamic-slice_fusion = (bf16[256,8,1,384]{0,3,2,1:T(8,128)(2,1)}, bf16[256,8,1,384]{0,3,2,1:T(8,128)(2,1)}) fusion(bf16[256,8,2,384]{0,3,2,1:T(8,128)(2,1)} %bitcast.97, s32[]{:T(128)S(6)} %select_n.44, s32[]{:T(128)S(6)} %select_n.43), kind=kLoop, calls=%fused_computation.84 | loop fusion | bytes 6291464 | tf_op jit(solution)/shard_map/jit(dynamic_index_in_dim)/dynamic_slice | solution.py:110
  70.8 5.6 %all-to-all-done.1 = bf16[64,5,128]{2,1,0:T(8,128)(2,1)} async-done(((bf16[64,5,128]{2,1,0:T(8,128)(2,1)}), bf16[64,5,128]{2,1,0:T(8,128)(2,1)}, u32[]{:S(2)}, u32[]{:S(2)}) %all-to-all-start.1) | async-done | bytes 81952 | tf_op jit(solution)/shard_map/all_to_all | solution.py:30
  78.4 3.1 %convolution_convert_fusion = bf16[160,3072]{1,0:T(8,128)(2,1)} fusion(bf16[160,256]{1,0:T(8,128)(2,1)S(1)} %fusion.10, bf16[256,3072]{0,1:T(8,128)(2,1)} %bitcast.99), kind=kOutput, calls=%fused_computation.2 | convolution fusion | flops 252149760 | bytes 2637824 | tf_op jit(solution)/shard_map/dot_general | solution.py:113
  81.5 2.0 %collective-permute-start = (bf16[160,3072]{1,0:T(8,128)(2,1)}, bf16[160,3072]{1,0:T(8,128)(2,1)}, u32[]{:S(2)}, u32[]{:S(2)}) collective-permute-start(bf16[160,3072]{1,0:T(8,128)(2,1)} %convolution_convert_fusion), channel_id=1, source_target_pairs={{0,1},{1,0},{2,3},{3,2},{4,5},{5,4},{6,7},{7,6},{8,9},{9,8},{10,11... | collective-permute-start | bytes 2949128 | tf_op jit(solution)/shard_map/ppermute | solution.py:115
  84.4 6.2 %all-to-all-start.4 = ((bf16[64,1,160]{2,1,0:T(2,128)(2,1)}), bf16[64,1,160]{2,1,0:T(2,128)(2,1)}, u32[]{:S(2)}, u32[]{:S(2)}) async-start(bf16[64,1,160]{2,1,0:T(2,128)(2,1)} %copy.125), calls=%async_computation.4 | async-start | bytes 131072 | tf_op jit(solution)/shard_map/all_to_all | solution.py:30
  90.6 2.4 %add_convert_fusion = bf16[160,3072]{1,0:T(8,128)(2,1)S(1)} fusion(bf16[160,3072]{1,0:T(8,128)(2,1)} %collective-permute-done, bf16[160,256]{1,0:T(8,128)(2,1)} %copy-done.1, bf16[256,3072]{0,1:T(8,128)(2,1)} %bitcast.98), kind=kOutput, calls=%fused_computation.4 | convolution fusion | flops 253132800 | bytes 3620864 | tf_op jit(solution)/shard_map/dot_general | solution.py:114
  94.0 5.5 %all-to-all-done.4 = bf16[64,1,160]{2,1,0:T(2,128)(2,1)} async-done(((bf16[64,1,160]{2,1,0:T(2,128)(2,1)}), bf16[64,1,160]{2,1,0:T(2,128)(2,1)}, u32[]{:S(2)}, u32[]{:S(2)}) %all-to-all-start.4) | async-done | bytes 20512 | tf_op jit(solution)/shard_map/all_to_all | solution.py:30
  99.5 4.2 %all-to-all-start.2 = ((bf16[8,160,384]{2,1,0:T(8,128)(2,1)}), bf16[8,160,384]{2,1,0:T(8,128)(2,1)}, u32[]{:S(2)}, u32[]{:S(2)}) async-start(bf16[8,160,384]{2,1,0:T(8,128)(2,1)} %bitcast.100), calls=%async_computation.2 | async-start | bytes 1966080 | tf_op jit(solution)/shard_map/all_to_all | solution.py:30
  104.8 2.6 %fusion.17 = bf16[160,64]{0,1:T(8,128)(2,1)S(1)} fusion(bf16[224,6144]{1,0:T(8,128)(2,1)} %all-gather.2.cloned.1.call-done), kind=kOutput, calls=%fused_computation.23 | convolution fusion | flops 125849600 | bytes 2772992 | tf_op jit(solution)/shard_map/dot_general | solution.py:122
  108.3 1.9 multiply_reduce_fusion
  112.0 19.7 %all-to-all-done.2 = bf16[8,160,384]{2,1,0:T(8,128)(2,1)} async-done(((bf16[8,160,384]{2,1,0:T(8,128)(2,1)}), bf16[8,160,384]{2,1,0:T(8,128)(2,1)}, u32[]{:S(2)}, u32[]{:S(2)}) %all-to-all-start.2) | async-done | bytes 983072 | tf_op jit(solution)/shard_map/all_to_all | solution.py:30
  131.6 5.5 %all-to-all-start.5 = ((bf16[64,8,128]{2,1,0:T(8,128)(2,1)}), bf16[64,8,128]{2,1,0:T(8,128)(2,1)S(1)}, u32[]{:S(2)}, u32[]{:S(2)}) async-start(bf16[64,8,128]{2,1,0:T(8,128)(2,1)} %copy.126), calls=%async_computation.5 | async-start | bytes 262144 | tf_op jit(solution)/shard_map/all_to_all | solution.py:30
  138.5 8.2 %all-to-all-done.5 = bf16[64,8,128]{2,1,0:T(8,128)(2,1)S(1)} async-done(((bf16[64,8,128]{2,1,0:T(8,128)(2,1)}), bf16[64,8,128]{2,1,0:T(8,128)(2,1)S(1)}, u32[]{:S(2)}, u32[]{:S(2)}) %all-to-all-start.5) | async-done | bytes 131104 | tf_op jit(solution)/shard_map/all_to_all | solution.py:30
  147.9 5.5 %all-to-all-start.7 = ((bf16[64,5,128]{2,1,0:T(8,128)(2,1)}), bf16[64,5,128]{2,1,0:T(8,128)(2,1)S(1)}, u32[]{:S(2)}, u32[]{:S(2)}) async-start(bf16[64,5,128]{2,1,0:T(8,128)(2,1)} %reshape.183), calls=%async_computation.7 | async-start | bytes 262144 | tf_op jit(solution)/shard_map/all_to_all | solution.py:30
  155.2 7.7 %all-to-all-done.7 = bf16[64,5,128]{2,1,0:T(8,128)(2,1)S(1)} async-done(((bf16[64,5,128]{2,1,0:T(8,128)(2,1)}), bf16[64,5,128]{2,1,0:T(8,128)(2,1)S(1)}, u32[]{:S(2)}, u32[]{:S(2)}) %all-to-all-start.7) | async-done | bytes 81952 | tf_op jit(solution)/shard_map/all_to_all | solution.py:30
  162.9 6.1 %all-to-all-start.6 = ((bf16[32,22,384]{2,1,0:T(8,128)(2,1)}), bf16[32,22,384]{2,1,0:T(8,128)(2,1)S(1)}, u32[]{:S(2)}, u32[]{:S(2)}) async-start(bf16[32,22,384]{2,1,0:T(8,128)(2,1)} %pad_maximum_fusion), calls=%async_computation.6 | async-start | bytes 1179648 | tf_op jit(solution)/shard_map/all_to_all | solution.py:30
  170.8 16.9 %all-to-all-done.6 = bf16[32,22,384]{2,1,0:T(8,128)(2,1)S(1)} async-done(((bf16[32,22,384]{2,1,0:T(8,128)(2,1)}), bf16[32,22,384]{2,1,0:T(8,128)(2,1)S(1)}, u32[]{:S(2)}, u32[]{:S(2)}) %all-to-all-start.6) | async-done | bytes 540704 | tf_op jit(solution)/shard_map/all_to_all | solution.py:30
  (126 shorter events, 25.9 us)
Async XLA Ops:
  7.2 14.6 %copy-start = (bf16[8,64,384]{2,1,0:T(8,128)(2,1)S(1)}, bf16[8,64,384]{2,1,0:T(8,128)(2,1)}, u32[]{:S(2)}) copy-start(bf16[8,64,384]{2,1,0:T(8,128)(2,1)} %param.17) | copy-start | bytes 1179652
  7.2 26.3 %copy-start.19 = (s32[256]{0:T(256)S(1)}, s32[256]{0:T(256)}, u32[]{:S(2)}) copy-start(s32[256]{0:T(256)} %param.15) | copy-start | bytes 3076
  7.2 26.3 %copy-start.13 = (bf16[160,256]{1,0:T(8,128)(2,1)S(1)}, bf16[160,256]{1,0:T(8,128)(2,1)}, u32[]{:S(2)}) copy-start(bf16[160,256]{1,0:T(8,128)(2,1)} %param.12) | copy-start | bytes 245764
  11.5 21.2 %all-to-all-start.3 = ((bf16[32,5,384]{2,1,0:T(8,128)(2,1)}), bf16[32,5,384]{2,1,0:T(8,128)(2,1)S(1)}, u32[]{:S(2)}, u32[]{:S(2)}) async-start(bf16[32,5,384]{2,1,0:T(8,128)(2,1)} %all_to_all.35), calls=%async_computation.3 | async-start | bytes 393216 | tf_op jit(solution)/shard_map/all_to_all | solution.py:30
  21.7 83.0 %all-gather.2.cloned.1.call-start = ((), (), s32[]{:S(2)}) async-start(), calls=%async_computation.8 | async-start | bytes 2924544 | tf_op jit(solution)/shard_map/all_gather | solution.py:92
  21.8 25.4 %copy-start.7 = (bf16[64,384]{1,0:T(8,128)(2,1)}, bf16[64,384]{1,0:T(8,128)(2,1)S(1)}, u32[]{:S(2)}) copy-start(bf16[64,384]{1,0:T(8,128)(2,1)S(1)} %dynamic-slice_bitcast_fusion) | copy-start | bytes 147460
  32.8 14.4 %copy-start.4 = (bf16[160,384]{1,0:T(8,128)(2,1)}, bf16[160,384]{1,0:T(8,128)(2,1)S(1)}, u32[]{:S(2)}) copy-start(bf16[160,384]{1,0:T(8,128)(2,1)S(1)} %all_to_all.37) | copy-start | bytes 368644
  34.4 22.2 %all-to-all-start = ((bf16[64,5,128]{2,1,0:T(8,128)(2,1)}), bf16[64,5,128]{2,1,0:T(8,128)(2,1)}, u32[]{:S(2)}, u32[]{:S(2)}) async-start(bf16[64,5,128]{2,1,0:T(8,128)(2,1)} %copy.119), calls=%async_computation | async-start | bytes 262144 | tf_op jit(solution)/shard_map/all_to_all | solution.py:30
  60.0 16.4 %all-to-all-start.1 = ((bf16[64,5,128]{2,1,0:T(8,128)(2,1)}), bf16[64,5,128]{2,1,0:T(8,128)(2,1)}, u32[]{:S(2)}, u32[]{:S(2)}) async-start(bf16[64,5,128]{2,1,0:T(8,128)(2,1)} %reshape.167), calls=%async_computation.1 | async-start | bytes 262144 | tf_op jit(solution)/shard_map/all_to_all | solution.py:30
  81.5 9.1 %collective-permute-start = (bf16[160,3072]{1,0:T(8,128)(2,1)}, bf16[160,3072]{1,0:T(8,128)(2,1)}, u32[]{:S(2)}, u32[]{:S(2)}) collective-permute-start(bf16[160,3072]{1,0:T(8,128)(2,1)} %convolution_convert_fusion), channel_id=1, source_target_pairs={{0,1},{1,0},{2,3},{3,2},{4,5},{5,4},{6,7},{7,6},{8,9},{9,8},{10,11... | collective-permute-start | bytes 2949128 | tf_op jit(solution)/shard_map/ppermute | solution.py:115
  84.4 15.1 %all-to-all-start.4 = ((bf16[64,1,160]{2,1,0:T(2,128)(2,1)}), bf16[64,1,160]{2,1,0:T(2,128)(2,1)}, u32[]{:S(2)}, u32[]{:S(2)}) async-start(bf16[64,1,160]{2,1,0:T(2,128)(2,1)} %copy.125), calls=%async_computation.4 | async-start | bytes 131072 | tf_op jit(solution)/shard_map/all_to_all | solution.py:30
  99.5 32.1 %all-to-all-start.2 = ((bf16[8,160,384]{2,1,0:T(8,128)(2,1)}), bf16[8,160,384]{2,1,0:T(8,128)(2,1)}, u32[]{:S(2)}, u32[]{:S(2)}) async-start(bf16[8,160,384]{2,1,0:T(8,128)(2,1)} %bitcast.100), calls=%async_computation.2 | async-start | bytes 1966080 | tf_op jit(solution)/shard_map/all_to_all | solution.py:30
  110.2 36.8 %copy-start.14 = (bf16[64,64]{1,0:T(8,128)(2,1)S(1)}, bf16[64,64]{1,0:T(8,128)(2,1)}, u32[]{:S(2)}) copy-start(bf16[64,64]{1,0:T(8,128)(2,1)} %constant.84.clone) | copy-start | bytes 24580
  110.2 43.2 %copy-start.8 = (bf16[64,384]{1,0:T(8,128)(2,1)S(1)}, bf16[64,384]{1,0:T(8,128)(2,1)}, u32[]{:S(2)}) copy-start(bf16[64,384]{1,0:T(8,128)(2,1)} %copy-done.7) | copy-start | bytes 147460
  110.3 43.3 %copy-start.5 = (bf16[160,384]{1,0:T(8,128)(2,1)S(1)}, bf16[160,384]{1,0:T(8,128)(2,1)}, u32[]{:S(2)}) copy-start(bf16[160,384]{1,0:T(8,128)(2,1)} %copy-done.4) | copy-start | bytes 368644
  131.6 15.0 %all-to-all-start.5 = ((bf16[64,8,128]{2,1,0:T(8,128)(2,1)}), bf16[64,8,128]{2,1,0:T(8,128)(2,1)S(1)}, u32[]{:S(2)}, u32[]{:S(2)}) async-start(bf16[64,8,128]{2,1,0:T(8,128)(2,1)} %copy.126), calls=%async_computation.5 | async-start | bytes 262144 | tf_op jit(solution)/shard_map/all_to_all | solution.py:30
  147.9 15.1 %all-to-all-start.7 = ((bf16[64,5,128]{2,1,0:T(8,128)(2,1)}), bf16[64,5,128]{2,1,0:T(8,128)(2,1)S(1)}, u32[]{:S(2)}, u32[]{:S(2)}) async-start(bf16[64,5,128]{2,1,0:T(8,128)(2,1)} %reshape.183), calls=%async_computation.7 | async-start | bytes 262144 | tf_op jit(solution)/shard_map/all_to_all | solution.py:30
  153.4 15.6 %copy-start.18 = (s32[32]{0:T(128)S(1)}, s32[32]{0:T(128)}, u32[]{:S(2)}) copy-start(s32[32]{0:T(128)} %copy-done.17) | copy-start | bytes 388
  153.4 15.8 %copy-start.15 = (s32[16,2]{0,1:T(2,128)S(1)}, s32[16,2]{0,1:T(2,128)}, u32[]{:S(2)}) copy-start(s32[16,2]{0,1:T(2,128)} %param.18) | copy-start | bytes 388
  153.4 15.8 %copy-start.16 = (f32[16,2]{0,1:T(2,128)S(1)}, f32[16,2]{0,1:T(2,128)}, u32[]{:S(2)}) copy-start(f32[16,2]{0,1:T(2,128)} %param.19) | copy-start | bytes 388
  153.4 15.8 %copy-start.3 = (bf16[160,256]{1,0:T(8,128)(2,1)S(1)}, bf16[160,256]{1,0:T(8,128)(2,1)}, u32[]{:S(2)}) copy-start(bf16[160,256]{1,0:T(8,128)(2,1)} %copy-done.1) | copy-start | bytes 245764
  153.4 15.8 %copy-start.12 = (bf16[160,64]{0,1:T(8,128)(2,1)S(1)}, bf16[160,64]{0,1:T(8,128)(2,1)}, u32[]{:S(2)}) copy-start(bf16[160,64]{0,1:T(8,128)(2,1)} %copy-done.11) | copy-start | bytes 61444
  154.1 33.9 %copy-start.21 = (s32[32]{0:T(128)S(1)}, s32[32]{0:T(128)}, u32[]{:S(2)}) copy-start(s32[32]{0:T(128)} %copy-done.20) | copy-start | bytes 388
  162.9 24.8 %all-to-all-start.6 = ((bf16[32,22,384]{2,1,0:T(8,128)(2,1)}), bf16[32,22,384]{2,1,0:T(8,128)(2,1)S(1)}, u32[]{:S(2)}, u32[]{:S(2)}) async-start(bf16[32,22,384]{2,1,0:T(8,128)(2,1)} %pad_maximum_fusion), calls=%async_computation.6 | async-start | bytes 1179648 | tf_op jit(solution)/shard_map/all_to_all | solution.py:30
  (9 other events, 27.4 us)
Sparse Core Ops, SparseCore 0:
  33.6 46.0 all-gather.1

commit v2 on v1

v2 whole, which is shorter than its diff:
```python
import math

import jax
import jax.numpy as jnp
import numpy as np
from jax import lax
from jax.sharding import Mesh
from jax.sharding import PartitionSpec as P

HIDDEN_UNITS = 16384
EXPERT_COUNT = 8
LOWRANK_SCALE = 0.5
HIGH_ACCURACY = lax.Precision.HIGHEST
BF = jnp.bfloat16
F32 = jnp.float32
EXPERT = ("e", "r")
TENSOR = ("z", "c")
LANES = 128


def sylvester(count):
    table = np.ones((1, 1), np.float32)
    while table.shape[0] < count:
        table = np.kron(np.array([[1.0, 1.0], [1.0, -1.0]], np.float32), table)
    return jnp.asarray(table, BF)


def exchange(value, axes):
    return lax.all_to_all(value, axes, split_axis=0, concat_axis=0, tiled=True)


def swapped(value, axis, bit):
    size = lax.axis_size(axis)
    return lax.ppermute(value, axis, [(i, i ^ 1 << bit) for i in range(size)])


def split(values):
    high = lax.reduce_precision(values, 8, 7)
    return high, lax.reduce_precision(values - high, 8, 7)


def butterfly(values, axis, bit, sums=(), exact=(), wire=BF):
    own = jnp.where(lax.axis_index(axis) // (1 << bit) % 2 == 1, -1.0, 1.0)
    parts = [values, *sums]
    for item in exact:
        parts += split(item) if wire == BF else [item]
    width = sum(part.shape[1] for part in parts)
    if width % LANES:
        parts.append(jnp.zeros((values.shape[0], -width % LANES), F32))
    message = jnp.concatenate(parts, axis=1) if len(parts) > 1 else values
    arrived = swapped(message.astype(wire), axis, bit).astype(F32)
    start = values.shape[1]
    values = arrived[:, :start] + own * values
    new_sums, new_exact = [], []
    for item in sums:
        new_sums.append(item + arrived[:, start : start + item.shape[1]])
        start += item.shape[1]
    for item in exact:
        size = item.shape[1]
        if wire == BF:
            high, low = split(item)
            other = arrived[:, start : start + size] + arrived[:, start + size : start + 2 * size]
            new_exact.append((high + low) + other)
            start += 2 * size
        else:
            new_exact.append(item + arrived[:, start : start + size])
            start += size
    return values, tuple(new_sums), tuple(new_exact)


def body(
    hidden, codes, scales, signs, lowrank_down_map, lowrank_up_map, experts, gates, output_gradient
):
    slot_rows, stride = hidden.shape
    replicas, depth, cores = lax.axis_size("r"), lax.axis_size("z"), lax.axis_size("c")
    devices = EXPERT_COUNT * replicas
    rank = lowrank_down_map.shape[1]
    expert_position = lax.axis_index("e")
    replica = lax.axis_index("r")
    core = lax.axis_index("c")
    capacity = slot_rows // devices
    tokens_here = experts.shape[0]
    columns = output_gradient.shape[1]
    scaling = 1.0 / math.sqrt(HIDDEN_UNITS)
    sign_values = (2 * signs - 1).astype(F32)
    group_size = codes.shape[0] // scales.shape[0]

    flat_ids = experts.reshape(tokens_here * 2)
    assigned = (flat_ids[:, None] == jnp.arange(EXPERT_COUNT, dtype=jnp.int32)[None, :]).astype(
        jnp.int32
    )
    earlier = jnp.cumsum(assigned, axis=0) - assigned
    slot_index = jnp.sum(earlier * assigned, axis=1)
    target = flat_ids * capacity + slot_index
    row = jnp.arange(devices * capacity, dtype=jnp.int32)
    row_slot = row // (replicas * capacity) * capacity + row % capacity
    copier = (row_slot[:, None] == target[None, :]).astype(BF)
    weighted = (
        (gates[:, :, None] * output_gradient.astype(F32)[:, None, :])
        .reshape(tokens_here * 2, columns)
        .astype(BF)
    )
    outgoing = jnp.dot(copier, weighted, preferred_element_type=F32).astype(BF)
    d_rows = exchange(outgoing, EXPERT)
    lowrank_local = lax.dynamic_index_in_dim(lowrank_up_map, expert_position, 0, keepdims=False)
    d_own = exchange(jnp.broadcast_to(d_rows[None], (depth, slot_rows, columns)), "z")
    d_other = swapped(d_own, "c", 0)

    spread_local = sylvester(stride)
    signed = (hidden.astype(F32) * sign_values).astype(BF)
    state = jnp.dot(signed, spread_local, preferred_element_type=F32)
    for bit in range(replicas.bit_length() - 1):
        state, _, _ = butterfly(state, "r", bit, wire=F32)
    adapter_grad = LOWRANK_SCALE * lax.dot_general(
        d_rows, lowrank_local, (((1,), (1,)), ((), ())), preferred_element_type=F32
    )
    state, _, (adapter_grad,) = butterfly(state, "c", 0, exact=(adapter_grad,), wire=F32)
    for bit in range(depth.bit_length() - 1):
        state, _, (adapter_grad,) = butterfly(state, "z", bit, exact=(adapter_grad,))
    rotated = (state * scaling).astype(BF)

    weights = (codes.astype(F32) * jnp.repeat(scales, group_size, axis=0)).astype(BF)
    adapter_part = jnp.dot(rotated, lowrank_down_map, preferred_element_type=F32)

    by_depth = weights.reshape(stride, depth, cores, columns)
    own = lax.dynamic_index_in_dim(by_depth, core, 2, keepdims=False)
    other = lax.dynamic_index_in_dim(by_depth, 1 - core, 2, keepdims=False)

    def forward(part):
        return jnp.einsum("sk,kzf->zsf", rotated, part, preferred_element_type=F32)

    arrived = swapped(forward(other).astype(BF), "c", 0)
    pair = (forward(own) + arrived.astype(F32)).astype(BF)

    def backward(cotangent, part):
        return jnp.einsum("zsf,kzf->sk", cotangent, part, preferred_element_type=F32)

    d_rotated = (
        backward(d_own, own)
        + backward(d_other, other)
        + lax.dot_general(
            adapter_grad.astype(BF),
            lowrank_down_map,
            (((1,), (1,)), ((), ())),
            preferred_element_type=F32,
        )
    )
    row_product = jnp.sum(rotated.astype(F32) * d_rotated, axis=1, keepdims=True)
    down_map_gradient = lax.dot_general(
        rotated, adapter_grad.astype(BF), (((0,), (0,)), ((), ())), preferred_element_type=F32
    )
    d_local = jnp.dot(d_rotated.astype(BF), spread_local, preferred_element_type=F32)
    d_local, pair = lax.optimization_barrier((d_local, pair))
    frozen = exchange(pair, "z").astype(F32).sum(axis=0)
    state, sums, exact = d_local, (adapter_part,), (row_product,)
    for bit in range(replicas.bit_length() - 1):
        state, sums, exact = butterfly(state, "r", bit, sums, exact)
    state, sums, exact = butterfly(state, "c", 0, sums, exact, wire=F32)
    for bit in range(depth.bit_length() - 1):
        state, sums, exact = butterfly(state, "z", bit, sums, exact)
    hidden_gradient = (state * (sign_values * scaling)[None, :]).astype(BF)
    adapter_in = sums[0]
    row_total = exact[0][:, 0]

    slot_output = frozen + (LOWRANK_SCALE / replicas) * jnp.dot(
        adapter_in.astype(BF), lowrank_local, preferred_element_type=F32
    )
    share = rank // replicas
    adapter_share = lax.dynamic_slice_in_dim(adapter_in, replica * share, share, 1)
    adapter_share = jnp.concatenate(split(adapter_share), axis=1).astype(BF)
    up_share = LOWRANK_SCALE * lax.dot_general(
        adapter_share, d_rows, (((0,), (0,)), ((), ())), preferred_element_type=F32
    )
    up_share = up_share[:share] + up_share[share:]
    totals = jnp.concatenate(
        [part.astype(BF).reshape(devices, capacity) for part in split(row_total)], axis=1
    )
    totals = jnp.pad(totals, ((0, 0), (0, columns - 2 * capacity)))[:, None, :]
    parcel = jnp.concatenate(
        [
            slot_output.astype(BF).reshape(devices, capacity, columns),
            totals,
            jnp.broadcast_to(up_share.astype(BF)[None], (devices, share, columns)),
        ],
        axis=1,
    )
    parcel = exchange(parcel, EXPERT)
    up_map_gradient = (
        parcel[:, capacity + 1 :].astype(F32).reshape(EXPERT_COUNT, rank, columns)
    )
    summed = (
        parcel[:, :capacity]
        .astype(F32)
        .reshape(EXPERT_COUNT, replicas, capacity, columns)
        .sum(axis=1)
        .reshape(EXPERT_COUNT * capacity, columns)
    )
    totals = parcel.reshape(EXPERT_COUNT, replicas, capacity + 1 + share, columns)[:, 0, capacity]
    totals = totals[:, : 2 * capacity].astype(F32)
    totals = (totals[:, :capacity] + totals[:, capacity:]).reshape(EXPERT_COUNT * capacity)
    slot_id = jnp.arange(EXPERT_COUNT * capacity, dtype=jnp.int32)
    chosen = target[:, None] == slot_id[None, :]
    gates_gradient = jnp.sum(jnp.where(chosen, totals[None, :], 0.0), axis=1)
    gates_gradient = gates_gradient.reshape(tokens_here, 2) / gates
    chosen = chosen.reshape(tokens_here, 2, EXPERT_COUNT * capacity)
    mixer = jnp.sum(jnp.where(chosen, gates[:, :, None], 0.0), axis=1)
    mixed = jnp.dot(mixer, summed, precision=HIGH_ACCURACY).astype(BF)
    return (mixed, hidden_gradient, down_map_gradient, up_map_gradient, gates_gradient)


def solution(mesh):
    owners, tensor = mesh.devices.shape
    split = Mesh(
        mesh.devices.reshape(EXPERT_COUNT, owners // EXPERT_COUNT, tensor // 2, 2),
        ("e", "r", "z", "c"),
    )
    every = EXPERT + TENSOR
    placed = (
        P(None, every),
        P(every, None),
        P(every, None),
        P(every),
        P(every, None),
        P(None, None, TENSOR),
        P(EXPERT, None),
        P(EXPERT, None),
        P(EXPERT, TENSOR),
    )
    return jax.shard_map(
        body,
        mesh=split,
        in_specs=placed,
        out_specs=(
            P(EXPERT, TENSOR),
            P(None, every),
            P(every, None),
            P(None, None, TENSOR),
            P(EXPERT, None),
        ),
        check_vma=False,
    )
```

time: 199 us -> 241 us (1.21)
  the two profiles are of different devices: /device:TPU:8 before, /device:TPU:72 now
where the time goes in v2:
time: 241 us; the launch traced here: 240 us
  waiting for transfers between devices  97.1 us (40%)
  starting transfers between devices  85.7 us (36%)
  local copies, waits for them, and re-layouts  25.4 us (11%)
  other arithmetic  19.1 us (8%)
  matrix products  11.3 us (5%)
    ppermute x14, waiting for transfers between devices, swapped(): return lax.ppermute(value, axis, [(i, i ^ 1 << bit) for i in range(size)])  73.7 us
    ppermute x14, starting transfers between devices, swapped(): return lax.ppermute(value, axis, [(i, i ^ 1 << bit) for i in range(size)])  48.9 us
    all_to_all x4, starting transfers between devices, exchange(): return lax.all_to_all(value, axes, split_axis=0, concat_axis=0, tiled=True)  36.9 us
    all_to_all x4, waiting for transfers between devices, exchange(): return lax.all_to_all(value, axes, split_axis=0, concat_axis=0, tiled=True)  23.4 us
    dynamic_slice x1, local copies, waits for them, and re-layouts, body(): other = lax.dynamic_index_in_dim(by_depth, 1 - core, 2, keepdims=False)  9.06 us
    reshape x1, local copies, waits for them, and re-layouts, body(): by_depth = weights.reshape(stride, depth, cores, columns)  7.06 us
    another operation x26, other arithmetic  5.03 us
  transfers between devices with their start and end apart: 18, of which 12 were waited for; matrix products, arithmetic and copies ran while one was open for 17% of the time, Pallas kernels for 0%

profile of v2, /device:TPU:72, one launch (start us, length us, event | category | flops | bytes accessed | tf_op | source)
XLA Modules:
  0.0 240.2 jit_solution(5462549696370374935)
XLA Ops:
  8.7 10.4 %all-to-all-start = ((bf16[32,5,384]{2,1,0:T(8,128)(2,1)}), bf16[32,5,384]{2,1,0:T(8,128)(2,1)S(1)}, u32[]{:S(2)}, u32[]{:S(2)}) async-start(bf16[32,5,384]{2,1,0:T(8,128)(2,1)} %all_to_all.15), calls=%async_computation | async-start | bytes 393216 | tf_op jit(solution)/shard_map/all_to_all | solution.py:29
  19.3 4.3 %collective-permute-start.2 = (f32[160,256]{0,1:T(8,128)S(1)}, f32[160,256]{0,1:T(8,128)S(1)}, u32[]{:S(2)}, u32[]{:S(2)}) collective-permute-start(f32[160,256]{0,1:T(8,128)S(1)} %multiply_add_fusion.1), channel_id=1, source_target_pairs={{0,32},{16,48},{32,0},{48,16},{1,33},{17,49},{33,1},{49,17},{2,34}... | collective-permute-start | bytes 491528 | tf_op jit(solution)/shard_map/ppermute | solution.py:34
  23.6 6.3 %all-to-all-done = bf16[32,5,384]{2,1,0:T(8,128)(2,1)S(1)} async-done(((bf16[32,5,384]{2,1,0:T(8,128)(2,1)}), bf16[32,5,384]{2,1,0:T(8,128)(2,1)S(1)}, u32[]{:S(2)}, u32[]{:S(2)}) %all-to-all-start) | async-done | bytes 122912 | tf_op jit(solution)/shard_map/all_to_all | solution.py:29
  30.1 4.3 %collective-permute-done.2 = f32[160,256]{0,1:T(8,128)S(1)} collective-permute-done((f32[160,256]{0,1:T(8,128)S(1)}, f32[160,256]{0,1:T(8,128)S(1)}, u32[]{:S(2)}, u32[]{:S(2)}) %collective-permute-start.2) | collective-permute-done | bytes 163872 | tf_op jit(solution)/shard_map/ppermute | solution.py:34
  41.3 11.4 %all-to-all-start.1 = ((bf16[8,160,384]{2,1,0:T(8,128)(2,1)}), bf16[8,160,384]{2,1,0:T(8,128)(2,1)}, u32[]{:S(2)}, u32[]{:S(2)}) async-start(bf16[8,160,384]{2,1,0:T(8,128)(2,1)} %broadcast_in_dim.66), calls=%async_computation.1 | async-start | bytes 1966080 | tf_op jit(solution)/shard_map/all_to_all | solution.py:29
  54.9 4.3 %collective-permute-start.5 = (bf16[160,384]{0,1:T(8,128)(2,1)}, bf16[160,384]{0,1:T(8,128)(2,1)}, u32[]{:S(2)}, u32[]{:S(2)}) collective-permute-start(bf16[160,384]{0,1:T(8,128)(2,1)} %pad_maximum_fusion.2), channel_id=1, source_target_pairs={{0,4},{2,6},{4,0},{6,2},{8,12},{10,14},{12,8},{14,10},{1,5},{3,7},... | collective-permute-start | bytes 368648 | tf_op jit(solution)/shard_map/ppermute | solution.py:34
  59.2 4.3 %fusion = bf16[256,6144]{1,0:T(8,128)(2,1)} fusion(bf16[256,6144]{1,0:T(8,128)(2,1)} %param.11, f32[4,6144]{1,0:T(4,128)S(1)} %copy-done.16), kind=kLoop, calls=%fused_computation.1 | loop fusion | flops 4718592 | bytes 6389760 | tf_op jit(solution)/shard_map/convert_element_type | solution.py:122
  63.5 7.1 %reshape.136 = bf16[256,8,2,384]{3,2,1,0:T(2,128)(2,1)S(1)} reshape(bf16[256,6144]{1,0:T(8,128)(2,1)} %fusion) | data formatting | bytes 6291456 | tf_op jit(solution)/shard_map/reshape | solution.py:125
  70.5 11.4 %collective-permute-done.5 = bf16[160,384]{0,1:T(8,128)(2,1)} collective-permute-done((bf16[160,384]{0,1:T(8,128)(2,1)}, bf16[160,384]{0,1:T(8,128)(2,1)}, u32[]{:S(2)}, u32[]{:S(2)}) %collective-permute-start.5) | collective-permute-done | bytes 122912 | tf_op jit(solution)/shard_map/ppermute | solution.py:34
  90.9 6.8 %collective-permute-start.6 = (bf16[160,384]{0,1:T(8,128)(2,1)}, bf16[160,384]{0,1:T(8,128)(2,1)}, u32[]{:S(2)}, u32[]{:S(2)}) collective-permute-start(bf16[160,384]{0,1:T(8,128)(2,1)} %pad_maximum_fusion.3), channel_id=1, source_target_pairs={{0,8},{2,10},{4,12},{6,14},{8,0},{10,2},{12,4},{14,6},{1,9},{3,11}... | collective-permute-start | bytes 368648 | tf_op jit(solution)/shard_map/ppermute | solution.py:34
  97.7 9.1 %constant_dynamic-slice_fusion = (bf16[256,8,1,384]{3,2,1,0:T(2,128)(2,1)}, bf16[256,8,1,384]{3,2,1,0:T(2,128)(2,1)}) fusion(bf16[256,8,2,384]{3,2,1,0:T(2,128)(2,1)S(1)} %reshape.136, s32[]{:T(128)S(6)} %select_n.128, s32[]{:T(128)S(6)} %select_n.127), kind=kLoop, calls=%fused_computation.155 | loop fusion | bytes 6291464 | tf_op jit(solution)/shard_map/jit(dynamic_index_in_dim)/dynamic_slice | solution.py:127
  108.8 2.9 %convolution_bitcast_fusion.1 = f32[160,256]{0,1:T(8,128)S(1)} fusion(bf16[8,160,384]{2,1,0:T(8,128)(2,1)} %all-to-all-done.1, bf16[256,8,1,384]{3,2,1,0:T(2,128)(2,1)} %get-tuple-element.58), kind=kOutput, calls=%fused_computation.10 | convolution fusion | flops 251658240 | bytes 2719744 | tf_op jit(solution)/shard_map/zsf,kzf->sk/dot_general | solution.py:136
  121.3 5.3 %collective-permute-start.8 = (bf16[160,384]{0,1:T(8,128)(2,1)S(1)}, bf16[160,384]{0,1:T(8,128)(2,1)S(1)}, u32[]{:S(2)}, u32[]{:S(2)}) collective-permute-start(bf16[160,384]{0,1:T(8,128)(2,1)S(1)} %concatenate.52), channel_id=1, source_target_pairs={{0,16},{16,0},{32,48},{48,32},{1,17},{17,1},{33,49},{49,33},{2,18}... | collective-permute-start | bytes 368648 | tf_op jit(solution)/shard_map/ppermute | solution.py:34
  126.5 5.3 %collective-permute-done.8 = bf16[160,384]{0,1:T(8,128)(2,1)S(1)} collective-permute-done((bf16[160,384]{0,1:T(8,128)(2,1)S(1)}, bf16[160,384]{0,1:T(8,128)(2,1)S(1)}, u32[]{:S(2)}, u32[]{:S(2)}) %collective-permute-start.8) | collective-permute-done | bytes 122912 | tf_op jit(solution)/shard_map/ppermute | solution.py:34
  132.2 3.7 %collective-permute-start.9 = (bf16[160,384]{0,1:T(8,128)(2,1)S(1)}, bf16[160,384]{0,1:T(8,128)(2,1)S(1)}, u32[]{:S(2)}, u32[]{:S(2)}) collective-permute-start(bf16[160,384]{0,1:T(8,128)(2,1)S(1)} %concatenate.53), channel_id=1, source_target_pairs={{0,32},{16,48},{32,0},{48,16},{1,33},{17,49},{33,1},{49,17},{2,34}... | collective-permute-start | bytes 368648 | tf_op jit(solution)/shard_map/ppermute | solution.py:34
  135.9 7.8 %collective-permute-done.9 = bf16[160,384]{0,1:T(8,128)(2,1)S(1)} collective-permute-done((bf16[160,384]{0,1:T(8,128)(2,1)S(1)}, bf16[160,384]{0,1:T(8,128)(2,1)S(1)}, u32[]{:S(2)}, u32[]{:S(2)}) %collective-permute-start.9) | collective-permute-done | bytes 122912 | tf_op jit(solution)/shard_map/ppermute | solution.py:34
  148.0 7.0 %collective-permute-start.11 = (bf16[160,384]{0,1:T(8,128)(2,1)S(1)}, bf16[160,384]{0,1:T(8,128)(2,1)S(1)}, u32[]{:S(2)}, u32[]{:S(2)}) collective-permute-start(bf16[160,384]{0,1:T(8,128)(2,1)S(1)} %concatenate.55), channel_id=1, source_target_pairs={{0,2},{2,0},{4,6},{6,4},{8,10},{10,8},{12,14},{14,12},{1,3},{3,1},... | collective-permute-start | bytes 368648 | tf_op jit(solution)/shard_map/ppermute | solution.py:34
  154.9 5.2 %collective-permute-done.11 = bf16[160,384]{0,1:T(8,128)(2,1)S(1)} collective-permute-done((bf16[160,384]{0,1:T(8,128)(2,1)S(1)}, bf16[160,384]{0,1:T(8,128)(2,1)S(1)}, u32[]{:S(2)}, u32[]{:S(2)}) %collective-permute-start.11) | collective-permute-done | bytes 122912 | tf_op jit(solution)/shard_map/ppermute | solution.py:34
  160.5 3.5 %collective-permute-start.12 = (bf16[160,384]{0,1:T(8,128)(2,1)S(1)}, bf16[160,384]{0,1:T(8,128)(2,1)S(1)}, u32[]{:S(2)}, u32[]{:S(2)}) collective-permute-start(bf16[160,384]{0,1:T(8,128)(2,1)S(1)} %concatenate.56), channel_id=1, source_target_pairs={{0,4},{2,6},{4,0},{6,2},{8,12},{10,14},{12,8},{14,10},{1,5},{3,7},... | collective-permute-start | bytes 368648 | tf_op jit(solution)/shard_map/ppermute | solution.py:34
  164.0 4.6 %all-to-all-start.2 = ((bf16[8,160,384]{2,1,0:T(8,128)(2,1)}), bf16[8,160,384]{2,1,0:T(8,128)(2,1)S(1)}, u32[]{:S(2)}, u32[]{:S(2)}) async-start(bf16[8,160,384]{2,1,0:T(8,128)(2,1)} %fusion.1), calls=%async_computation.2 | async-start | bytes 1966080 | tf_op jit(solution)/shard_map/all_to_all | solution.py:29
  168.6 9.7 %collective-permute-done.12 = bf16[160,384]{0,1:T(8,128)(2,1)S(1)} collective-permute-done((bf16[160,384]{0,1:T(8,128)(2,1)S(1)}, bf16[160,384]{0,1:T(8,128)(2,1)S(1)}, u32[]{:S(2)}, u32[]{:S(2)}) %collective-permute-start.12) | collective-permute-done | bytes 122912 | tf_op jit(solution)/shard_map/ppermute | solution.py:34
  180.8 24.6 %collective-permute-done.13 = bf16[160,384]{0,1:T(8,128)(2,1)S(1)} collective-permute-done((bf16[160,384]{0,1:T(8,128)(2,1)S(1)}, bf16[160,384]{0,1:T(8,128)(2,1)S(1)}, u32[]{:S(2)}, u32[]{:S(2)}) %collective-permute-start.13) | collective-permute-done | bytes 122912 | tf_op jit(solution)/shard_map/ppermute | solution.py:34
  207.6 10.5 %all-to-all-start.3 = ((bf16[32,22,384]{2,1,0:T(8,128)(2,1)}), bf16[32,22,384]{2,1,0:T(8,128)(2,1)S(1)}, u32[]{:S(2)}, u32[]{:S(2)}) async-start(bf16[32,22,384]{2,1,0:T(8,128)(2,1)} %pad_maximum_fusion), calls=%async_computation.3 | async-start | bytes 1179648 | tf_op jit(solution)/shard_map/all_to_all | solution.py:29
  220.0 17.2 %all-to-all-done.3 = bf16[32,22,384]{2,1,0:T(8,128)(2,1)S(1)} async-done(((bf16[32,22,384]{2,1,0:T(8,128)(2,1)}), bf16[32,22,384]{2,1,0:T(8,128)(2,1)S(1)}, u32[]{:S(2)}, u32[]{:S(2)}) %all-to-all-start.3) | async-done | bytes 540704 | tf_op jit(solution)/shard_map/all_to_all | solution.py:29
  (175 shorter events, 52.1 us)
Async XLA Ops:
  2.6 16.7 %collective-permute-start.1 = (f32[160,256]{0,1:T(8,128)S(1)}, f32[160,256]{0,1:T(8,128)S(1)}, u32[]{:S(2)}, u32[]{:S(2)}) collective-permute-start(f32[160,256]{0,1:T(8,128)S(1)} %fusion.19), channel_id=1, source_target_pairs={{0,16},{16,0},{32,48},{48,32},{1,17},{17,1},{33,49},{49,33},{2,18}... | collective-permute-start | bytes 491528 | tf_op jit(solution)/shard_map/ppermute | solution.py:34
  8.7 21.1 %all-to-all-start = ((bf16[32,5,384]{2,1,0:T(8,128)(2,1)}), bf16[32,5,384]{2,1,0:T(8,128)(2,1)S(1)}, u32[]{:S(2)}, u32[]{:S(2)}) async-start(bf16[32,5,384]{2,1,0:T(8,128)(2,1)} %all_to_all.15), calls=%async_computation | async-start | bytes 393216 | tf_op jit(solution)/shard_map/all_to_all | solution.py:29
  19.3 15.1 %collective-permute-start.2 = (f32[160,256]{0,1:T(8,128)S(1)}, f32[160,256]{0,1:T(8,128)S(1)}, u32[]{:S(2)}, u32[]{:S(2)}) collective-permute-start(f32[160,256]{0,1:T(8,128)S(1)} %multiply_add_fusion.1), channel_id=1, source_target_pairs={{0,32},{16,48},{32,0},{48,16},{1,33},{17,49},{33,1},{49,17},{2,34}... | collective-permute-start | bytes 491528 | tf_op jit(solution)/shard_map/ppermute | solution.py:34
  34.5 3.6 %collective-permute-start.3 = (f32[160,384]{0,1:T(8,128)S(1)}, f32[160,384]{0,1:T(8,128)S(1)}, u32[]{:S(2)}, u32[]{:S(2)}) collective-permute-start(f32[160,384]{0,1:T(8,128)S(1)} %maximum_maximum_fusion), channel_id=1, source_target_pairs={{0,1},{1,0},{2,3},{3,2},{4,5},{5,4},{6,7},{7,6},{8,9},{9,8},{10,11... | collective-permute-start | bytes 737288 | tf_op jit(solution)/shard_map/ppermute | solution.py:34
  38.3 14.4 %collective-permute-start.4 = (bf16[160,384]{0,1:T(8,128)(2,1)S(1)}, bf16[160,384]{0,1:T(8,128)(2,1)S(1)}, u32[]{:S(2)}, u32[]{:S(2)}) collective-permute-start(bf16[160,384]{0,1:T(8,128)(2,1)S(1)} %pad_maximum_fusion.1), channel_id=1, source_target_pairs={{0,2},{2,0},{4,6},{6,4},{8,10},{10,8},{12,14},{14,12},{1,3},{3,1},... | collective-permute-start | bytes 368648 | tf_op jit(solution)/shard_map/ppermute | solution.py:34
  41.3 46.1 %all-to-all-start.1 = ((bf16[8,160,384]{2,1,0:T(8,128)(2,1)}), bf16[8,160,384]{2,1,0:T(8,128)(2,1)}, u32[]{:S(2)}, u32[]{:S(2)}) async-start(bf16[8,160,384]{2,1,0:T(8,128)(2,1)} %broadcast_in_dim.66), calls=%async_computation.1 | async-start | bytes 1966080 | tf_op jit(solution)/shard_map/all_to_all | solution.py:29
  54.9 27.0 %collective-permute-start.5 = (bf16[160,384]{0,1:T(8,128)(2,1)}, bf16[160,384]{0,1:T(8,128)(2,1)}, u32[]{:S(2)}, u32[]{:S(2)}) collective-permute-start(bf16[160,384]{0,1:T(8,128)(2,1)} %pad_maximum_fusion.2), channel_id=1, source_target_pairs={{0,4},{2,6},{4,0},{6,2},{8,12},{10,14},{12,8},{14,10},{1,5},{3,7},... | collective-permute-start | bytes 368648 | tf_op jit(solution)/shard_map/ppermute | solution.py:34
  87.4 24.3 %collective-permute-start = (bf16[8,160,384]{2,1,0:T(8,128)(2,1)}, bf16[8,160,384]{2,1,0:T(8,128)(2,1)}, u32[]{:S(2)}, u32[]{:S(2)}) collective-permute-start(bf16[8,160,384]{2,1,0:T(8,128)(2,1)} %all-to-all-done.1), channel_id=1, source_target_pairs={{0,1},{1,0},{2,3},{3,2},{4,5},{5,4},{6,7},{7,6},{8,9},{9,8},{10,11... | collective-permute-start | bytes 2949128 | tf_op jit(solution)/shard_map/ppermute | solution.py:34
  90.9 15.9 %collective-permute-start.6 = (bf16[160,384]{0,1:T(8,128)(2,1)}, bf16[160,384]{0,1:T(8,128)(2,1)}, u32[]{:S(2)}, u32[]{:S(2)}) collective-permute-start(bf16[160,384]{0,1:T(8,128)(2,1)} %pad_maximum_fusion.3), channel_id=1, source_target_pairs={{0,8},{2,10},{4,12},{6,14},{8,0},{10,2},{12,4},{14,6},{1,9},{3,11}... | collective-permute-start | bytes 368648 | tf_op jit(solution)/shard_map/ppermute | solution.py:34
  114.6 4.5 %collective-permute-start.7 = (bf16[8,160,384]{2,1,0:T(8,128)(2,1)S(1)}, bf16[8,160,384]{2,1,0:T(8,128)(2,1)S(1)}, u32[]{:S(2)}, u32[]{:S(2)}) collective-permute-start(bf16[8,160,384]{2,1,0:T(8,128)(2,1)S(1)} %fusion.2), channel_id=1, source_target_pairs={{0,1},{1,0},{2,3},{3,2},{4,5},{5,4},{6,7},{7,6},{8,9},{9,8},{10,11... | collective-permute-start | bytes 2949128 | tf_op jit(solution)/shard_map/ppermute | solution.py:34
  121.3 10.5 %collective-permute-start.8 = (bf16[160,384]{0,1:T(8,128)(2,1)S(1)}, bf16[160,384]{0,1:T(8,128)(2,1)S(1)}, u32[]{:S(2)}, u32[]{:S(2)}) collective-permute-start(bf16[160,384]{0,1:T(8,128)(2,1)S(1)} %concatenate.52), channel_id=1, source_target_pairs={{0,16},{16,0},{32,48},{48,32},{1,17},{17,1},{33,49},{49,33},{2,18}... | collective-permute-start | bytes 368648 | tf_op jit(solution)/shard_map/ppermute | solution.py:34
  132.2 11.6 %collective-permute-start.9 = (bf16[160,384]{0,1:T(8,128)(2,1)S(1)}, bf16[160,384]{0,1:T(8,128)(2,1)S(1)}, u32[]{:S(2)}, u32[]{:S(2)}) collective-permute-start(bf16[160,384]{0,1:T(8,128)(2,1)S(1)} %concatenate.53), channel_id=1, source_target_pairs={{0,32},{16,48},{32,0},{48,16},{1,33},{17,49},{33,1},{49,17},{2,34}... | collective-permute-start | bytes 368648 | tf_op jit(solution)/shard_map/ppermute | solution.py:34
  144.0 3.6 %collective-permute-start.10 = (f32[160,384]{0,1:T(8,128)S(1)}, f32[160,384]{0,1:T(8,128)S(1)}, u32[]{:S(2)}, u32[]{:S(2)}) collective-permute-start(f32[160,384]{0,1:T(8,128)S(1)} %maximum_maximum_fusion.1), channel_id=1, source_target_pairs={{0,1},{1,0},{2,3},{3,2},{4,5},{5,4},{6,7},{7,6},{8,9},{9,8},{10,11... | collective-permute-start | bytes 737288 | tf_op jit(solution)/shard_map/ppermute | solution.py:34
  148.0 12.2 %collective-permute-start.11 = (bf16[160,384]{0,1:T(8,128)(2,1)S(1)}, bf16[160,384]{0,1:T(8,128)(2,1)S(1)}, u32[]{:S(2)}, u32[]{:S(2)}) collective-permute-start(bf16[160,384]{0,1:T(8,128)(2,1)S(1)} %concatenate.55), channel_id=1, source_target_pairs={{0,2},{2,0},{4,6},{6,4},{8,10},{10,8},{12,14},{14,12},{1,3},{3,1},... | collective-permute-start | bytes 368648 | tf_op jit(solution)/shard_map/ppermute | solution.py:34
  160.2 45.6 %copy-start.9 = (bf16[160,384]{1,0:T(8,128)(2,1)S(1)}, bf16[160,384]{1,0:T(8,128)(2,1)}, u32[]{:S(2)}) copy-start(bf16[160,384]{1,0:T(8,128)(2,1)} %copy-done.8) | copy-start | bytes 368644
  160.5 17.8 %collective-permute-start.12 = (bf16[160,384]{0,1:T(8,128)(2,1)S(1)}, bf16[160,384]{0,1:T(8,128)(2,1)S(1)}, u32[]{:S(2)}, u32[]{:S(2)}) collective-permute-start(bf16[160,384]{0,1:T(8,128)(2,1)S(1)} %concatenate.56), channel_id=1, source_target_pairs={{0,4},{2,6},{4,0},{6,2},{8,12},{10,14},{12,8},{14,10},{1,5},{3,7},... | collective-permute-start | bytes 368648 | tf_op jit(solution)/shard_map/ppermute | solution.py:34
  164.0 42.0 %all-to-all-start.2 = ((bf16[8,160,384]{2,1,0:T(8,128)(2,1)}), bf16[8,160,384]{2,1,0:T(8,128)(2,1)S(1)}, u32[]{:S(2)}, u32[]{:S(2)}) async-start(bf16[8,160,384]{2,1,0:T(8,128)(2,1)} %fusion.1), calls=%async_computation.2 | async-start | bytes 1966080 | tf_op jit(solution)/shard_map/all_to_all | solution.py:29
  178.7 39.5 %copy-start.17 = (s32[16,2]{0,1:T(2,128)S(1)}, s32[16,2]{0,1:T(2,128)}, u32[]{:S(2)}) copy-start(s32[16,2]{0,1:T(2,128)} %param.16) | copy-start | bytes 388
  178.7 39.5 %copy-start.18 = (f32[16,2]{0,1:T(2,128)S(1)}, f32[16,2]{0,1:T(2,128)}, u32[]{:S(2)}) copy-start(f32[16,2]{0,1:T(2,128)} %param.17) | copy-start | bytes 388
  178.7 39.6 %copy-start.19 = (s32[256]{0:T(256)S(1)}, s32[256]{0:T(256)}, u32[]{:S(2)}) copy-start(s32[256]{0:T(256)} %param.13) | copy-start | bytes 3076
  178.7 39.6 %copy-start.4 = (bf16[160,256]{0,1:T(8,128)(2,1)S(1)}, bf16[160,256]{0,1:T(8,128)(2,1)}, u32[]{:S(2)}) copy-start(bf16[160,256]{0,1:T(8,128)(2,1)} %copy-done.3) | copy-start | bytes 245764
  178.7 39.6 %copy-start.14 = (bf16[160,64]{0,1:T(8,128)(2,1)S(1)}, bf16[160,64]{0,1:T(8,128)(2,1)}, u32[]{:S(2)}) copy-start(bf16[160,64]{0,1:T(8,128)(2,1)} %copy-done.13) | copy-start | bytes 61444
  178.7 26.7 %collective-permute-start.13 = (bf16[160,384]{0,1:T(8,128)(2,1)S(1)}, bf16[160,384]{0,1:T(8,128)(2,1)S(1)}, u32[]{:S(2)}, u32[]{:S(2)}) collective-permute-start(bf16[160,384]{0,1:T(8,128)(2,1)S(1)} %concatenate.57), channel_id=1, source_target_pairs={{0,8},{2,10},{4,12},{6,14},{8,0},{10,2},{12,4},{14,6},{1,9},{3,11}... | collective-permute-start | bytes 368648 | tf_op jit(solution)/shard_map/ppermute | solution.py:34
  207.6 29.6 %all-to-all-start.3 = ((bf16[32,22,384]{2,1,0:T(8,128)(2,1)}), bf16[32,22,384]{2,1,0:T(8,128)(2,1)S(1)}, u32[]{:S(2)}, u32[]{:S(2)}) async-start(bf16[32,22,384]{2,1,0:T(8,128)(2,1)} %pad_maximum_fusion), calls=%async_computation.3 | async-start | bytes 1179648 | tf_op jit(solution)/shard_map/all_to_all | solution.py:29
  (16 other events, 162.3 us)

commit v3 on v1

--- a/solution.py
+++ b/solution.py
@@ -43,6 +43,11 @@
     blocks = chunks.shape[0] // halves
     shaped = chunks.reshape(blocks, halves, height // blocks, LANES)
     return shaped.transpose(0, 2, 1, 3).reshape(height, stride)
+
+
+def split(values):
+    high = lax.reduce_precision(values, 8, 7)
+    return high, lax.reduce_precision(values - high, 8, 7)
 
 
 def mix_blocks(chunks):
@@ -102,8 +107,6 @@
     weights = (codes.astype(F32) * jnp.repeat(scales, group_size, axis=0)).astype(BF)
 
     adapter_part = jnp.dot(rotated, lowrank_down_map, preferred_element_type=F32)
-    adapter_column = exchange(adapter_part.T.astype(BF), SLAB)
-    adapter_column = adapter_column.astype(F32).sum(axis=0)
 
     by_depth = weights.reshape(stride, depth, cores, columns)
     own = lax.dynamic_index_in_dim(by_depth, core, 2, keepdims=False).reshape(stride, depth * columns)
@@ -113,9 +116,9 @@
     part_other = jnp.dot(rotated, other, preferred_element_type=F32).astype(BF)
     part_own = jnp.dot(rotated, own, preferred_element_type=F32)
     arrived = lax.ppermute(part_other, "c", [(0, 1), (1, 0)])
-    pair = (part_own + arrived.astype(F32)).astype(BF)
+    pair = part_own + arrived.astype(F32)
     pair = pair.reshape(slot_rows, depth, columns).transpose(1, 0, 2)
-    frozen = exchange(pair, "z").astype(F32).sum(axis=0)
+    frozen = lax.psum_scatter(pair, "z", scatter_dimension=0, tiled=False)
 
     d_full = gathered[:slot_rows]
     lowrank_full = gathered[slot_rows:]
@@ -137,18 +140,26 @@
     d_local = jnp.dot(d_rotated.astype(BF), spread_local, preferred_element_type=F32)
     chunk_rows = slot_rows * stride // (peers * LANES)
     riders = jnp.concatenate(
-        [adapter_column, row_product, jnp.zeros((3 * LANES - 2 * slot_rows,), F32)]
+        [
+            adapter_part.T,
+            jnp.broadcast_to(row_product[None], (peers, slot_rows)),
+            jnp.zeros((peers, 3 * LANES - 2 * slot_rows), F32),
+        ],
+        axis=1,
     ).astype(BF)
-    riders = jnp.broadcast_to(riders.reshape(1, 3, LANES), (peers, 3, LANES))
-    d_chunks = jnp.concatenate([to_chunks((d_local * scaling).astype(BF), peers), riders], axis=1)
+    d_chunks = to_chunks((d_local * scaling).astype(BF), peers)
+    d_chunks = jnp.concatenate([d_chunks, riders.reshape(peers, 3, LANES)], axis=1)
     d_chunks = exchange(d_chunks, SLAB)
-    d_mixed = exchange(mix_blocks(d_chunks[:, :chunk_rows]), SLAB)
+    riders = d_chunks[:, chunk_rows:].astype(F32).sum(axis=0).reshape(3 * LANES)
+    row_total = riders[slot_rows : 2 * slot_rows]
+    column = jnp.pad(riders[:slot_rows], (0, 2 * LANES - slot_rows)).astype(BF)
+    column = jnp.broadcast_to(column.reshape(1, 2, LANES), (peers, 2, LANES))
+    d_mixed = jnp.concatenate([mix_blocks(d_chunks[:, :chunk_rows]), column], axis=1)
+    d_mixed = exchange(d_mixed, SLAB)
     hidden_gradient = (
-        from_chunks(d_mixed, slot_rows, stride).astype(F32) * sign_values
+        from_chunks(d_mixed[:, :chunk_rows], slot_rows, stride).astype(F32) * sign_values
     ).astype(BF)
-    riders = d_chunks[:, chunk_rows:].reshape(peers, 3 * LANES)
-    adapter_in = riders[:, :slot_rows]
-    row_total = riders[:, slot_rows : 2 * slot_rows].astype(F32).sum(axis=0)
+    adapter_in = d_mixed[:, chunk_rows:].reshape(peers, 2 * LANES)[:, :slot_rows]
 
     slot_output = frozen + (LOWRANK_SCALE / replicas) * lax.dot_general(
         adapter_in, lowrank_local, (((0,), (0,)), ((), ())), preferred_element_type=F32
@@ -156,10 +167,8 @@
     share = rank // replicas
     adapter_share = lax.dynamic_slice_in_dim(adapter_in, replica * share, share, 0)
     up_share = LOWRANK_SCALE * jnp.dot(adapter_share, d_rows, preferred_element_type=F32)
-    total_high = row_total.astype(BF)
-    total_low = (row_total - total_high.astype(F32)).astype(BF)
     totals = jnp.concatenate(
-        [total_high.reshape(devices, capacity), total_low.reshape(devices, capacity)], axis=1
+        [part.astype(BF).reshape(devices, capacity) for part in split(row_total)], axis=1
     )
     totals = jnp.pad(totals, ((0, 0), (0, columns - 2 * capacity)))[:, None, :]
     parcel = jnp.concatenate(

time: 199 us -> 168 us (0.84)
  waiting for transfers between devices: 78.5 us -> 55.5 us
  starting transfers between devices: 59.4 us -> 52.9 us
    all_to_all x8 -> x6, waiting for transfers between devices: 78.5 us -> 53 us  [exchange(): return lax.all_to_all(value, axes, split_axis=0, concat_axis=0, tiled=True)]
    all_to_all x8 -> x6, starting transfers between devices: 57.3 us -> 50.8 us  [exchange(): return lax.all_to_all(value, axes, split_axis=0, concat_axis=0, tiled=True)]
    ppermute x1, waiting for transfers between devices: 0.01 us -> 2.45 us  [body(): arrived = lax.ppermute(part_other, 'c', [(0, 1), (1, 0)])]
    reduce_sum x3 -> x1, other arithmetic: 2.39 us -> 0.08 us  [body(): riders = d_chunks[:, chunk_rows:].astype(F32).sum(axis=0).reshape(3 * LANES)]
  transfers between devices with their start and end apart: 10 -> 9, of which waited for: 8 -> 7; matrix products, arithmetic and copies ran while one was open for 18% -> 19% of each run, Pallas kernels for 0% -> 0%
where the time goes in v3:
time: 168 us; the launch traced here: 167 us
  waiting for transfers between devices  55.5 us (33%)
  starting transfers between devices  52.9 us (31%)
  local copies, waits for them, and re-layouts  18.9 us (11%)
  between operations  16.1 us (10%)
  matrix products  14.5 us (9%)
  other arithmetic  9.47 us (6%)
    all_to_all x6, waiting for transfers between devices, exchange(): return lax.all_to_all(value, axes, split_axis=0, concat_axis=0, tiled=True)  53 us
    all_to_all x6, starting transfers between devices, exchange(): return lax.all_to_all(value, axes, split_axis=0, concat_axis=0, tiled=True)  50.8 us
    dynamic_slice x1, local copies, waits for them, and re-layouts, body(): lax.dynamic_index_in_dim(by_depth, 1 - core, 2, keepdims=False)  3.95 us
    unnamed x52, local copies, waits for them, and re-layouts  3.47 us
  transfers between devices with their start and end apart: 9, of which 7 were waited for; matrix products, arithmetic and copies ran while one was open for 19% of the time, Pallas kernels for 0%

profile of v3, /device:TPU:8, one launch (start us, length us, event | category | flops | bytes accessed | tf_op | source)
XLA Modules:
  0.0 167.5 jit_solution(1374318995701246514)
XLA Ops:
  12.4 10.2 %all-to-all-start.2 = ((bf16[32,5,384]{2,1,0:T(8,128)(2,1)}), bf16[32,5,384]{2,1,0:T(8,128)(2,1)S(1)}, u32[]{:S(2)}, u32[]{:S(2)}) async-start(bf16[32,5,384]{2,1,0:T(8,128)(2,1)} %all_to_all.25), calls=%async_computation.3 | async-start | bytes 393216 | tf_op jit(solution)/shard_map/all_to_all | solution.py:30
  22.6 10.9 %all-to-all-done.2 = bf16[32,5,384]{2,1,0:T(8,128)(2,1)S(1)} async-done(((bf16[32,5,384]{2,1,0:T(8,128)(2,1)}), bf16[32,5,384]{2,1,0:T(8,128)(2,1)S(1)}, u32[]{:S(2)}, u32[]{:S(2)}) %all-to-all-start.2) | async-done | bytes 122912 | tf_op jit(solution)/shard_map/all_to_all | solution.py:30
  35.2 12.8 %all-to-all-start = ((bf16[64,5,128]{2,1,0:T(8,128)(2,1)}), bf16[64,5,128]{2,1,0:T(8,128)(2,1)}, u32[]{:S(2)}, u32[]{:S(2)}) async-start(bf16[64,5,128]{2,1,0:T(8,128)(2,1)} %copy.123), calls=%async_computation | async-start | bytes 262144 | tf_op jit(solution)/shard_map/all_to_all | solution.py:30
  48.0 2.6 %fusion = bf16[256,6144]{1,0:T(8,128)(2,1)S(1)} fusion(bf16[256,6144]{1,0:T(8,128)(2,1)} %param.13, f32[4,6144]{1,0:T(4,128)} %param.14), kind=kLoop, calls=%fused_computation.1 | loop fusion | flops 4718592 | bytes 6389760 | tf_op jit(solution)/shard_map/convert_element_type | solution.py:107
  50.6 2.8 %copy.125 = bf16[256,6144]{0,1:T(8,128)(2,1)} copy(bf16[256,6144]{1,0:T(8,128)(2,1)S(1)} %fusion) | data formatting | bytes 6291456 | tf_op jit(solution)/shard_map/convert_element_type | solution.py:107
  53.4 4.0 %all-to-all-done = bf16[64,5,128]{2,1,0:T(8,128)(2,1)} async-done(((bf16[64,5,128]{2,1,0:T(8,128)(2,1)}), bf16[64,5,128]{2,1,0:T(8,128)(2,1)}, u32[]{:S(2)}, u32[]{:S(2)}) %all-to-all-start) | async-done | bytes 81952 | tf_op jit(solution)/shard_map/all_to_all | solution.py:30
  57.4 1.7 %fusion.10 = bf16[64,640]{1,0:T(8,128)(2,1)} fusion(bf16[64,64]{1,0:T(8,128)(2,1)} %constant.89.clone, bf16[8,8,5,128]{3,2,1,0:T(8,128)(2,1)} %bitcast.34), kind=kOutput, calls=%fused_computation.18 | convolution fusion | flops 5283840 | bytes 172032 | tf_op jit(solution)/shard_map/dot_general | solution.py:55
  59.1 1.6 reshape.172
  60.8 6.9 %all-to-all-start.1 = ((bf16[64,5,128]{2,1,0:T(8,128)(2,1)}), bf16[64,5,128]{2,1,0:T(8,128)(2,1)}, u32[]{:S(2)}, u32[]{:S(2)}) async-start(bf16[64,5,128]{2,1,0:T(8,128)(2,1)} %reshape.172), calls=%async_computation.1 | async-start | bytes 262144 | tf_op jit(solution)/shard_map/all_to_all | solution.py:30
  67.8 3.9 %constant_dynamic-slice_fusion = (bf16[256,8,1,384]{0,3,2,1:T(8,128)(2,1)}, bf16[256,8,1,384]{0,3,2,1:T(8,128)(2,1)}) fusion(bf16[256,8,2,384]{0,3,2,1:T(8,128)(2,1)} %bitcast.105, s32[]{:T(128)S(6)} %select_n.44, s32[]{:T(128)S(6)} %select_n.43), kind=kLoop, calls=%fused_computation.89 | loop fusion | bytes 6291464 | tf_op jit(solution)/shard_map/jit(dynamic_index_in_dim)/dynamic_slice | solution.py:113
  71.7 5.4 %all-to-all-done.1 = bf16[64,5,128]{2,1,0:T(8,128)(2,1)} async-done(((bf16[64,5,128]{2,1,0:T(8,128)(2,1)}), bf16[64,5,128]{2,1,0:T(8,128)(2,1)}, u32[]{:S(2)}, u32[]{:S(2)}) %all-to-all-start.1) | async-done | bytes 81952 | tf_op jit(solution)/shard_map/all_to_all | solution.py:30
  79.4 2.1 %convolution_convert_fusion = bf16[160,3072]{1,0:T(8,128)(2,1)S(1)} fusion(bf16[160,256]{1,0:T(8,128)(2,1)S(1)} %fusion.8, bf16[256,3072]{0,1:T(8,128)(2,1)} %bitcast.108), kind=kOutput, calls=%fused_computation.2 | convolution fusion | flops 252149760 | bytes 2637824 | tf_op jit(solution)/shard_map/dot_general | solution.py:116
  81.5 2.0 %collective-permute-start = (bf16[160,3072]{1,0:T(8,128)(2,1)S(1)}, bf16[160,3072]{1,0:T(8,128)(2,1)S(1)}, u32[]{:S(2)}, u32[]{:S(2)}) collective-permute-start(bf16[160,3072]{1,0:T(8,128)(2,1)S(1)} %convolution_convert_fusion), channel_id=1, source_target_pairs={{0,1},{1,0},{2,3},{3,2},{4,5},{5,4},{6,7},{7,6},{8,9},{9,8},{10,11... | collective-permute-start | bytes 2949128 | tf_op jit(solution)/shard_map/ppermute | solution.py:118
  83.5 2.5 %collective-permute-done = bf16[160,3072]{1,0:T(8,128)(2,1)S(1)} collective-permute-done((bf16[160,3072]{1,0:T(8,128)(2,1)S(1)}, bf16[160,3072]{1,0:T(8,128)(2,1)S(1)}, u32[]{:S(2)}, u32[]{:S(2)}) %collective-permute-start) | collective-permute-done | bytes 983072 | tf_op jit(solution)/shard_map/ppermute | solution.py:118
  86.6 1.4 copy.166
  88.2 1.7 fusion.18
  89.9 2.6 %fusion.15 = bf16[160,64]{0,1:T(8,128)(2,1)S(1)} fusion(bf16[224,6144]{1,0:T(8,128)(2,1)} %all-gather.2.cloned.1.call-done), kind=kOutput, calls=%fused_computation.21 | convolution fusion | flops 125849600 | bytes 2772992 | tf_op jit(solution)/shard_map/dot_general | solution.py:125
  93.4 1.3 multiply_reduce_fusion
  96.6 5.6 %all-to-all-start.3 = ((bf16[64,8,128]{2,1,0:T(8,128)(2,1)}), bf16[64,8,128]{2,1,0:T(8,128)(2,1)S(1)}, u32[]{:S(2)}, u32[]{:S(2)}) async-start(bf16[64,8,128]{2,1,0:T(8,128)(2,1)} %copy.130), calls=%async_computation.4 | async-start | bytes 262144 | tf_op jit(solution)/shard_map/all_to_all | solution.py:30
  102.2 9.5 %all-to-all-done.3 = bf16[64,8,128]{2,1,0:T(8,128)(2,1)S(1)} async-done(((bf16[64,8,128]{2,1,0:T(8,128)(2,1)}), bf16[64,8,128]{2,1,0:T(8,128)(2,1)S(1)}, u32[]{:S(2)}, u32[]{:S(2)}) %all-to-all-start.3) | async-done | bytes 131104 | tf_op jit(solution)/shard_map/all_to_all | solution.py:30
  113.7 5.7 %all-to-all-start.4 = ((bf16[64,7,128]{2,1,0:T(8,128)(2,1)}), bf16[64,7,128]{2,1,0:T(8,128)(2,1)S(1)}, u32[]{:S(2)}, u32[]{:S(2)}) async-start(bf16[64,7,128]{2,1,0:T(8,128)(2,1)} %pad_maximum_fusion.3), calls=%async_computation.5 | async-start | bytes 262144 | tf_op jit(solution)/shard_map/all_to_all | solution.py:30
  119.6 9.4 %all-to-all-done.4 = bf16[64,7,128]{2,1,0:T(8,128)(2,1)S(1)} async-done(((bf16[64,7,128]{2,1,0:T(8,128)(2,1)}), bf16[64,7,128]{2,1,0:T(8,128)(2,1)S(1)}, u32[]{:S(2)}, u32[]{:S(2)}) %all-to-all-start.4) | async-done | bytes 114720 | tf_op jit(solution)/shard_map/all_to_all | solution.py:30
  131.8 9.6 %all-to-all-start.5 = ((bf16[32,22,384]{2,1,0:T(8,128)(2,1)}), bf16[32,22,384]{2,1,0:T(8,128)(2,1)S(1)}, u32[]{:S(2)}, u32[]{:S(2)}) async-start(bf16[32,22,384]{2,1,0:T(8,128)(2,1)} %pad_maximum_fusion), calls=%async_computation.6 | async-start | bytes 1179648 | tf_op jit(solution)/shard_map/all_to_all | solution.py:30
  143.2 13.8 %all-to-all-done.5 = bf16[32,22,384]{2,1,0:T(8,128)(2,1)S(1)} async-done(((bf16[32,22,384]{2,1,0:T(8,128)(2,1)}), bf16[32,22,384]{2,1,0:T(8,128)(2,1)S(1)}, u32[]{:S(2)}, u32[]{:S(2)}) %all-to-all-start.5) | async-done | bytes 540704 | tf_op jit(solution)/shard_map/all_to_all | solution.py:30
  (127 shorter events, 21.2 us)
Async XLA Ops:
  8.0 14.6 %copy-start = (bf16[8,64,384]{2,1,0:T(8,128)(2,1)S(1)}, bf16[8,64,384]{2,1,0:T(8,128)(2,1)}, u32[]{:S(2)}) copy-start(bf16[8,64,384]{2,1,0:T(8,128)(2,1)} %param.17) | copy-start | bytes 1179652
  8.0 26.3 %copy-start.18 = (s32[256]{0:T(256)S(1)}, s32[256]{0:T(256)}, u32[]{:S(2)}) copy-start(s32[256]{0:T(256)} %param.15) | copy-start | bytes 3076
  8.0 26.3 %copy-start.13 = (bf16[160,256]{1,0:T(8,128)(2,1)S(1)}, bf16[160,256]{1,0:T(8,128)(2,1)}, u32[]{:S(2)}) copy-start(bf16[160,256]{1,0:T(8,128)(2,1)} %param.12) | copy-start | bytes 245764
  12.4 21.2 %all-to-all-start.2 = ((bf16[32,5,384]{2,1,0:T(8,128)(2,1)}), bf16[32,5,384]{2,1,0:T(8,128)(2,1)S(1)}, u32[]{:S(2)}, u32[]{:S(2)}) async-start(bf16[32,5,384]{2,1,0:T(8,128)(2,1)} %all_to_all.25), calls=%async_computation.3 | async-start | bytes 393216 | tf_op jit(solution)/shard_map/all_to_all | solution.py:30
  22.6 67.3 %all-gather.2.cloned.1.call-start = ((), (), s32[]{:S(2)}) async-start(), calls=%async_computation.8 | async-start | bytes 2924544 | tf_op jit(solution)/shard_map/all_gather | solution.py:97
  22.6 25.4 %copy-start.8 = (bf16[64,384]{1,0:T(8,128)(2,1)}, bf16[64,384]{1,0:T(8,128)(2,1)S(1)}, u32[]{:S(2)}) copy-start(bf16[64,384]{1,0:T(8,128)(2,1)S(1)} %dynamic-slice_bitcast_fusion) | copy-start | bytes 147460
  33.6 14.4 %copy-start.5 = (bf16[160,384]{1,0:T(8,128)(2,1)}, bf16[160,384]{1,0:T(8,128)(2,1)S(1)}, u32[]{:S(2)}) copy-start(bf16[160,384]{1,0:T(8,128)(2,1)S(1)} %all_to_all.27) | copy-start | bytes 368644
  35.2 22.2 %all-to-all-start = ((bf16[64,5,128]{2,1,0:T(8,128)(2,1)}), bf16[64,5,128]{2,1,0:T(8,128)(2,1)}, u32[]{:S(2)}, u32[]{:S(2)}) async-start(bf16[64,5,128]{2,1,0:T(8,128)(2,1)} %copy.123), calls=%async_computation | async-start | bytes 262144 | tf_op jit(solution)/shard_map/all_to_all | solution.py:30
  60.8 16.4 %all-to-all-start.1 = ((bf16[64,5,128]{2,1,0:T(8,128)(2,1)}), bf16[64,5,128]{2,1,0:T(8,128)(2,1)}, u32[]{:S(2)}, u32[]{:S(2)}) async-start(bf16[64,5,128]{2,1,0:T(8,128)(2,1)} %reshape.172), calls=%async_computation.1 | async-start | bytes 262144 | tf_op jit(solution)/shard_map/all_to_all | solution.py:30
  67.7 61.6 %reduce-scatter.2.cloned.1.call-start = ((), (), s32[]{:S(2)}) async-start(), calls=%async_computation.7 | async-start | bytes 2211840 | tf_op jit(solution)/shard_map/reduce_scatter | solution.py:121
  77.2 8.8 %copy-start.1 = (bf16[256,8,1,384]{0,3,2,1:T(8,128)(2,1)S(1)}, bf16[256,8,1,384]{0,3,2,1:T(8,128)(2,1)}, u32[]{:S(2)}) copy-start(bf16[256,8,1,384]{0,3,2,1:T(8,128)(2,1)} %get-tuple-element.41) | copy-start | bytes 4718596
  81.5 4.5 %collective-permute-start = (bf16[160,3072]{1,0:T(8,128)(2,1)S(1)}, bf16[160,3072]{1,0:T(8,128)(2,1)S(1)}, u32[]{:S(2)}, u32[]{:S(2)}) collective-permute-start(bf16[160,3072]{1,0:T(8,128)(2,1)S(1)} %convolution_convert_fusion), channel_id=1, source_target_pairs={{0,1},{1,0},{2,3},{3,2},{4,5},{5,4},{6,7},{7,6},{8,9},{9,8},{10,11... | collective-permute-start | bytes 2949128 | tf_op jit(solution)/shard_map/ppermute | solution.py:118
  94.7 18.3 %copy-start.22 = (pred[2,128]{1,0:T(4,128)(4,1)S(1)}, pred[2,128]{1,0:T(4,128)(4,1)}, u32[]{:S(2)}) copy-start(pred[2,128]{1,0:T(4,128)(4,1)} %constant.83.clone.1) | copy-start | bytes 772
  94.7 34.4 %copy-start.9 = (bf16[64,384]{1,0:T(8,128)(2,1)S(1)}, bf16[64,384]{1,0:T(8,128)(2,1)}, u32[]{:S(2)}) copy-start(bf16[64,384]{1,0:T(8,128)(2,1)} %copy-done.8) | copy-start | bytes 147460
  94.9 35.5 %copy-start.6 = (bf16[160,384]{1,0:T(8,128)(2,1)S(1)}, bf16[160,384]{1,0:T(8,128)(2,1)}, u32[]{:S(2)}) copy-start(bf16[160,384]{1,0:T(8,128)(2,1)} %copy-done.5) | copy-start | bytes 368644
  96.6 15.1 %all-to-all-start.3 = ((bf16[64,8,128]{2,1,0:T(8,128)(2,1)}), bf16[64,8,128]{2,1,0:T(8,128)(2,1)S(1)}, u32[]{:S(2)}, u32[]{:S(2)}) async-start(bf16[64,8,128]{2,1,0:T(8,128)(2,1)} %copy.130), calls=%async_computation.4 | async-start | bytes 262144 | tf_op jit(solution)/shard_map/all_to_all | solution.py:30
  113.7 15.3 %all-to-all-start.4 = ((bf16[64,7,128]{2,1,0:T(8,128)(2,1)}), bf16[64,7,128]{2,1,0:T(8,128)(2,1)S(1)}, u32[]{:S(2)}, u32[]{:S(2)}) async-start(bf16[64,7,128]{2,1,0:T(8,128)(2,1)} %pad_maximum_fusion.3), calls=%async_computation.5 | async-start | bytes 262144 | tf_op jit(solution)/shard_map/all_to_all | solution.py:30
  129.3 12.1 %copy-start.17 = (s32[32]{0:T(128)S(1)}, s32[32]{0:T(128)}, u32[]{:S(2)}) copy-start(s32[32]{0:T(128)} %copy-done.16) | copy-start | bytes 388
  129.3 12.3 %copy-start.14 = (s32[16,2]{0,1:T(2,128)S(1)}, s32[16,2]{0,1:T(2,128)}, u32[]{:S(2)}) copy-start(s32[16,2]{0,1:T(2,128)} %param.18) | copy-start | bytes 388
  129.3 12.3 %copy-start.15 = (f32[16,2]{0,1:T(2,128)S(1)}, f32[16,2]{0,1:T(2,128)}, u32[]{:S(2)}) copy-start(f32[16,2]{0,1:T(2,128)} %param.19) | copy-start | bytes 388
  129.3 12.3 %copy-start.4 = (bf16[160,256]{1,0:T(8,128)(2,1)S(1)}, bf16[160,256]{1,0:T(8,128)(2,1)}, u32[]{:S(2)}) copy-start(bf16[160,256]{1,0:T(8,128)(2,1)} %copy-done.2) | copy-start | bytes 245764
  129.3 12.3 %copy-start.12 = (bf16[160,64]{0,1:T(8,128)(2,1)S(1)}, bf16[160,64]{0,1:T(8,128)(2,1)}, u32[]{:S(2)}) copy-start(bf16[160,64]{0,1:T(8,128)(2,1)} %copy-done.11) | copy-start | bytes 61444
  130.6 26.5 %copy-start.20 = (s32[32]{0:T(128)S(1)}, s32[32]{0:T(128)}, u32[]{:S(2)}) copy-start(s32[32]{0:T(128)} %copy-done.19) | copy-start | bytes 388
  131.8 25.2 %all-to-all-start.5 = ((bf16[32,22,384]{2,1,0:T(8,128)(2,1)}), bf16[32,22,384]{2,1,0:T(8,128)(2,1)S(1)}, u32[]{:S(2)}, u32[]{:S(2)}) async-start(bf16[32,22,384]{2,1,0:T(8,128)(2,1)} %pad_maximum_fusion), calls=%async_computation.6 | async-start | bytes 1179648 | tf_op jit(solution)/shard_map/all_to_all | solution.py:30
  (8 other events, 21.8 us)
Sparse Core Ops, SparseCore 0:
  34.5 46.0 all-gather.1
Sparse Core Ops, SparseCore 1:
  88.2 40.8 reduce-scatter.1

commit v4 on v3

--- a/solution.py
+++ b/solution.py
@@ -4,6 +4,8 @@
 import jax.numpy as jnp
 import numpy as np
 from jax import lax
+from jax.experimental import pallas as pl
+from jax.experimental.pallas import tpu as pltpu
 from jax.sharding import Mesh
 from jax.sharding import PartitionSpec as P
 
@@ -17,6 +19,8 @@
 TENSOR = ("z", "c")
 SLAB = ("r", "z", "c")
 LANES = 128
+TILE = 8
+ROWS = 5
 
 
 def sylvester(count):
@@ -30,32 +34,154 @@
     return lax.all_to_all(value, axes, split_axis=0, concat_axis=0, tiled=True)
 
 
-def to_chunks(values, peers):
+def dot(left, right, dims=((1,), (0,))):
+    return lax.dot_general(left, right, (dims, ((), ())), preferred_element_type=F32)
+
+
+def placement(blocks, rows):
+    out_row = lax.broadcasted_iota(jnp.int32, (blocks * TILE, blocks * rows), 0)
+    in_row = lax.broadcasted_iota(jnp.int32, (blocks * TILE, blocks * rows), 1)
+    k = out_row % TILE
+    return jnp.where((k < rows) & (out_row // TILE * rows + k == in_row), 1.0, 0.0).astype(BF)
+
+
+def rider_rows(peers, k):
+    out_row = lax.broadcasted_iota(jnp.int32, (peers * TILE, peers), 0)
+    in_row = lax.broadcasted_iota(jnp.int32, (peers * TILE, peers), 1)
+    return jnp.where(out_row == in_row * TILE + k, 1.0, 0.0).astype(BF)
+
+
+def whole(kernel, out_shape, *operands):
+    return pl.pallas_call(
+        kernel,
+        out_shape=out_shape,
+        compiler_params=pltpu.CompilerParams(vmem_limit_bytes=32 * 1024 * 1024),
+    )(*operands)
+
+
+def to_chunks(values, signs):
     height, stride = values.shape
     halves = stride // LANES
-    blocks = peers // halves
-    shaped = values.reshape(blocks, height // blocks, halves, LANES)
-    return shaped.transpose(0, 2, 1, 3).reshape(peers, height // blocks, LANES)
-
-
-def from_chunks(chunks, height, stride):
+    blocks = height // ROWS
+
+    def kernel(values_ref, signs_ref, out_ref):
+        sign = (2 * signs_ref[...] - 1).astype(F32)
+        signed = (values_ref[...].astype(F32) * sign).astype(BF)
+        place = placement(blocks, ROWS)
+        for half in range(halves):
+            part = dot(place, signed[:, half * LANES : (half + 1) * LANES])
+            part = part.astype(BF).reshape(blocks, TILE, LANES)
+            out_ref[half * blocks : (half + 1) * blocks] = part
+
+    out = jax.ShapeDtypeStruct((halves * blocks, TILE, LANES), BF)
+    return whole(kernel, out, values, signs.reshape(1, stride))
+
+
+def hadamard(parts):
+    step = 1
+    while step < len(parts):
+        for low in range(len(parts)):
+            if low & step == 0:
+                one, two = parts[low], parts[low + step]
+                parts[low], parts[low + step] = one + two, one - two
+        step *= 2
+    return parts
+
+
+def mix_blocks(chunks):
+    def kernel(chunks_ref, out_ref, sum_ref):
+        values = chunks_ref[...].astype(F32)
+        mixed = hadamard([values[p] for p in range(values.shape[0])])
+        row = lax.broadcasted_iota(jnp.int32, (TILE, LANES), 0)
+        sum_ref[...] = mixed[0]
+        for p, part in enumerate(mixed):
+            out_ref[p] = jnp.where(row < ROWS, part, mixed[0]).astype(BF)
+
+    out = jax.ShapeDtypeStruct(chunks.shape, BF), jax.ShapeDtypeStruct((TILE, LANES), F32)
+    return whole(kernel, out, chunks)
+
+
+def gather_rows(chunks, blocks):
+    flat = chunks.reshape(-1, LANES)
+    place = placement(blocks, ROWS)
+    size = blocks * TILE
+    halves = flat.shape[0] // size
+    parts = [
+        dot(place, flat[half * size : (half + 1) * size], ((0,), (0,))) for half in range(halves)
+    ]
+    return jnp.concatenate(parts, axis=1)
+
+
+def finish_rotation(chunks, spread, scaling):
+    blocks = chunks.shape[0] * LANES // spread.shape[0]
+
+    def kernel(chunks_ref, spread_ref, out_ref):
+        values = gather_rows(chunks_ref[...], blocks).astype(BF)
+        out_ref[...] = (dot(values, spread_ref[...]) * scaling).astype(BF)
+
+    out = jax.ShapeDtypeStruct((blocks * ROWS, spread.shape[0]), BF)
+    return whole(kernel, out, chunks, spread)
+
+
+def finish_gradient(chunks, signs):
+    stride = signs.shape[0]
+    blocks = chunks.shape[0] * LANES // stride
+
+    def kernel(chunks_ref, signs_ref, out_ref):
+        sign = (2 * signs_ref[...] - 1).astype(F32)
+        out_ref[...] = (gather_rows(chunks_ref[...], blocks) * sign).astype(BF)
+
+    out = jax.ShapeDtypeStruct((blocks * ROWS, stride), BF)
+    return whole(kernel, out, chunks, signs.reshape(1, stride))
+
+
+def backward_chunks(main, adapter_grad, down_map, rotated, spread, scaling):
+    height, stride = main.shape
     halves = stride // LANES
-    blocks = chunks.shape[0] // halves
-    shaped = chunks.reshape(blocks, halves, height // blocks, LANES)
-    return shaped.transpose(0, 2, 1, 3).reshape(height, stride)
+    blocks = height // ROWS
+    peers = halves * blocks
+    rest = height - LANES
+
+    def kernel(main_ref, grad_ref, down_ref, rotated_ref, spread_ref, out_ref):
+        rotated_value = rotated_ref[...]
+        down = down_ref[...]
+        d_rotated = main_ref[...] + dot(grad_ref[...], down, ((1,), (1,)))
+        local = dot(d_rotated.astype(BF), spread_ref[...])
+        local = (local * scaling).astype(BF)
+        product = rotated_value.astype(F32) * d_rotated
+        totals = lax.dot_general(
+            jnp.ones((TILE, stride), F32),
+            product,
+            (((1,), (1,)), ((), ())),
+            precision=HIGH_ACCURACY,
+            preferred_element_type=F32,
+        )
+        adapter = dot(down, rotated_value, ((0,), (1,))).astype(BF)
+        pad = jnp.zeros((peers, LANES - rest), BF)
+        riders = dot(rider_rows(peers, ROWS), adapter[:, :LANES])
+        tail = jnp.concatenate([adapter[:, LANES:], pad], axis=1)
+        riders += dot(rider_rows(peers, ROWS + 1), tail)
+        row_tail = jnp.concatenate(
+            [totals[:, LANES:], jnp.zeros((TILE, LANES - rest), F32)], axis=1
+        )
+        row_tail = pltpu.roll(row_tail, rest, 1)
+        k = lax.broadcasted_iota(jnp.int32, (TILE, LANES), 0)
+        extra = jnp.where(k == ROWS + 2, totals[:, :LANES], 0.0)
+        extra += jnp.where(k == ROWS + 1, row_tail, 0.0)
+        place = placement(blocks, ROWS)
+        for half in range(halves):
+            part = dot(place, local[:, half * LANES : (half + 1) * LANES])
+            part += riders[half * blocks * TILE : (half + 1) * blocks * TILE]
+            part = part.reshape(blocks, TILE, LANES) + extra[None]
+            out_ref[half * blocks : (half + 1) * blocks] = part.astype(BF)
+
+    out = jax.ShapeDtypeStruct((peers, TILE, LANES), BF)
+    return whole(kernel, out, main, adapter_grad, down_map, rotated, spread)
 
 
 def split(values):
     high = lax.reduce_precision(values, 8, 7)
     return high, lax.reduce_precision(values - high, 8, 7)
-
-
-def mix_blocks(chunks):
-    peers, rows, lanes = chunks.shape
-    mixed = jnp.dot(
-        sylvester(peers), chunks.reshape(peers, rows * lanes), preferred_element_type=F32
-    )
-    return mixed.astype(BF).reshape(peers, rows, lanes)
 
 
 def body(
@@ -64,7 +190,6 @@
     slot_rows, stride = hidden.shape
     replicas, depth, cores = lax.axis_size("r"), lax.axis_size("z"), lax.axis_size("c")
     devices = EXPERT_COUNT * replicas
-    peers = replicas * depth * cores
     rank = lowrank_down_map.shape[1]
     expert_position = lax.axis_index("e")
     replica = lax.axis_index("r")
@@ -73,7 +198,6 @@
     tokens_here = experts.shape[0]
     columns = output_gradient.shape[1]
     scaling = 1.0 / math.sqrt(HIDDEN_UNITS)
-    sign_values = (2 * signs - 1).astype(F32)
     group_size = codes.shape[0] // scales.shape[0]
 
     flat_ids = experts.reshape(tokens_here * 2)
@@ -98,26 +222,18 @@
         jnp.concatenate([d_rows, lowrank_local], axis=0), TENSOR, axis=1, tiled=True
     )
 
-    signed = (hidden.astype(F32) * sign_values).astype(BF)
-    mixed_blocks = mix_blocks(exchange(to_chunks(signed, peers), SLAB))
-    unrotated = from_chunks(exchange(mixed_blocks, SLAB), slot_rows, stride)
     spread_local = sylvester(stride)
-    rotated = (jnp.dot(unrotated, spread_local, preferred_element_type=F32) * scaling).astype(BF)
+    mixed_blocks, _ = mix_blocks(exchange(to_chunks(hidden, signs), SLAB))
+    rotated = finish_rotation(exchange(mixed_blocks, SLAB), spread_local, scaling)
 
     weights = (codes.astype(F32) * jnp.repeat(scales, group_size, axis=0)).astype(BF)
-
-    adapter_part = jnp.dot(rotated, lowrank_down_map, preferred_element_type=F32)
-
     by_depth = weights.reshape(stride, depth, cores, columns)
-    own = lax.dynamic_index_in_dim(by_depth, core, 2, keepdims=False).reshape(stride, depth * columns)
-    other = lax.dynamic_index_in_dim(by_depth, 1 - core, 2, keepdims=False).reshape(
-        stride, depth * columns
-    )
-    part_other = jnp.dot(rotated, other, preferred_element_type=F32).astype(BF)
-    part_own = jnp.dot(rotated, own, preferred_element_type=F32)
-    arrived = lax.ppermute(part_other, "c", [(0, 1), (1, 0)])
-    pair = part_own + arrived.astype(F32)
-    pair = pair.reshape(slot_rows, depth, columns).transpose(1, 0, 2)
+    own = lax.dynamic_index_in_dim(by_depth, core, 2, keepdims=False)
+    other = lax.dynamic_index_in_dim(by_depth, 1 - core, 2, keepdims=False)
+    other = lax.ppermute(other, "c", [(0, 1), (1, 0)])
+    neighbour = lax.ppermute(rotated, "c", [(0, 1), (1, 0)])
+    pair = jnp.einsum("sk,kzf->zsf", rotated, own, preferred_element_type=F32)
+    pair = pair + jnp.einsum("sk,kzf->zsf", neighbour, other, preferred_element_type=F32)
     frozen = lax.psum_scatter(pair, "z", scatter_dimension=0, tiled=False)
 
     d_full = gathered[:slot_rows]
@@ -125,41 +241,18 @@
     adapter_grad = LOWRANK_SCALE * lax.dot_general(
         d_full, lowrank_full, (((1,), (1,)), ((), ())), preferred_element_type=F32
     )
-    d_rotated = lax.dot_general(
-        d_full, weights, (((1,), (1,)), ((), ())), preferred_element_type=F32
-    ) + lax.dot_general(
-        adapter_grad.astype(BF),
-        lowrank_down_map,
-        (((1,), (1,)), ((), ())),
-        preferred_element_type=F32,
-    )
-    row_product = jnp.sum(rotated.astype(F32) * d_rotated, axis=1)
-    down_map_gradient = lax.dot_general(
-        rotated, adapter_grad.astype(BF), (((0,), (0,)), ((), ())), preferred_element_type=F32
-    )
-    d_local = jnp.dot(d_rotated.astype(BF), spread_local, preferred_element_type=F32)
-    chunk_rows = slot_rows * stride // (peers * LANES)
-    riders = jnp.concatenate(
-        [
-            adapter_part.T,
-            jnp.broadcast_to(row_product[None], (peers, slot_rows)),
-            jnp.zeros((peers, 3 * LANES - 2 * slot_rows), F32),
-        ],
-        axis=1,
-    ).astype(BF)
-    d_chunks = to_chunks((d_local * scaling).astype(BF), peers)
-    d_chunks = jnp.concatenate([d_chunks, riders.reshape(peers, 3, LANES)], axis=1)
-    d_chunks = exchange(d_chunks, SLAB)
-    riders = d_chunks[:, chunk_rows:].astype(F32).sum(axis=0).reshape(3 * LANES)
-    row_total = riders[slot_rows : 2 * slot_rows]
-    column = jnp.pad(riders[:slot_rows], (0, 2 * LANES - slot_rows)).astype(BF)
-    column = jnp.broadcast_to(column.reshape(1, 2, LANES), (peers, 2, LANES))
-    d_mixed = jnp.concatenate([mix_blocks(d_chunks[:, :chunk_rows]), column], axis=1)
+    adapter_grad = adapter_grad.astype(BF)
+    main = dot(d_full, weights, ((1,), (1,)))
+    down_map_gradient = dot(rotated, adapter_grad, ((0,), (0,)))
+    d_chunks = exchange(
+        backward_chunks(main, adapter_grad, lowrank_down_map, rotated, spread_local, scaling), SLAB
+    )
+    d_mixed, sums = mix_blocks(d_chunks)
+    rest = slot_rows - LANES
+    row_total = jnp.concatenate([sums[ROWS + 2], sums[ROWS + 1, rest : 2 * rest]])
     d_mixed = exchange(d_mixed, SLAB)
-    hidden_gradient = (
-        from_chunks(d_mixed[:, :chunk_rows], slot_rows, stride).astype(F32) * sign_values
-    ).astype(BF)
-    adapter_in = d_mixed[:, chunk_rows:].reshape(peers, 2 * LANES)[:, :slot_rows]
+    hidden_gradient = finish_gradient(d_mixed, signs)
+    adapter_in = jnp.concatenate([d_mixed[:, ROWS], d_mixed[:, ROWS + 1, :rest]], axis=1)
 
     slot_output = frozen + (LOWRANK_SCALE / replicas) * lax.dot_general(
         adapter_in, lowrank_local, (((0,), (0,)), ((), ())), preferred_element_type=F32

time: 168 us -> 180 us (1.071)
  blocking collectives: 0 us -> 36.8 us
  starting transfers between devices: 52.9 us -> 35.6 us
  waiting for transfers between devices: 55.5 us -> 46.6 us
  matrix products: 14.5 us -> 9.93 us
  Pallas kernels: 0 us -> 4.21 us
  local copies, waits for them, and re-layouts: 18.9 us -> 20.9 us
    all_to_all x0 -> x2, blocking collectives: none -> 36.8 us  [exchange(): return lax.all_to_all(value, axes, split_axis=0, concat_axis=0, tiled=True)]
    all_to_all x6 -> x4, starting transfers between devices: 50.8 us -> 31.5 us  [exchange(): return lax.all_to_all(value, axes, split_axis=0, concat_axis=0, tiled=True)]
    all_to_all x6 -> x4, waiting for transfers between devices: 53 us -> 42.9 us  [exchange(): return lax.all_to_all(value, axes, split_axis=0, concat_axis=0, tiled=True)]
    dot_general x10 -> x4, matrix products: 10.5 us -> 6.05 us  [the longest x2 3.58 us: dot(): lax.dot_general(left, right, (dims, ((), ())), preferred_element_type=F32)]
    pallas_call x0 -> x6, Pallas kernels: none -> 4.21 us  [whole(): pl.pallas_call(kernel, out_shape=out_shape, compiler_params=pltpu.Compile...]
    dynamic_slice x1, local copies, waits for them, and re-layouts: 3.95 us -> 8.15 us  [body(): other = lax.dynamic_index_in_dim(by_depth, 1 - core, 2, keepdims=False)]
    reduce_scatter x1, waiting for transfers between devices: 0.03 us -> 3.22 us  [body(): frozen = lax.psum_scatter(pair, 'z', scatter_dimension=0, tiled=False)]
    convert_element_type x2 -> x0, local copies, waits for them, and re-layouts: 2.89 us -> none  [the longest x1 2.81 us: body(): (codes.astype(F32) * jnp.repeat(scales, group_size, axis=0)).astype(BF)]
  transfers between devices with their start and end apart: 9 -> 8, of which waited for: 7 -> 6; matrix products, arithmetic and copies ran while one was open for 19% -> 17% of each run, Pallas kernels for 0% -> 2%
where the time goes in v4:
time: 180 us; the launch traced here: 179 us
  waiting for transfers between devices  46.6 us (26%)
  blocking collectives  36.8 us (20%)
  starting transfers between devices  35.6 us (20%)
  local copies, waits for them, and re-layouts  20.9 us (12%)
  between operations  15.9 us (9%)
  matrix products  9.93 us (6%)
  other arithmetic  8.83 us (5%)
  Pallas kernels  4.21 us (2%)
    all_to_all x4, waiting for transfers between devices, exchange(): return lax.all_to_all(value, axes, split_axis=0, concat_axis=0, tiled=True)  42.9 us
    all_to_all x2, blocking collectives, exchange(): return lax.all_to_all(value, axes, split_axis=0, concat_axis=0, tiled=True)  36.8 us
    all_to_all x4, starting transfers between devices, exchange(): return lax.all_to_all(value, axes, split_axis=0, concat_axis=0, tiled=True)  31.5 us
    dynamic_slice x1, local copies, waits for them, and re-layouts, body(): other = lax.dynamic_index_in_dim(by_depth, 1 - core, 2, keepdims=False)  8.15 us
    reshape x1, local copies, waits for them, and re-layouts, body(): by_depth = weights.reshape(stride, depth, cores, columns)  7.06 us
    convert_element_type x1, other arithmetic, body(): (codes.astype(F32) * jnp.repeat(scales, group_size, axis=0)).astype(BF)  4.27 us
    pallas_call x6, Pallas kernels, whole(): pl.pallas_call(kernel, out_shape=out_shape, compiler_params=pltpu.Compile...  4.21 us
  transfers between devices with their start and end apart: 8, of which 6 were waited for; matrix products, arithmetic and copies ran while one was open for 17% of the time, Pallas kernels for 2%

profile of v4, /device:TPU:8, one launch (start us, length us, event | category | flops | bytes accessed | tf_op | source)
XLA Modules:
  0.0 178.8 jit_solution(10428201765937359367)
XLA Ops:
  11.8 10.2 %all-to-all-start.2 = ((bf16[32,5,384]{2,1,0:T(8,128)(2,1)}), bf16[32,5,384]{2,1,0:T(8,128)(2,1)S(1)}, u32[]{:S(2)}, u32[]{:S(2)}) async-start(bf16[32,5,384]{2,1,0:T(8,128)(2,1)} %all_to_all.25), calls=%async_computation.3 | async-start | bytes 393216 | tf_op jit(solution)/shard_map/all_to_all | solution.py:34
  22.1 10.9 %all-to-all-done.2 = bf16[32,5,384]{2,1,0:T(8,128)(2,1)S(1)} async-done(((bf16[32,5,384]{2,1,0:T(8,128)(2,1)}), bf16[32,5,384]{2,1,0:T(8,128)(2,1)S(1)}, u32[]{:S(2)}, u32[]{:S(2)}) %all-to-all-start.2) | async-done | bytes 122912 | tf_op jit(solution)/shard_map/all_to_all | solution.py:34
  33.9 4.3 %fusion = bf16[256,6144]{1,0:T(8,128)(2,1)} fusion(bf16[256,6144]{1,0:T(8,128)(2,1)} %param.11, f32[4,6144]{1,0:T(4,128)} %param.12), kind=kLoop, calls=%fused_computation.1 | loop fusion | flops 4718592 | bytes 6389760 | tf_op jit(solution)/shard_map/convert_element_type | solution.py:229
  38.1 7.1 %reshape.108 = bf16[256,8,2,384]{3,2,1,0:T(2,128)(2,1)S(1)} reshape(bf16[256,6144]{1,0:T(8,128)(2,1)} %fusion) | data formatting | bytes 6291456 | tf_op jit(solution)/shard_map/reshape | solution.py:230
  45.2 8.2 %constant_dynamic-slice_fusion = (bf16[256,8,1,384]{3,2,1,0:T(2,128)(2,1)S(1)}, bf16[256,8,1,384]{3,2,1,0:T(2,128)(2,1)}) fusion(bf16[256,8,2,384]{3,2,1,0:T(2,128)(2,1)S(1)} %reshape.108, s32[]{:T(128)S(6)} %select_n.44, s32[]{:T(128)S(6)} %select_n.43), kind=kLoop, calls=%fused_computation.64 | loop fusion | bytes 6291464 | tf_op jit(solution)/shard_map/jit(dynamic_index_in_dim)/dynamic_slice | solution.py:232
  53.9 2.1 %collective-permute-start = (bf16[256,8,384]{2,0,1:T(8,128)(2,1)S(1)}, bf16[256,8,384]{2,0,1:T(8,128)(2,1)S(1)}, u32[]{:S(2)}, u32[]{:S(2)}) collective-permute-start(bf16[256,8,384]{2,0,1:T(8,128)(2,1)S(1)} %bitcast.63), channel_id=1, source_target_pairs={{0,1},{1,0},{2,3},{3,2},{4,5},{5,4},{6,7},{7,6},{8,9},{9,8},{10,11... | collective-permute-start | bytes 4718600 | tf_op jit(solution)/shard_map/ppermute | solution.py:233
  56.2 22.0 %all_to_all.37.chunks_ref = bf16[64,8,128]{2,1,0:T(8,128)(2,1)S(1)} all-to-all(bf16[64,8,128]{2,1,0:T(8,128)(2,1)S(1)} %shard_map.137), channel_id=1, replica_groups=mesh['e'=8,'r'=4,'z'=8,'c'=2] {'r','z','c'}, dimensions={0} | all-to-all | bytes 262144 | tf_op jit(solution)/shard_map/all_to_all | solution.py:34
  78.9 14.7 %all_to_all.38.chunks_ref = bf16[64,8,128]{2,1,0:T(8,128)(2,1)S(1)} all-to-all(bf16[64,8,128]{2,1,0:T(8,128)(2,1)S(1)} %get-tuple-element.8), channel_id=1, replica_groups=mesh['e'=8,'r'=4,'z'=8,'c'=2] {'r','z','c'}, dimensions={0} | all-to-all | bytes 262144 | tf_op jit(solution)/shard_map/all_to_all | solution.py:34
  94.0 2.0 %collective-permute-start.1 = (bf16[160,256]{1,0:T(8,128)(2,1)S(1)}, bf16[160,256]{1,0:T(8,128)(2,1)S(1)}, u32[]{:S(2)}, u32[]{:S(2)}) collective-permute-start(bf16[160,256]{1,0:T(8,128)(2,1)S(1)} %shard_map.139.rotated_ref), channel_id=1, source_target_pairs={{0,1},{1,0},{2,3},{3,2},{4,5},{5,4},{6,7},{7,6},{8,9},{9,8},{10,11... | collective-permute-start | bytes 245768 | tf_op jit(solution)/shard_map/ppermute | solution.py:234
  97.2 1.8 add_bitcast_fusion
  99.1 2.5 %fusion.9.grad_ref = bf16[160,64]{1,0:T(8,128)(2,1)S(1)} fusion(bf16[224,6144]{1,0:T(8,128)(2,1)} %all-gather.2.cloned.1.call-done), kind=kOutput, calls=%fused_computation.13 | convolution fusion | flops 125849600 | bytes 2772992 | tf_op jit(solution)/shard_map/dot_general | solution.py:241
  101.8 2.7 %fusion.3.main_ref = f32[160,256]{1,0:T(8,128)S(1)} fusion(bf16[256,6144]{1,0:T(8,128)(2,1)S(1)} %copy-done.4, bf16[224,6144]{1,0:T(8,128)(2,1)} %all-gather.2.cloned.1.call-done), kind=kOutput, calls=%fused_computation.5 | convolution fusion | flops 503316480 | bytes 5275648 | tf_op jit(solution)/shard_map/dot_general | solution.py:38
  104.6 1.3 shard_map.140
  106.0 5.7 %all-to-all-start.3 = ((bf16[64,8,128]{2,1,0:T(8,128)(2,1)}), bf16[64,8,128]{2,1,0:T(8,128)(2,1)S(1)}, u32[]{:S(2)}, u32[]{:S(2)}) async-start(bf16[64,8,128]{2,1,0:T(8,128)(2,1)} %shard_map.140), calls=%async_computation.4 | async-start | bytes 262144 | tf_op jit(solution)/shard_map/all_to_all | solution.py:34
  111.6 9.5 %all-to-all-done.3.chunks_ref = bf16[64,8,128]{2,1,0:T(8,128)(2,1)S(1)} async-done(((bf16[64,8,128]{2,1,0:T(8,128)(2,1)}), bf16[64,8,128]{2,1,0:T(8,128)(2,1)S(1)}, u32[]{:S(2)}, u32[]{:S(2)}) %all-to-all-start.3) | async-done | bytes 131104 | tf_op jit(solution)/shard_map/all_to_all | solution.py:34
  121.9 5.6 %all-to-all-start.4 = ((bf16[64,8,128]{2,1,0:T(8,128)(2,1)}), bf16[64,8,128]{2,1,0:T(8,128)(2,1)S(1)}, u32[]{:S(2)}, u32[]{:S(2)}) async-start(bf16[64,8,128]{2,1,0:T(8,128)(2,1)} %get-tuple-element.9), calls=%async_computation.5 | async-start | bytes 262144 | tf_op jit(solution)/shard_map/all_to_all | solution.py:34
  127.9 9.2 %all-to-all-done.4.chunks_ref = bf16[64,8,128]{2,1,0:T(8,128)(2,1)S(1)} async-done(((bf16[64,8,128]{2,1,0:T(8,128)(2,1)}), bf16[64,8,128]{2,1,0:T(8,128)(2,1)S(1)}, u32[]{:S(2)}, u32[]{:S(2)}) %all-to-all-start.4) | async-done | bytes 131104 | tf_op jit(solution)/shard_map/all_to_all | solution.py:34
  137.4 3.2 %reduce-scatter.2.cloned.1.call-done = f32[1,160,384]{2,1,0:T(8,128)} async-done(((f32[8,160,384]{2,1,0:T(8,128)}), f32[1,160,384]{2,1,0:T(8,128)}) %reduce-scatter.2.cloned.1.call-update) | async-done | bytes 245776 | tf_op jit(solution)/shard_map/reduce_scatter | solution.py:237
  140.6 1.0 fusion.14
  141.9 1.1 pad_maximum_fusion
  143.0 10.1 %all-to-all-start.5 = ((bf16[32,22,384]{2,1,0:T(8,128)(2,1)}), bf16[32,22,384]{2,1,0:T(8,128)(2,1)S(1)}, u32[]{:S(2)}, u32[]{:S(2)}) async-start(bf16[32,22,384]{2,1,0:T(8,128)(2,1)} %pad_maximum_fusion), calls=%async_computation.6 | async-start | bytes 1179648 | tf_op jit(solution)/shard_map/all_to_all | solution.py:34
  154.2 0.9 shard_map.142
  155.0 13.3 %all-to-all-done.5 = bf16[32,22,384]{2,1,0:T(8,128)(2,1)S(1)} async-done(((bf16[32,22,384]{2,1,0:T(8,128)(2,1)}), bf16[32,22,384]{2,1,0:T(8,128)(2,1)S(1)}, u32[]{:S(2)}, u32[]{:S(2)}) %all-to-all-start.5) | async-done | bytes 540704 | tf_op jit(solution)/shard_map/all_to_all | solution.py:34
  168.4 0.9 bitcast_convert_fusion
  (89 shorter events, 12.6 us)
Async XLA Ops:
  8.0 14.1 %copy-start = (bf16[8,64,384]{2,1,0:T(8,128)(2,1)S(1)}, bf16[8,64,384]{2,1,0:T(8,128)(2,1)}, u32[]{:S(2)}) copy-start(bf16[8,64,384]{2,1,0:T(8,128)(2,1)} %param.15) | copy-start | bytes 1179652
  11.8 21.2 %all-to-all-start.2 = ((bf16[32,5,384]{2,1,0:T(8,128)(2,1)}), bf16[32,5,384]{2,1,0:T(8,128)(2,1)S(1)}, u32[]{:S(2)}, u32[]{:S(2)}) async-start(bf16[32,5,384]{2,1,0:T(8,128)(2,1)} %all_to_all.25), calls=%async_computation.3 | async-start | bytes 393216 | tf_op jit(solution)/shard_map/all_to_all | solution.py:34
  22.0 77.1 %all-gather.2.cloned.1.call-start = ((), (), s32[]{:S(2)}) async-start(), calls=%async_computation.8 | async-start | bytes 2924544 | tf_op jit(solution)/shard_map/all_gather | solution.py:221
  22.1 11.8 %copy-start.8 = (bf16[64,384]{1,0:T(8,128)(2,1)}, bf16[64,384]{1,0:T(8,128)(2,1)S(1)}, u32[]{:S(2)}) copy-start(bf16[64,384]{1,0:T(8,128)(2,1)S(1)} %dynamic-slice_bitcast_fusion) | copy-start | bytes 147460
  33.1 0.8 copy-start.6
  33.8 106.8 %reduce-scatter.2.cloned.1.call-start = ((), (), s32[]{:S(2)}) async-start(), calls=%async_computation.7 | async-start | bytes 2211840 | tf_op jit(solution)/shard_map/reduce_scatter | solution.py:237
  53.4 2.6 %copy-start.2 = (bf16[160,256]{1,0:T(8,128)(2,1)S(1)}, bf16[160,256]{1,0:T(8,128)(2,1)}, u32[]{:S(2)}) copy-start(bf16[160,256]{1,0:T(8,128)(2,1)} %values_ref.1) | copy-start | bytes 245764
  53.4 2.6 %copy-start.3 = (s32[256]{0:T(256)S(1)}, s32[256]{0:T(256)}, u32[]{:S(2)}) copy-start(s32[256]{0:T(256)} %param.13) | copy-start | bytes 3076
  53.4 40.2 %copy-start.1 = (bf16[256,256]{1,0:T(8,128)(2,1)S(1)}, bf16[256,256]{1,0:T(8,128)(2,1)}, u32[]{:S(2)}) copy-start(bf16[256,256]{1,0:T(8,128)(2,1)} %constant.75.clone.spread_ref) | copy-start | bytes 393220
  53.4 42.7 %copy-start.5 = (bf16[256,8,1,384]{3,2,1,0:T(2,128)(2,1)S(1)}, bf16[256,8,1,384]{3,2,1,0:T(2,128)(2,1)}, u32[]{:S(2)}) copy-start(bf16[256,8,1,384]{3,2,1,0:T(2,128)(2,1)} %get-tuple-element.42) | copy-start | bytes 4718596
  53.9 43.2 %collective-permute-start = (bf16[256,8,384]{2,0,1:T(8,128)(2,1)S(1)}, bf16[256,8,384]{2,0,1:T(8,128)(2,1)S(1)}, u32[]{:S(2)}, u32[]{:S(2)}) collective-permute-start(bf16[256,8,384]{2,0,1:T(8,128)(2,1)S(1)} %bitcast.63), channel_id=1, source_target_pairs={{0,1},{1,0},{2,3},{3,2},{4,5},{5,4},{6,7},{7,6},{8,9},{9,8},{10,11... | collective-permute-start | bytes 4718600 | tf_op jit(solution)/shard_map/ppermute | solution.py:233
  94.0 3.2 %collective-permute-start.1 = (bf16[160,256]{1,0:T(8,128)(2,1)S(1)}, bf16[160,256]{1,0:T(8,128)(2,1)S(1)}, u32[]{:S(2)}, u32[]{:S(2)}) collective-permute-start(bf16[160,256]{1,0:T(8,128)(2,1)S(1)} %shard_map.139.rotated_ref), channel_id=1, source_target_pairs={{0,1},{1,0},{2,3},{3,2},{4,5},{5,4},{6,7},{7,6},{8,9},{9,8},{10,11... | collective-permute-start | bytes 245768 | tf_op jit(solution)/shard_map/ppermute | solution.py:234
  96.7 2.2 %copy-start.10 = (bf16[256,64]{0,1:T(8,128)(2,1)S(1)}, bf16[256,64]{0,1:T(8,128)(2,1)}, u32[]{:S(2)}) copy-start(bf16[256,64]{0,1:T(8,128)(2,1)} %param.14) | copy-start | bytes 98308
  99.1 2.7 %copy-start.4 = (bf16[256,6144]{1,0:T(8,128)(2,1)S(1)}, bf16[256,6144]{1,0:T(8,128)(2,1)}, u32[]{:S(2)}) copy-start(bf16[256,6144]{1,0:T(8,128)(2,1)} %fusion) | copy-start | bytes 9437188
  101.8 35.3 %copy-start.9 = (bf16[64,384]{1,0:T(8,128)(2,1)S(1)}, bf16[64,384]{1,0:T(8,128)(2,1)}, u32[]{:S(2)}) copy-start(bf16[64,384]{1,0:T(8,128)(2,1)} %copy-done.8) | copy-start | bytes 147460
  104.6 37.1 %copy-start.7 = (bf16[160,384]{1,0:T(8,128)(2,1)S(1)}, bf16[160,384]{1,0:T(8,128)(2,1)}, u32[]{:S(2)}) copy-start(bf16[160,384]{1,0:T(8,128)(2,1)} %copy-done.6) | copy-start | bytes 368644
  106.0 47.3 %copy-start.11 = (s32[16,2]{0,1:T(2,128)S(1)}, s32[16,2]{0,1:T(2,128)}, u32[]{:S(2)}) copy-start(s32[16,2]{0,1:T(2,128)} %param.16) | copy-start | bytes 388
  106.0 47.3 %copy-start.12 = (f32[16,2]{0,1:T(2,128)S(1)}, f32[16,2]{0,1:T(2,128)}, u32[]{:S(2)}) copy-start(f32[16,2]{0,1:T(2,128)} %param.17) | copy-start | bytes 388
  106.0 15.2 %all-to-all-start.3 = ((bf16[64,8,128]{2,1,0:T(8,128)(2,1)}), bf16[64,8,128]{2,1,0:T(8,128)(2,1)S(1)}, u32[]{:S(2)}, u32[]{:S(2)}) async-start(bf16[64,8,128]{2,1,0:T(8,128)(2,1)} %shard_map.140), calls=%async_computation.4 | async-start | bytes 262144 | tf_op jit(solution)/shard_map/all_to_all | solution.py:34
  121.9 15.1 %all-to-all-start.4 = ((bf16[64,8,128]{2,1,0:T(8,128)(2,1)}), bf16[64,8,128]{2,1,0:T(8,128)(2,1)S(1)}, u32[]{:S(2)}, u32[]{:S(2)}) async-start(bf16[64,8,128]{2,1,0:T(8,128)(2,1)} %get-tuple-element.9), calls=%async_computation.5 | async-start | bytes 262144 | tf_op jit(solution)/shard_map/all_to_all | solution.py:34
  143.0 25.3 %all-to-all-start.5 = ((bf16[32,22,384]{2,1,0:T(8,128)(2,1)}), bf16[32,22,384]{2,1,0:T(8,128)(2,1)S(1)}, u32[]{:S(2)}, u32[]{:S(2)}) async-start(bf16[32,22,384]{2,1,0:T(8,128)(2,1)} %pad_maximum_fusion), calls=%async_computation.6 | async-start | bytes 1179648 | tf_op jit(solution)/shard_map/all_to_all | solution.py:34
Sparse Core Ops, SparseCore 0:
  33.9 43.1 all-gather.1
Sparse Core Ops, SparseCore 1:
  99.1 41.5 reduce-scatter.1

commit v5 on v4

--- a/solution.py
+++ b/solution.py
@@ -57,6 +57,106 @@
         out_shape=out_shape,
         compiler_params=pltpu.CompilerParams(vmem_limit_bytes=32 * 1024 * 1024),
     )(*operands)
+
+
+def route(experts, gates, output_gradient, row_slot, capacity):
+    tokens, columns = output_gradient.shape
+    choices = experts.shape[1]
+
+    def kernel(experts_ref, gates_ref, grad_ref, row_slot_ref, out_ref, target_ref):
+        ids = experts_ref[...]
+        gate = gates_ref[...]
+        grad = grad_ref[...].astype(F32)
+        expert = lax.broadcasted_iota(jnp.int32, (tokens, EXPERT_COUNT), 1)
+        named = [
+            jnp.where(ids[:, k : k + 1] == expert, 1.0, 0.0) for k in range(choices)
+        ]
+        row = lax.broadcasted_iota(jnp.int32, (tokens, tokens), 0)
+        col = lax.broadcasted_iota(jnp.int32, (tokens, tokens), 1)
+        lower = jnp.where(row > col, 1.0, 0.0).astype(BF)
+        earlier = dot(lower, sum(named).astype(BF))
+        rows = 0.0
+        targets = []
+        for k in range(choices):
+            slot = jnp.sum(earlier * named[k], axis=1, keepdims=True).astype(jnp.int32)
+            target = ids[:, k : k + 1] * capacity + slot
+            match = jnp.where(target == row_slot_ref[...], 1.0, 0.0).astype(BF)
+            weighted = (gate[:, k : k + 1] * grad).astype(BF)
+            rows = rows + dot(match, weighted, ((0,), (0,)))
+            earlier = earlier + named[k]
+            targets.append(target)
+        out_ref[...] = rows.astype(BF)
+        choice = lax.broadcasted_iota(jnp.int32, (tokens, choices), 1)
+        chosen = targets[0]
+        for k in range(1, choices):
+            chosen = jnp.where(choice == k, targets[k], chosen)
+        target_ref[...] = chosen
+
+    out = (
+        jax.ShapeDtypeStruct((row_slot.shape[1], columns), BF),
+        jax.ShapeDtypeStruct((tokens, choices), jnp.int32),
+    )
+    return whole(kernel, out, experts, gates, output_gradient, row_slot)
+
+
+def dequantize(codes, scales, depth, columns):
+    stride, width = codes.shape
+    groups = scales.shape[0]
+    size = stride // groups
+
+    def kernel(codes_ref, scales_ref, all_ref, own_ref, other_ref):
+        first = lax.axis_index("c") == 0
+        for group in range(groups):
+            rows = slice(group * size, (group + 1) * size)
+            values = codes_ref[rows, :].astype(F32) * scales_ref[group : group + 1, :]
+            all_ref[rows, :] = values.astype(BF)
+            low, high = values[:, :columns], values[:, columns:]
+            own_ref[0, rows, :] = jnp.where(first, low, high).astype(BF)
+            other_ref[0, rows, :] = jnp.where(first, high, low).astype(BF)
+
+    half = pl.BlockSpec((1, stride, columns), lambda z: (z, 0, 0))
+    halves = jax.ShapeDtypeStruct((depth, stride, columns), BF)
+    return pl.pallas_call(
+        kernel,
+        grid=(depth,),
+        in_specs=[
+            pl.BlockSpec((stride, 2 * columns), lambda z: (0, z)),
+            pl.BlockSpec((groups, 2 * columns), lambda z: (0, z)),
+        ],
+        out_specs=(pl.BlockSpec((stride, 2 * columns), lambda z: (0, z)), half, half),
+        out_shape=(jax.ShapeDtypeStruct((stride, width), BF), halves, halves),
+        cost_estimate=pl.CostEstimate(
+            flops=2 * stride * width, bytes_accessed=6 * stride * width, transcendentals=0
+        ),
+        compiler_params=pltpu.CompilerParams(vmem_limit_bytes=32 * 1024 * 1024),
+    )(codes, scales)
+
+
+def pair_products(rotated, neighbour, own, other):
+    depth, stride, columns = own.shape
+    height = rotated.shape[0]
+    step = 2
+
+    def kernel(rotated_ref, neighbour_ref, own_ref, other_ref, out_ref):
+        for z in range(step):
+            total = dot(rotated_ref[...], own_ref[z]) + dot(neighbour_ref[...], other_ref[z])
+            out_ref[z] = total
+
+    rows = pl.BlockSpec((height, stride), lambda z: (0, 0))
+    half = pl.BlockSpec((step, stride, columns), lambda z: (z, 0, 0))
+    return pl.pallas_call(
+        kernel,
+        grid=(depth // step,),
+        in_specs=[rows, rows, half, half],
+        out_specs=pl.BlockSpec((step, height, columns), lambda z: (z, 0, 0)),
+        out_shape=jax.ShapeDtypeStruct((depth, height, columns), F32),
+        cost_estimate=pl.CostEstimate(
+            flops=4 * height * stride * depth * columns,
+            bytes_accessed=4 * depth * columns * (stride + height),
+            transcendentals=0,
+        ),
+        compiler_params=pltpu.CompilerParams(vmem_limit_bytes=32 * 1024 * 1024),
+    )(rotated, neighbour, own, other)
 
 
 def to_chunks(values, signs):
@@ -188,52 +288,39 @@
     hidden, codes, scales, signs, lowrank_down_map, lowrank_up_map, experts, gates, output_gradient
 ):
     slot_rows, stride = hidden.shape
-    replicas, depth, cores = lax.axis_size("r"), lax.axis_size("z"), lax.axis_size("c")
+    replicas, depth = lax.axis_size("r"), lax.axis_size("z")
     devices = EXPERT_COUNT * replicas
     rank = lowrank_down_map.shape[1]
     expert_position = lax.axis_index("e")
     replica = lax.axis_index("r")
-    core = lax.axis_index("c")
     capacity = slot_rows // devices
     tokens_here = experts.shape[0]
     columns = output_gradient.shape[1]
     scaling = 1.0 / math.sqrt(HIDDEN_UNITS)
-    group_size = codes.shape[0] // scales.shape[0]
-
-    flat_ids = experts.reshape(tokens_here * 2)
-    assigned = (flat_ids[:, None] == jnp.arange(EXPERT_COUNT, dtype=jnp.int32)[None, :]).astype(
-        jnp.int32
-    )
-    earlier = jnp.cumsum(assigned, axis=0) - assigned
-    slot_index = jnp.sum(earlier * assigned, axis=1)
-    target = flat_ids * capacity + slot_index
-    row = jnp.arange(devices * capacity, dtype=jnp.int32)
+
+    row = np.arange(devices * capacity)
     row_slot = row // (replicas * capacity) * capacity + row % capacity
-    copier = (row_slot[:, None] == target[None, :]).astype(BF)
-    weighted = (
-        (gates[:, :, None] * output_gradient.astype(F32)[:, None, :])
-        .reshape(tokens_here * 2, columns)
-        .astype(BF)
-    )
-    outgoing = jnp.dot(copier, weighted, preferred_element_type=F32).astype(BF)
+    row_slot = jnp.asarray(row_slot[None], jnp.int32)
+    outgoing, target = route(experts, gates, output_gradient, row_slot, capacity)
+    target = target.reshape(tokens_here * 2)
+    weights, own, other = dequantize(codes, scales, depth, columns)
     d_rows = exchange(outgoing, EXPERT)
+    chunks = to_chunks(hidden, signs)
+    d_rows, weights, own, other, chunks = lax.optimization_barrier(
+        (d_rows, weights, own, other, chunks)
+    )
     lowrank_local = lax.dynamic_index_in_dim(lowrank_up_map, expert_position, 0, keepdims=False)
     gathered = lax.all_gather(
         jnp.concatenate([d_rows, lowrank_local], axis=0), TENSOR, axis=1, tiled=True
     )
 
     spread_local = sylvester(stride)
-    mixed_blocks, _ = mix_blocks(exchange(to_chunks(hidden, signs), SLAB))
+    mixed_blocks, _ = mix_blocks(exchange(chunks, SLAB))
     rotated = finish_rotation(exchange(mixed_blocks, SLAB), spread_local, scaling)
 
-    weights = (codes.astype(F32) * jnp.repeat(scales, group_size, axis=0)).astype(BF)
-    by_depth = weights.reshape(stride, depth, cores, columns)
-    own = lax.dynamic_index_in_dim(by_depth, core, 2, keepdims=False)
-    other = lax.dynamic_index_in_dim(by_depth, 1 - core, 2, keepdims=False)
     other = lax.ppermute(other, "c", [(0, 1), (1, 0)])
     neighbour = lax.ppermute(rotated, "c", [(0, 1), (1, 0)])
-    pair = jnp.einsum("sk,kzf->zsf", rotated, own, preferred_element_type=F32)
-    pair = pair + jnp.einsum("sk,kzf->zsf", neighbour, other, preferred_element_type=F32)
+    pair = pair_products(rotated, neighbour, own, other)
     frozen = lax.psum_scatter(pair, "z", scatter_dimension=0, tiled=False)
 
     d_full = gathered[:slot_rows]

time: 180 us -> 164 us (0.911)
  local copies, waits for them, and re-layouts: 20.9 us -> 13.4 us
  waiting for transfers between devices: 46.6 us -> 39.5 us
  Pallas kernels: 4.21 us -> 8.83 us
  other arithmetic: 8.83 us -> 4.21 us
  matrix products: 9.93 us -> 7.21 us
    unnamed x34 -> x35, local copies, waits for them, and re-layouts: 3.12 us -> 11.8 us
    dynamic_slice x1 -> x0, local copies, waits for them, and re-layouts: 8.15 us -> none  [body(): other = lax.dynamic_index_in_dim(by_depth, 1 - core, 2, keepdims=False)]
    reshape x1 -> x0, local copies, waits for them, and re-layouts: 7.06 us -> none  [body(): by_depth = weights.reshape(stride, depth, cores, columns)]
    all_to_all x4, waiting for transfers between devices: 42.9 us -> 36.6 us  [exchange(): return lax.all_to_all(value, axes, split_axis=0, concat_axis=0, tiled=True)]
    convert_element_type x2 -> x0, other arithmetic: 4.34 us -> none  [the longest x1 4.27 us: body(): (codes.astype(F32) * jnp.repeat(scales, group_size, axis=0)).astype(BF)]
    pallas_call x0 -> x2, Pallas kernels: none -> 4.03 us  [the longest x1 2.58 us: pair_products(): pl.pallas_call(kernel, grid=(depth // step,), in_specs=[rows, rows, half,...]
    reduce_scatter x1, waiting for transfers between devices: 3.22 us -> 0.03 us  [body(): frozen = lax.psum_scatter(pair, 'z', scatter_dimension=0, tiled=False)]
    dot_general x3 -> x0, matrix products: 2.71 us -> none  [the longest x1 1.77 us: body(): jnp.einsum('sk,kzf->zsf', neighbour, other, preferred_element_type=F32)]
  transfers between devices with their start and end apart: 8 -> 8, of which waited for: 6 -> 6; matrix products, arithmetic and copies ran while one was open for 17% -> 4% of each run, Pallas kernels for 2% -> 5%
where the time goes in v5:
time: 164 us; the launch traced here: 163 us
  waiting for transfers between devices  39.5 us (24%)
  starting transfers between devices  37 us (23%)
  blocking collectives  36.9 us (22%)
  between operations  15.8 us (10%)
  local copies, waits for them, and re-layouts  13.4 us (8%)
  Pallas kernels  8.83 us (5%)
  matrix products  7.21 us (4%)
  other arithmetic  4.21 us (3%)
    all_to_all x2, blocking collectives, exchange(): return lax.all_to_all(value, axes, split_axis=0, concat_axis=0, tiled=True)  36.9 us
    all_to_all x4, waiting for transfers between devices, exchange(): return lax.all_to_all(value, axes, split_axis=0, concat_axis=0, tiled=True)  36.6 us
    all_to_all x4, starting transfers between devices, exchange(): return lax.all_to_all(value, axes, split_axis=0, concat_axis=0, tiled=True)  33 us
    unnamed x35, local copies, waits for them, and re-layouts  11.8 us
    pallas_call x7, Pallas kernels, whole(): pl.pallas_call(kernel, out_shape=out_shape, compiler_params=pltpu.Compile...  4.8 us
    dot_general x2, matrix products, dot(): lax.dot_general(left, right, (dims, ((), ())), preferred_element_type=F32)  3.57 us
  transfers between devices with their start and end apart: 8, of which 6 were waited for; matrix products, arithmetic and copies ran while one was open for 4% of the time, Pallas kernels for 5%

profile of v5, /device:TPU:8, one launch (start us, length us, event | category | flops | bytes accessed | tf_op | source)
XLA Modules:
  0.0 162.9 jit_solution(1647779065886311575)
XLA Ops:
  12.3 10.2 %all-to-all-start = ((bf16[32,5,384]{2,1,0:T(8,128)(2,1)}), bf16[32,5,384]{2,1,0:T(8,128)(2,1)S(1)}, u32[]{:S(2)}, u32[]{:S(2)}) async-start(bf16[32,5,384]{2,1,0:T(8,128)(2,1)} %all_to_all.23), calls=%async_computation | async-start | bytes 393216 | tf_op jit(solution)/shard_map/all_to_all | solution.py:34
  24.3 1.9 %copy-done.1 = bf16[256,6144]{1,0:T(8,128)(2,1)S(1)} copy-done((bf16[256,6144]{1,0:T(8,128)(2,1)S(1)}, bf16[256,6144]{1,0:T(8,128)(2,1)}, u32[]{:S(2)}) %copy-start.1) | copy-done | bytes 3145752
  27.1 1.4 shard_map.147
  28.6 1.6 %copy-done.9 = bf16[256,6144]{1,0:T(8,128)(2,1)} copy-done((bf16[256,6144]{1,0:T(8,128)(2,1)}, bf16[256,6144]{1,0:T(8,128)(2,1)S(1)}, u32[]{:S(2)}) %copy-start.9) | copy-done | bytes 3145752
  30.2 1.1 copy-done.11
  31.4 2.1 %all-to-all-done = bf16[32,5,384]{2,1,0:T(8,128)(2,1)S(1)} async-done(((bf16[32,5,384]{2,1,0:T(8,128)(2,1)}), bf16[32,5,384]{2,1,0:T(8,128)(2,1)S(1)}, u32[]{:S(2)}, u32[]{:S(2)}) %all-to-all-start) | async-done | bytes 122912 | tf_op jit(solution)/shard_map/all_to_all | solution.py:34
  34.3 1.9 %collective-permute-start.1 = (bf16[8,256,384]{2,1,0:T(8,128)(2,1)}, bf16[8,256,384]{2,1,0:T(8,128)(2,1)S(1)}, u32[]{:S(2)}, u32[]{:S(2)}) collective-permute-start(bf16[8,256,384]{2,1,0:T(8,128)(2,1)} %copy-done.11), channel_id=1, source_target_pairs={{0,1},{1,0},{2,3},{3,2},{4,5},{5,4},{6,7},{7,6},{8,9},{9,8},{10,11... | collective-permute-start | bytes 4718600 | tf_op jit(solution)/shard_map/ppermute | solution.py:321
  36.2 22.0 %all_to_all.37.chunks_ref = bf16[64,8,128]{2,1,0:T(8,128)(2,1)S(1)} all-to-all(bf16[64,8,128]{2,1,0:T(8,128)(2,1)S(1)} %shard_map.148), channel_id=1, replica_groups=mesh['e'=8,'r'=4,'z'=8,'c'=2] {'r','z','c'}, dimensions={0} | all-to-all | bytes 262144 | tf_op jit(solution)/shard_map/all_to_all | solution.py:34
  58.8 14.8 %all_to_all.38.chunks_ref = bf16[64,8,128]{2,1,0:T(8,128)(2,1)S(1)} all-to-all(bf16[64,8,128]{2,1,0:T(8,128)(2,1)S(1)} %get-tuple-element.24), channel_id=1, replica_groups=mesh['e'=8,'r'=4,'z'=8,'c'=2] {'r','z','c'}, dimensions={0} | all-to-all | bytes 262144 | tf_op jit(solution)/shard_map/all_to_all | solution.py:34
  74.1 2.0 %collective-permute-start = (bf16[160,256]{1,0:T(8,128)(2,1)S(1)}, bf16[160,256]{1,0:T(8,128)(2,1)S(1)}, u32[]{:S(2)}, u32[]{:S(2)}) collective-permute-start(bf16[160,256]{1,0:T(8,128)(2,1)S(1)} %shard_map.150.rotated_ref), channel_id=1, source_target_pairs={{0,1},{1,0},{2,3},{3,2},{4,5},{5,4},{6,7},{7,6},{8,9},{9,8},{10,11... | collective-permute-start | bytes 245768 | tf_op jit(solution)/shard_map/ppermute | solution.py:322
  76.1 1.1 collective-permute-done.neighbour_ref
  77.2 2.6 %shard_map.151 = f32[8,160,384]{2,1,0:T(8,128)} custom-call(bf16[160,256]{1,0:T(8,128)(2,1)S(1)} %shard_map.150.rotated_ref, bf16[160,256]{1,0:T(8,128)(2,1)S(1)} %collective-permute-done.neighbour_ref, bf16[8,256,384]{2,1,0:T(8,128)(2,1)S(1)} %get-tuple-element.25.own_ref, bf16[8,256,384]{2,1,0:T(8,128)(2,1)S(1)} %collective-permute-done.1.other_ref), custom_call_target="tpu_custom_call" | custom-call | flops 503316480 | bytes 5111808 | tf_op jit(solution)/shard_map/pallas_call | solution.py:147
  80.7 1.7 %all-gather.2.cloned.1.call-done = bf16[224,6144]{1,0:T(8,128)(2,1)} async-done(((bf16[224,384]{1,0:T(8,128)(2,1)}), bf16[224,6144]{1,0:T(8,128)(2,1)}) %all-gather.2.cloned.1.call-update) | async-done | bytes 2752528 | tf_op jit(solution)/shard_map/all_gather | solution.py:313
  82.4 2.5 %fusion.7.grad_ref = bf16[160,64]{1,0:T(8,128)(2,1)S(1)} fusion(bf16[224,6144]{1,0:T(8,128)(2,1)} %all-gather.2.cloned.1.call-done), kind=kOutput, calls=%fused_computation.6 | convolution fusion | flops 125849600 | bytes 2772992 | tf_op jit(solution)/shard_map/dot_general | solution.py:328
  85.1 2.7 %fusion.2.main_ref = f32[160,256]{1,0:T(8,128)S(1)} fusion(bf16[256,6144]{1,0:T(8,128)(2,1)S(1)} %copy-done.10, bf16[224,6144]{1,0:T(8,128)(2,1)} %all-gather.2.cloned.1.call-done), kind=kOutput, calls=%fused_computation.2 | convolution fusion | flops 503316480 | bytes 5275648 | tf_op jit(solution)/shard_map/dot_general | solution.py:38
  87.9 1.3 shard_map.152
  89.2 8.9 %all-to-all-start.3 = ((bf16[64,8,128]{2,1,0:T(8,128)(2,1)}), bf16[64,8,128]{2,1,0:T(8,128)(2,1)S(1)}, u32[]{:S(2)}, u32[]{:S(2)}) async-start(bf16[64,8,128]{2,1,0:T(8,128)(2,1)} %shard_map.152), calls=%async_computation.4 | async-start | bytes 262144 | tf_op jit(solution)/shard_map/all_to_all | solution.py:34
  98.1 9.5 %all-to-all-done.3.chunks_ref = bf16[64,8,128]{2,1,0:T(8,128)(2,1)S(1)} async-done(((bf16[64,8,128]{2,1,0:T(8,128)(2,1)}), bf16[64,8,128]{2,1,0:T(8,128)(2,1)S(1)}, u32[]{:S(2)}, u32[]{:S(2)}) %all-to-all-start.3) | async-done | bytes 131104 | tf_op jit(solution)/shard_map/all_to_all | solution.py:34
  108.4 5.6 %all-to-all-start.4 = ((bf16[64,8,128]{2,1,0:T(8,128)(2,1)}), bf16[64,8,128]{2,1,0:T(8,128)(2,1)S(1)}, u32[]{:S(2)}, u32[]{:S(2)}) async-start(bf16[64,8,128]{2,1,0:T(8,128)(2,1)} %get-tuple-element.29), calls=%async_computation.5 | async-start | bytes 262144 | tf_op jit(solution)/shard_map/all_to_all | solution.py:34
  114.3 9.2 %all-to-all-done.4.chunks_ref = bf16[64,8,128]{2,1,0:T(8,128)(2,1)S(1)} async-done(((bf16[64,8,128]{2,1,0:T(8,128)(2,1)}), bf16[64,8,128]{2,1,0:T(8,128)(2,1)S(1)}, u32[]{:S(2)}, u32[]{:S(2)}) %all-to-all-start.4) | async-done | bytes 131104 | tf_op jit(solution)/shard_map/all_to_all | solution.py:34
  123.9 1.0 fusion.12
  125.1 1.1 pad_maximum_fusion
  126.2 8.4 %all-to-all-start.5 = ((bf16[32,22,384]{2,1,0:T(8,128)(2,1)}), bf16[32,22,384]{2,1,0:T(8,128)(2,1)S(1)}, u32[]{:S(2)}, u32[]{:S(2)}) async-start(bf16[32,22,384]{2,1,0:T(8,128)(2,1)} %pad_maximum_fusion), calls=%async_computation.6 | async-start | bytes 1179648 | tf_op jit(solution)/shard_map/all_to_all | solution.py:34
  136.6 15.8 %all-to-all-done.5 = bf16[32,22,384]{2,1,0:T(8,128)(2,1)S(1)} async-done(((bf16[32,22,384]{2,1,0:T(8,128)(2,1)}), bf16[32,22,384]{2,1,0:T(8,128)(2,1)S(1)}, u32[]{:S(2)}, u32[]{:S(2)}) %all-to-all-start.5) | async-done | bytes 540704 | tf_op jit(solution)/shard_map/all_to_all | solution.py:34
  (77 shorter events, 16.4 us)
Async XLA Ops:
  8.0 23.4 %copy-start = (bf16[8,64,384]{2,1,0:T(8,128)(2,1)S(1)}, bf16[8,64,384]{2,1,0:T(8,128)(2,1)}, u32[]{:S(2)}) copy-start(bf16[8,64,384]{2,1,0:T(8,128)(2,1)} %param.16) | copy-start | bytes 1179652
  9.6 0.7 copy-start.5
  10.3 0.7 copy-start.8
  12.3 21.2 %all-to-all-start = ((bf16[32,5,384]{2,1,0:T(8,128)(2,1)}), bf16[32,5,384]{2,1,0:T(8,128)(2,1)S(1)}, u32[]{:S(2)}, u32[]{:S(2)}) async-start(bf16[32,5,384]{2,1,0:T(8,128)(2,1)} %all_to_all.23), calls=%async_computation | async-start | bytes 393216 | tf_op jit(solution)/shard_map/all_to_all | solution.py:34
  22.5 59.9 %all-gather.2.cloned.1.call-start = ((), (), s32[]{:S(2)}) async-start(), calls=%async_computation.8 | async-start | bytes 2924544 | tf_op jit(solution)/shard_map/all_gather | solution.py:313
  22.5 0.9 copy-start.4
  23.4 0.7 copy-start.6
  24.3 1.9 %copy-start.1 = (bf16[256,6144]{1,0:T(8,128)(2,1)S(1)}, bf16[256,6144]{1,0:T(8,128)(2,1)}, u32[]{:S(2)}) copy-start(bf16[256,6144]{1,0:T(8,128)(2,1)} %codes_ref.1) | copy-start | bytes 9437188
  26.2 0.9 copy-start.3
  27.1 46.6 %copy-start.2 = (bf16[256,256]{1,0:T(8,128)(2,1)S(1)}, bf16[256,256]{1,0:T(8,128)(2,1)}, u32[]{:S(2)}) copy-start(bf16[256,256]{1,0:T(8,128)(2,1)} %constant.37.clone.spread_ref) | copy-start | bytes 393220
  28.6 1.6 %copy-start.9 = (bf16[256,6144]{1,0:T(8,128)(2,1)}, bf16[256,6144]{1,0:T(8,128)(2,1)S(1)}, u32[]{:S(2)}) copy-start(bf16[256,6144]{1,0:T(8,128)(2,1)S(1)} %get-tuple-element.28) | copy-start | bytes 9437188
  30.2 1.1 copy-start.11
  34.2 89.7 %reduce-scatter.2.cloned.1.call-start = ((), (), s32[]{:S(2)}) async-start(), calls=%async_computation.7 | async-start | bytes 2211840 | tf_op jit(solution)/shard_map/reduce_scatter | solution.py:324
  34.3 43.0 %collective-permute-start.1 = (bf16[8,256,384]{2,1,0:T(8,128)(2,1)}, bf16[8,256,384]{2,1,0:T(8,128)(2,1)S(1)}, u32[]{:S(2)}, u32[]{:S(2)}) collective-permute-start(bf16[8,256,384]{2,1,0:T(8,128)(2,1)} %copy-done.11), channel_id=1, source_target_pairs={{0,1},{1,0},{2,3},{3,2},{4,5},{5,4},{6,7},{7,6},{8,9},{9,8},{10,11... | collective-permute-start | bytes 4718600 | tf_op jit(solution)/shard_map/ppermute | solution.py:321
  74.1 3.2 %collective-permute-start = (bf16[160,256]{1,0:T(8,128)(2,1)S(1)}, bf16[160,256]{1,0:T(8,128)(2,1)S(1)}, u32[]{:S(2)}, u32[]{:S(2)}) collective-permute-start(bf16[160,256]{1,0:T(8,128)(2,1)S(1)} %shard_map.150.rotated_ref), channel_id=1, source_target_pairs={{0,1},{1,0},{2,3},{3,2},{4,5},{5,4},{6,7},{7,6},{8,9},{9,8},{10,11... | collective-permute-start | bytes 245768 | tf_op jit(solution)/shard_map/ppermute | solution.py:322
  79.8 0.8 copy-start.12
  82.4 2.7 %copy-start.10 = (bf16[256,6144]{1,0:T(8,128)(2,1)S(1)}, bf16[256,6144]{1,0:T(8,128)(2,1)}, u32[]{:S(2)}) copy-start(bf16[256,6144]{1,0:T(8,128)(2,1)} %copy-done.9) | copy-start | bytes 9437188
  89.2 18.4 %all-to-all-start.3 = ((bf16[64,8,128]{2,1,0:T(8,128)(2,1)}), bf16[64,8,128]{2,1,0:T(8,128)(2,1)S(1)}, u32[]{:S(2)}, u32[]{:S(2)}) async-start(bf16[64,8,128]{2,1,0:T(8,128)(2,1)} %shard_map.152), calls=%async_computation.4 | async-start | bytes 262144 | tf_op jit(solution)/shard_map/all_to_all | solution.py:34
  108.4 15.1 %all-to-all-start.4 = ((bf16[64,8,128]{2,1,0:T(8,128)(2,1)}), bf16[64,8,128]{2,1,0:T(8,128)(2,1)S(1)}, u32[]{:S(2)}, u32[]{:S(2)}) async-start(bf16[64,8,128]{2,1,0:T(8,128)(2,1)} %get-tuple-element.29), calls=%async_computation.5 | async-start | bytes 262144 | tf_op jit(solution)/shard_map/all_to_all | solution.py:34
  123.8 11.0 %copy-start.13 = (f32[16,2]{0,1:T(2,128)S(1)}, f32[16,2]{0,1:T(2,128)}, u32[]{:S(2)}) copy-start(f32[16,2]{0,1:T(2,128)} %param.18) | copy-start | bytes 388
  123.8 11.9 %copy-start.7 = (s32[256]{0:T(256)S(1)}, s32[256]{0:T(256)}, u32[]{:S(2)}) copy-start(s32[256]{0:T(256)} %param.14) | copy-start | bytes 3076
  126.2 26.2 %all-to-all-start.5 = ((bf16[32,22,384]{2,1,0:T(8,128)(2,1)}), bf16[32,22,384]{2,1,0:T(8,128)(2,1)S(1)}, u32[]{:S(2)}, u32[]{:S(2)}) async-start(bf16[32,22,384]{2,1,0:T(8,128)(2,1)} %pad_maximum_fusion), calls=%async_computation.6 | async-start | bytes 1179648 | tf_op jit(solution)/shard_map/all_to_all | solution.py:34
Sparse Core Ops, SparseCore 0:
  34.3 48.0 all-gather.1
Sparse Core Ops, SparseCore 1:
  79.9 42.2 reduce-scatter.1

commit v6 on v5

--- a/solution.py
+++ b/solution.py
@@ -59,44 +59,51 @@
     )(*operands)
 
 
-def route(experts, gates, output_gradient, row_slot, capacity):
-    tokens, columns = output_gradient.shape
-    choices = experts.shape[1]
-
-    def kernel(experts_ref, gates_ref, grad_ref, row_slot_ref, out_ref, target_ref):
+def route(experts, gates, output_gradient, replicas, capacity):
+    choices, tokens = experts.shape
+    columns = output_gradient.shape[1]
+    devices = EXPERT_COUNT * replicas
+
+    def kernel(experts_ref, gates_ref, grad_ref, out_ref, target_ref):
         ids = experts_ref[...]
         gate = gates_ref[...]
-        grad = grad_ref[...].astype(F32)
-        expert = lax.broadcasted_iota(jnp.int32, (tokens, EXPERT_COUNT), 1)
+        expert = lax.broadcasted_iota(jnp.int32, (EXPERT_COUNT, tokens), 0)
         named = [
-            jnp.where(ids[:, k : k + 1] == expert, 1.0, 0.0) for k in range(choices)
+            jnp.where(ids[k : k + 1] == expert, 1.0, 0.0) for k in range(choices)
         ]
         row = lax.broadcasted_iota(jnp.int32, (tokens, tokens), 0)
         col = lax.broadcasted_iota(jnp.int32, (tokens, tokens), 1)
-        lower = jnp.where(row > col, 1.0, 0.0).astype(BF)
-        earlier = dot(lower, sum(named).astype(BF))
-        rows = 0.0
+        upper = jnp.where(row < col, 1.0, 0.0).astype(BF)
+        earlier = dot(sum(named).astype(BF), upper)
+        place = lax.broadcasted_iota(jnp.int32, (devices * TILE, tokens), 0)
+        k_row = place % TILE
+        slot_row = place // (replicas * TILE) * capacity + k_row
+        picked = jnp.zeros((devices * TILE, tokens), F32)
+        weight = jnp.zeros((devices * TILE, tokens), F32)
         targets = []
         for k in range(choices):
-            slot = jnp.sum(earlier * named[k], axis=1, keepdims=True).astype(jnp.int32)
-            target = ids[:, k : k + 1] * capacity + slot
-            match = jnp.where(target == row_slot_ref[...], 1.0, 0.0).astype(BF)
-            weighted = (gate[:, k : k + 1] * grad).astype(BF)
-            rows = rows + dot(match, weighted, ((0,), (0,)))
+            slot = jnp.sum(earlier * named[k], axis=0, keepdims=True).astype(jnp.int32)
+            target = ids[k : k + 1] * capacity + slot
+            match = jnp.where((target == slot_row) & (k_row < capacity), 1.0, 0.0)
+            picked = picked + match
+            weight = weight + match * gate[k : k + 1]
             earlier = earlier + named[k]
             targets.append(target)
-        out_ref[...] = rows.astype(BF)
-        choice = lax.broadcasted_iota(jnp.int32, (tokens, choices), 1)
-        chosen = targets[0]
+        values = dot(picked.astype(BF), grad_ref[...])
+        values = values * jnp.sum(weight, axis=1, keepdims=True)
+        values = values.reshape(devices, TILE, columns)[:, :capacity]
+        out_ref[...] = values.astype(BF)
+        choice = lax.broadcasted_iota(jnp.int32, (choices, tokens), 0)
+        chosen = jnp.broadcast_to(targets[0], (choices, tokens))
         for k in range(1, choices):
             chosen = jnp.where(choice == k, targets[k], chosen)
         target_ref[...] = chosen
 
     out = (
-        jax.ShapeDtypeStruct((row_slot.shape[1], columns), BF),
-        jax.ShapeDtypeStruct((tokens, choices), jnp.int32),
-    )
-    return whole(kernel, out, experts, gates, output_gradient, row_slot)
+        jax.ShapeDtypeStruct((devices, capacity, columns), BF),
+        jax.ShapeDtypeStruct((choices, tokens), jnp.int32),
+    )
+    return whole(kernel, out, experts, gates, output_gradient)
 
 
 def dequantize(codes, scales, depth, columns):
@@ -235,48 +242,91 @@
     return whole(kernel, out, chunks, signs.reshape(1, stride))
 
 
-def backward_chunks(main, adapter_grad, down_map, rotated, spread, scaling):
-    height, stride = main.shape
+def backward_chunks(gathered, weights, down_map, rotated, spread, scaling):
+    height, stride = rotated.shape
+    rank = down_map.shape[1]
+    width = weights.shape[1]
     halves = stride // LANES
     blocks = height // ROWS
     peers = halves * blocks
     rest = height - LANES
-
-    def kernel(main_ref, grad_ref, down_ref, rotated_ref, spread_ref, out_ref):
-        rotated_value = rotated_ref[...]
-        down = down_ref[...]
-        d_rotated = main_ref[...] + dot(grad_ref[...], down, ((1,), (1,)))
-        local = dot(d_rotated.astype(BF), spread_ref[...])
-        local = (local * scaling).astype(BF)
-        product = rotated_value.astype(F32) * d_rotated
-        totals = lax.dot_general(
-            jnp.ones((TILE, stride), F32),
-            product,
-            (((1,), (1,)), ((), ())),
-            precision=HIGH_ACCURACY,
-            preferred_element_type=F32,
-        )
-        adapter = dot(down, rotated_value, ((0,), (1,))).astype(BF)
-        pad = jnp.zeros((peers, LANES - rest), BF)
-        riders = dot(rider_rows(peers, ROWS), adapter[:, :LANES])
-        tail = jnp.concatenate([adapter[:, LANES:], pad], axis=1)
-        riders += dot(rider_rows(peers, ROWS + 1), tail)
-        row_tail = jnp.concatenate(
-            [totals[:, LANES:], jnp.zeros((TILE, LANES - rest), F32)], axis=1
-        )
-        row_tail = pltpu.roll(row_tail, rest, 1)
-        k = lax.broadcasted_iota(jnp.int32, (TILE, LANES), 0)
-        extra = jnp.where(k == ROWS + 2, totals[:, :LANES], 0.0)
-        extra += jnp.where(k == ROWS + 1, row_tail, 0.0)
-        place = placement(blocks, ROWS)
-        for half in range(halves):
-            part = dot(place, local[:, half * LANES : (half + 1) * LANES])
-            part += riders[half * blocks * TILE : (half + 1) * blocks * TILE]
-            part = part.reshape(blocks, TILE, LANES) + extra[None]
-            out_ref[half * blocks : (half + 1) * blocks] = part.astype(BF)
-
-    out = jax.ShapeDtypeStruct((peers, TILE, LANES), BF)
-    return whole(kernel, out, main, adapter_grad, down_map, rotated, spread)
+    steps = 4
+    block = width // steps
+
+    def kernel(
+        gathered_ref, weights_ref, down_ref, rotated_ref, spread_ref, out_ref, grad_ref, acc, small
+    ):
+        @pl.when(pl.program_id(0) == 0)
+        def _():
+            acc[...] = jnp.zeros_like(acc)
+            small[...] = jnp.zeros_like(small)
+
+        slots = gathered_ref[:height, :]
+        acc[...] += dot(slots, weights_ref[...], ((1,), (1,)))
+        small[...] += dot(slots, gathered_ref[height:, :], ((1,), (1,)))
+
+        @pl.when(pl.program_id(0) == steps - 1)
+        def _():
+            rotated_value = rotated_ref[...]
+            down = down_ref[...]
+            adapter_grad = (LOWRANK_SCALE * small[...]).astype(BF)
+            grad_ref[...] = adapter_grad
+            d_rotated = acc[...] + dot(adapter_grad, down, ((1,), (1,)))
+            local = dot(d_rotated.astype(BF), spread_ref[...])
+            local = (local * scaling).astype(BF)
+            product = rotated_value.astype(F32) * d_rotated
+            totals = lax.dot_general(
+                jnp.ones((TILE, stride), F32),
+                product,
+                (((1,), (1,)), ((), ())),
+                precision=HIGH_ACCURACY,
+                preferred_element_type=F32,
+            )
+            adapter = dot(down, rotated_value, ((0,), (1,))).astype(BF)
+            pad = jnp.zeros((peers, LANES - rest), BF)
+            riders = dot(rider_rows(peers, ROWS), adapter[:, :LANES])
+            tail = jnp.concatenate([adapter[:, LANES:], pad], axis=1)
+            riders += dot(rider_rows(peers, ROWS + 1), tail)
+            row_tail = jnp.concatenate(
+                [totals[:, LANES:], jnp.zeros((TILE, LANES - rest), F32)], axis=1
+            )
+            row_tail = pltpu.roll(row_tail, rest, 1)
+            k = lax.broadcasted_iota(jnp.int32, (TILE, LANES), 0)
+            extra = jnp.where(k == ROWS + 2, totals[:, :LANES], 0.0)
+            extra += jnp.where(k == ROWS + 1, row_tail, 0.0)
+            place = placement(blocks, ROWS)
+            for half in range(halves):
+                part = dot(place, local[:, half * LANES : (half + 1) * LANES])
+                part += riders[half * blocks * TILE : (half + 1) * blocks * TILE]
+                part = part.reshape(blocks, TILE, LANES) + extra[None]
+                out_ref[half * blocks : (half + 1) * blocks] = part.astype(BF)
+
+    def fixed(shape):
+        return pl.BlockSpec(shape, lambda i: (0,) * len(shape))
+
+    return pl.pallas_call(
+        kernel,
+        grid=(steps,),
+        in_specs=[
+            pl.BlockSpec((height + rank, block), lambda i: (0, i)),
+            pl.BlockSpec((stride, block), lambda i: (0, i)),
+            fixed(down_map.shape),
+            fixed(rotated.shape),
+            fixed(spread.shape),
+        ],
+        out_specs=(fixed((peers, TILE, LANES)), fixed((height, rank))),
+        out_shape=(
+            jax.ShapeDtypeStruct((peers, TILE, LANES), BF),
+            jax.ShapeDtypeStruct((height, rank), BF),
+        ),
+        scratch_shapes=[pltpu.VMEM((height, stride), F32), pltpu.VMEM((height, rank), F32)],
+        cost_estimate=pl.CostEstimate(
+            flops=2 * height * stride * width,
+            bytes_accessed=2 * width * (stride + height + rank),
+            transcendentals=0,
+        ),
+        compiler_params=pltpu.CompilerParams(vmem_limit_bytes=32 * 1024 * 1024),
+    )(gathered, weights, down_map, rotated, spread)
 
 
 def split(values):
@@ -298,13 +348,10 @@
     columns = output_gradient.shape[1]
     scaling = 1.0 / math.sqrt(HIDDEN_UNITS)
 
-    row = np.arange(devices * capacity)
-    row_slot = row // (replicas * capacity) * capacity + row % capacity
-    row_slot = jnp.asarray(row_slot[None], jnp.int32)
-    outgoing, target = route(experts, gates, output_gradient, row_slot, capacity)
-    target = target.reshape(tokens_here * 2)
+    outgoing, target = route(experts.T, gates.T, output_gradient, replicas, capacity)
+    target = target.T.reshape(tokens_here * 2)
     weights, own, other = dequantize(codes, scales, depth, columns)
-    d_rows = exchange(outgoing, EXPERT)
+    d_rows = exchange(outgoing, EXPERT).reshape(slot_rows, columns)
     chunks = to_chunks(hidden, signs)
     d_rows, weights, own, other, chunks = lax.optimization_barrier(
         (d_rows, weights, own, other, chunks)
@@ -323,17 +370,11 @@
     pair = pair_products(rotated, neighbour, own, other)
     frozen = lax.psum_scatter(pair, "z", scatter_dimension=0, tiled=False)
 
-    d_full = gathered[:slot_rows]
-    lowrank_full = gathered[slot_rows:]
-    adapter_grad = LOWRANK_SCALE * lax.dot_general(
-        d_full, lowrank_full, (((1,), (1,)), ((), ())), preferred_element_type=F32
-    )
-    adapter_grad = adapter_grad.astype(BF)
-    main = dot(d_full, weights, ((1,), (1,)))
+    d_chunks, adapter_grad = backward_chunks(
+        gathered, weights, lowrank_down_map, rotated, spread_local, scaling
+    )
     down_map_gradient = dot(rotated, adapter_grad, ((0,), (0,)))
-    d_chunks = exchange(
-        backward_chunks(main, adapter_grad, lowrank_down_map, rotated, spread_local, scaling), SLAB
-    )
+    d_chunks = exchange(d_chunks, SLAB)
     d_mixed, sums = mix_blocks(d_chunks)
     rest = slot_rows - LANES
     row_total = jnp.concatenate([sums[ROWS + 2], sums[ROWS + 1, rest : 2 * rest]])

time: 164 us -> 169 us (1.030)
  local copies, waits for them, and re-layouts: 13.4 us -> 23.4 us
  matrix products: 7.21 us -> 2.74 us
  waiting for transfers between devices: 39.5 us -> 37 us
  Pallas kernels: 8.83 us -> 11.2 us
    unnamed x35 -> x56, local copies, waits for them, and re-layouts: 11.8 us -> 20.3 us
    pallas_call x0 -> x1, Pallas kernels: none -> 3.26 us  [backward_chunks(): pl.pallas_call(kernel, grid=(steps,), in_specs=[pl.BlockSpec((height + ra...]
    dot_general x2 -> x1, matrix products: 3.57 us -> 0.83 us  [dot(): lax.dot_general(left, right, (dims, ((), ())), preferred_element_type=F32)]
    dot_general x1 -> x0, matrix products: 2.53 us -> none  [body(): lax.dot_general(d_full, lowrank_full, (((1,), (1,)), ((), ())), preferred...]
    all_gather x1, waiting for transfers between devices: 1.71 us -> 0.01 us  [body(): lax.all_gather(jnp.concatenate([d_rows, lowrank_local], axis=0), TENSOR,...]
    pallas_call x7 -> x6, Pallas kernels: 4.8 us -> 3.86 us  [whole(): pl.pallas_call(kernel, out_shape=out_shape, compiler_params=pltpu.Compile...]
  transfers between devices with their start and end apart: 8 -> 8, of which waited for: 6 -> 5; matrix products, arithmetic and copies ran while one was open for 4% -> 3% of each run, Pallas kernels for 5% -> 6%
where the time goes in v6:
time: 169 us; the launch traced here: 168 us
  blocking collectives  37.3 us (22%)
  waiting for transfers between devices  37 us (22%)
  starting transfers between devices  35.8 us (21%)
  local copies, waits for them, and re-layouts  23.4 us (14%)
  between operations  15.8 us (9%)
  Pallas kernels  11.2 us (7%)
  other arithmetic  5.13 us (3%)
  matrix products  2.74 us (2%)
    all_to_all x2, blocking collectives, exchange(): return lax.all_to_all(value, axes, split_axis=0, concat_axis=0, tiled=True)  37.3 us
    all_to_all x4, waiting for transfers between devices, exchange(): return lax.all_to_all(value, axes, split_axis=0, concat_axis=0, tiled=True)  35.8 us
    all_to_all x4, starting transfers between devices, exchange(): return lax.all_to_all(value, axes, split_axis=0, concat_axis=0, tiled=True)  31.7 us
    unnamed x56, local copies, waits for them, and re-layouts  20.3 us
    pallas_call x6, Pallas kernels, whole(): pl.pallas_call(kernel, out_shape=out_shape, compiler_params=pltpu.Compile...  3.86 us
  transfers between devices with their start and end apart: 8, of which 5 were waited for; matrix products, arithmetic and copies ran while one was open for 3% of the time, Pallas kernels for 6%

profile of v6, /device:TPU:8, one launch (start us, length us, event | category | flops | bytes accessed | tf_op | source)
XLA Modules:
  0.0 168.3 jit_solution(14362651780373643282)
XLA Ops:
  11.1 10.2 %all-to-all-start = ((bf16[32,5,384]{2,1,0:T(8,128)(2,1)}), bf16[32,5,384]{2,1,0:T(8,128)(2,1)}, u32[]{:S(2)}, u32[]{:S(2)}) async-start(bf16[32,5,384]{2,1,0:T(8,128)(2,1)} %get-tuple-element.21), calls=%async_computation | async-start | bytes 393216 | tf_op jit(solution)/shard_map/all_to_all | solution.py:34
  23.9 1.9 %copy-done.1 = bf16[256,6144]{1,0:T(8,128)(2,1)S(1)} copy-done((bf16[256,6144]{1,0:T(8,128)(2,1)S(1)}, bf16[256,6144]{1,0:T(8,128)(2,1)}, u32[]{:S(2)}) %copy-start.1) | copy-done | bytes 3145752
  26.6 1.4 shard_map.138
  28.1 1.1 copy-done.3
  29.2 1.2 copy-done.23
  31.0 1.4 all-to-all-done
  32.4 1.6 reshape.58
  34.0 1.6 pad_maximum_fusion.1
  35.7 1.9 %collective-permute-start.1 = (bf16[8,256,384]{2,1,0:T(8,128)(2,1)}, bf16[8,256,384]{2,1,0:T(8,128)(2,1)S(1)}, u32[]{:S(2)}, u32[]{:S(2)}) collective-permute-start(bf16[8,256,384]{2,1,0:T(8,128)(2,1)} %copy-done.23), channel_id=1, source_target_pairs={{0,1},{1,0},{2,3},{3,2},{4,5},{5,4},{6,7},{7,6},{8,9},{9,8},{10,11... | collective-permute-start | bytes 4718600 | tf_op jit(solution)/shard_map/ppermute | solution.py:368
  37.7 22.4 %all_to_all.30.chunks_ref = bf16[64,8,128]{2,1,0:T(8,128)(2,1)S(1)} all-to-all(bf16[64,8,128]{2,1,0:T(8,128)(2,1)} %copy-done.10), channel_id=1, replica_groups=mesh['e'=8,'r'=4,'z'=8,'c'=2] {'r','z','c'}, dimensions={0} | all-to-all | bytes 262144 | tf_op jit(solution)/shard_map/all_to_all | solution.py:34
  60.7 14.8 %all_to_all.31.chunks_ref = bf16[64,8,128]{2,1,0:T(8,128)(2,1)S(1)} all-to-all(bf16[64,8,128]{2,1,0:T(8,128)(2,1)S(1)} %get-tuple-element.26), channel_id=1, replica_groups=mesh['e'=8,'r'=4,'z'=8,'c'=2] {'r','z','c'}, dimensions={0} | all-to-all | bytes 262144 | tf_op jit(solution)/shard_map/all_to_all | solution.py:34
  76.8 2.0 %collective-permute-start = (bf16[160,256]{1,0:T(8,128)(2,1)S(1)}, bf16[160,256]{1,0:T(8,128)(2,1)S(1)}, u32[]{:S(2)}, u32[]{:S(2)}) collective-permute-start(bf16[160,256]{1,0:T(8,128)(2,1)S(1)} %shard_map.141.rotated_ref), channel_id=1, source_target_pairs={{0,1},{1,0},{2,3},{3,2},{4,5},{5,4},{6,7},{7,6},{8,9},{9,8},{10,11... | collective-permute-start | bytes 245768 | tf_op jit(solution)/shard_map/ppermute | solution.py:369
  78.9 1.1 collective-permute-done.neighbour_ref
  80.0 1.4 copy-done.4
  81.4 2.6 %shard_map.142 = f32[8,160,384]{2,1,0:T(8,128)} custom-call(bf16[160,256]{1,0:T(8,128)(2,1)S(1)} %shard_map.141.rotated_ref, bf16[160,256]{1,0:T(8,128)(2,1)S(1)} %collective-permute-done.neighbour_ref, bf16[8,256,384]{2,1,0:T(8,128)(2,1)S(1)} %copy-done.4, bf16[8,256,384]{2,1,0:T(8,128)(2,1)S(1)} %collective-permute-done.1.other_ref), custom_call_target="tpu_custom_call" | custom-call | flops 503316480 | bytes 5111808 | tf_op jit(solution)/shard_map/pallas_call | solution.py:154
  84.7 1.5 copy.53.down_ref
  86.2 1.8 %copy-done.2 = bf16[224,6144]{1,0:T(8,128)(2,1)S(1)} copy-done((bf16[224,6144]{1,0:T(8,128)(2,1)S(1)}, bf16[224,6144]{1,0:T(8,128)(2,1)}, u32[]{:S(2)}) %copy-start.2) | copy-done | bytes 2752536
  90.6 3.3 %shard_map.143 = (bf16[64,8,128]{2,1,0:T(8,128)(2,1)S(1)}, bf16[160,64]{1,0:T(8,128)(2,1)S(1)}) custom-call(bf16[224,6144]{1,0:T(8,128)(2,1)S(1)} %copy-done.2, bf16[256,6144]{1,0:T(8,128)(2,1)S(1)} %get-tuple-element.30.weights_ref, bf16[256,64]{1,0:T(8,128)(2,1)S(1)} %copy-done.11, bf16[160,256]{1,0:T(8,128)(2,1)S(1)} %copy-done.6, ...), custom_call_target="tpu_custom_call" | custom-call | flops 503316480 | bytes 5898240 | tf_op jit(solution)/shard_map/pallas_call | solution.py:307
  95.1 7.2 %all-to-all-start.3 = ((bf16[64,8,128]{2,1,0:T(8,128)(2,1)}), bf16[64,8,128]{2,1,0:T(8,128)(2,1)S(1)}, u32[]{:S(2)}, u32[]{:S(2)}) async-start(bf16[64,8,128]{2,1,0:T(8,128)(2,1)} %copy-done.12), calls=%async_computation.4 | async-start | bytes 262144 | tf_op jit(solution)/shard_map/all_to_all | solution.py:34
  102.3 9.5 %all-to-all-done.3.chunks_ref = bf16[64,8,128]{2,1,0:T(8,128)(2,1)S(1)} async-done(((bf16[64,8,128]{2,1,0:T(8,128)(2,1)}), bf16[64,8,128]{2,1,0:T(8,128)(2,1)S(1)}, u32[]{:S(2)}, u32[]{:S(2)}) %all-to-all-start.3) | async-done | bytes 131104 | tf_op jit(solution)/shard_map/all_to_all | solution.py:34
  112.6 5.6 %all-to-all-start.4 = ((bf16[64,8,128]{2,1,0:T(8,128)(2,1)}), bf16[64,8,128]{2,1,0:T(8,128)(2,1)S(1)}, u32[]{:S(2)}, u32[]{:S(2)}) async-start(bf16[64,8,128]{2,1,0:T(8,128)(2,1)} %get-tuple-element.32), calls=%async_computation.5 | async-start | bytes 262144 | tf_op jit(solution)/shard_map/all_to_all | solution.py:34
  118.5 9.2 %all-to-all-done.4.chunks_ref = bf16[64,8,128]{2,1,0:T(8,128)(2,1)S(1)} async-done(((bf16[64,8,128]{2,1,0:T(8,128)(2,1)}), bf16[64,8,128]{2,1,0:T(8,128)(2,1)S(1)}, u32[]{:S(2)}, u32[]{:S(2)}) %all-to-all-start.4) | async-done | bytes 131104 | tf_op jit(solution)/shard_map/all_to_all | solution.py:34
  131.2 8.8 %all-to-all-start.5 = ((bf16[32,22,384]{2,1,0:T(8,128)(2,1)}), bf16[32,22,384]{2,1,0:T(8,128)(2,1)S(1)}, u32[]{:S(2)}, u32[]{:S(2)}) async-start(bf16[32,22,384]{2,1,0:T(8,128)(2,1)} %pad_maximum_fusion), calls=%async_computation.6 | async-start | bytes 1179648 | tf_op jit(solution)/shard_map/all_to_all | solution.py:34
  142.1 15.7 %all-to-all-done.5 = bf16[32,22,384]{2,1,0:T(8,128)(2,1)S(1)} async-done(((bf16[32,22,384]{2,1,0:T(8,128)(2,1)}), bf16[32,22,384]{2,1,0:T(8,128)(2,1)S(1)}, u32[]{:S(2)}, u32[]{:S(2)}) %all-to-all-start.5) | async-done | bytes 540704 | tf_op jit(solution)/shard_map/all_to_all | solution.py:34
  (95 shorter events, 23.2 us)
Async XLA Ops:
  8.0 22.4 %copy-start = (bf16[8,64,384]{2,1,0:T(8,128)(2,1)S(1)}, bf16[8,64,384]{2,1,0:T(8,128)(2,1)}, u32[]{:S(2)}) copy-start(bf16[8,64,384]{2,1,0:T(8,128)(2,1)} %param.15) | copy-start | bytes 1179652
  11.1 21.3 %all-to-all-start = ((bf16[32,5,384]{2,1,0:T(8,128)(2,1)}), bf16[32,5,384]{2,1,0:T(8,128)(2,1)}, u32[]{:S(2)}, u32[]{:S(2)}) async-start(bf16[32,5,384]{2,1,0:T(8,128)(2,1)} %get-tuple-element.21), calls=%async_computation | async-start | bytes 393216 | tf_op jit(solution)/shard_map/all_to_all | solution.py:34
  21.4 64.8 %all-gather.2.cloned.1.call-start = ((), (), s32[]{:S(2)}) async-start(), calls=%async_computation.8 | async-start | bytes 2924544 | tf_op jit(solution)/shard_map/all_gather | solution.py:360
  21.4 0.9 copy-start.14
  23.8 1.9 %copy-start.1 = (bf16[256,6144]{1,0:T(8,128)(2,1)S(1)}, bf16[256,6144]{1,0:T(8,128)(2,1)}, u32[]{:S(2)}) copy-start(bf16[256,6144]{1,0:T(8,128)(2,1)} %codes_ref.1) | copy-start | bytes 9437188
  25.7 0.9 copy-start.13
  28.1 1.1 copy-start.3
  29.2 1.2 copy-start.23
  35.7 93.1 %reduce-scatter.2.cloned.1.call-start = ((), (), s32[]{:S(2)}) async-start(), calls=%async_computation.7 | async-start | bytes 2211840 | tf_op jit(solution)/shard_map/reduce_scatter | solution.py:371
  35.7 44.3 %collective-permute-start.1 = (bf16[8,256,384]{2,1,0:T(8,128)(2,1)}, bf16[8,256,384]{2,1,0:T(8,128)(2,1)S(1)}, u32[]{:S(2)}, u32[]{:S(2)}) collective-permute-start(bf16[8,256,384]{2,1,0:T(8,128)(2,1)} %copy-done.23), channel_id=1, source_target_pairs={{0,1},{1,0},{2,3},{3,2},{4,5},{5,4},{6,7},{7,6},{8,9},{9,8},{10,11... | collective-permute-start | bytes 4718600 | tf_op jit(solution)/shard_map/ppermute | solution.py:368
  75.5 0.9 copy-start.8
  76.8 3.2 %collective-permute-start = (bf16[160,256]{1,0:T(8,128)(2,1)S(1)}, bf16[160,256]{1,0:T(8,128)(2,1)S(1)}, u32[]{:S(2)}, u32[]{:S(2)}) collective-permute-start(bf16[160,256]{1,0:T(8,128)(2,1)S(1)} %shard_map.141.rotated_ref), channel_id=1, source_target_pairs={{0,1},{1,0},{2,3},{3,2},{4,5},{5,4},{6,7},{7,6},{8,9},{9,8},{10,11... | collective-permute-start | bytes 245768 | tf_op jit(solution)/shard_map/ppermute | solution.py:369
  80.0 1.4 copy-start.4
  86.2 1.8 %copy-start.2 = (bf16[224,6144]{1,0:T(8,128)(2,1)S(1)}, bf16[224,6144]{1,0:T(8,128)(2,1)}, u32[]{:S(2)}) copy-start(bf16[224,6144]{1,0:T(8,128)(2,1)} %all-gather.2.cloned.1.call-done.gathered_ref) | copy-start | bytes 8257540
  87.9 0.9 copy-start.6
  88.8 0.9 copy-start.9
  95.1 34.8 %copy-start.24 = (bf16[160,384]{1,0:T(8,128)(2,1)S(1)}, bf16[160,384]{1,0:T(8,128)(2,1)}, u32[]{:S(2)}) copy-start(bf16[160,384]{1,0:T(8,128)(2,1)} %reshape.58) | copy-start | bytes 368644
  95.1 16.7 %all-to-all-start.3 = ((bf16[64,8,128]{2,1,0:T(8,128)(2,1)}), bf16[64,8,128]{2,1,0:T(8,128)(2,1)S(1)}, u32[]{:S(2)}, u32[]{:S(2)}) async-start(bf16[64,8,128]{2,1,0:T(8,128)(2,1)} %copy-done.12), calls=%async_computation.4 | async-start | bytes 262144 | tf_op jit(solution)/shard_map/all_to_all | solution.py:34
  112.6 15.1 %all-to-all-start.4 = ((bf16[64,8,128]{2,1,0:T(8,128)(2,1)}), bf16[64,8,128]{2,1,0:T(8,128)(2,1)S(1)}, u32[]{:S(2)}, u32[]{:S(2)}) async-start(bf16[64,8,128]{2,1,0:T(8,128)(2,1)} %get-tuple-element.32), calls=%async_computation.5 | async-start | bytes 262144 | tf_op jit(solution)/shard_map/all_to_all | solution.py:34
  129.8 10.2 %copy-start.19 = (f32[16,2]{0,1:T(2,128)S(1)}, f32[16,2]{0,1:T(2,128)}, u32[]{:S(2)}) copy-start(f32[16,2]{0,1:T(2,128)} %param.17) | copy-start | bytes 388
  129.9 10.5 %copy-start.7 = (bf16[160,256]{1,0:T(8,128)(2,1)S(1)}, bf16[160,256]{1,0:T(8,128)(2,1)}, u32[]{:S(2)}) copy-start(bf16[160,256]{1,0:T(8,128)(2,1)} %copy-done.5) | copy-start | bytes 245764
  129.9 10.5 %copy-start.16 = (bf16[160,64]{1,0:T(8,128)(2,1)S(1)}, bf16[160,64]{1,0:T(8,128)(2,1)}, u32[]{:S(2)}) copy-start(bf16[160,64]{1,0:T(8,128)(2,1)} %copy-done.15) | copy-start | bytes 61444
  129.9 11.3 %copy-start.21 = (s32[256]{0:T(256)S(1)}, s32[256]{0:T(256)}, u32[]{:S(2)}) copy-start(s32[256]{0:T(256)} %param.13) | copy-start | bytes 3076
  131.2 26.6 %all-to-all-start.5 = ((bf16[32,22,384]{2,1,0:T(8,128)(2,1)}), bf16[32,22,384]{2,1,0:T(8,128)(2,1)S(1)}, u32[]{:S(2)}, u32[]{:S(2)}) async-start(bf16[32,22,384]{2,1,0:T(8,128)(2,1)} %pad_maximum_fusion), calls=%async_computation.6 | async-start | bytes 1179648 | tf_op jit(solution)/shard_map/all_to_all | solution.py:34
  (9 other events, 6.2 us)
Sparse Core Ops, SparseCore 0:
  35.8 48.4 all-gather.1
Sparse Core Ops, SparseCore 1:
  84.7 43.4 reduce-scatter.1

commit v7 on v5

--- a/solution.py
+++ b/solution.py
@@ -59,44 +59,134 @@
     )(*operands)
 
 
-def route(experts, gates, output_gradient, row_slot, capacity):
-    tokens, columns = output_gradient.shape
-    choices = experts.shape[1]
-
-    def kernel(experts_ref, gates_ref, grad_ref, row_slot_ref, out_ref, target_ref):
+def route(experts, gates, output_gradient, replicas, capacity):
+    choices, tokens = experts.shape
+    columns = output_gradient.shape[1]
+    rows = EXPERT_COUNT * replicas * capacity
+
+    def kernel(experts_ref, gates_ref, grad_ref, out_ref, target_ref):
         ids = experts_ref[...]
         gate = gates_ref[...]
-        grad = grad_ref[...].astype(F32)
-        expert = lax.broadcasted_iota(jnp.int32, (tokens, EXPERT_COUNT), 1)
+        expert = lax.broadcasted_iota(jnp.int32, (EXPERT_COUNT, tokens), 0)
         named = [
-            jnp.where(ids[:, k : k + 1] == expert, 1.0, 0.0) for k in range(choices)
+            jnp.where(ids[k : k + 1] == expert, 1.0, 0.0) for k in range(choices)
         ]
         row = lax.broadcasted_iota(jnp.int32, (tokens, tokens), 0)
         col = lax.broadcasted_iota(jnp.int32, (tokens, tokens), 1)
-        lower = jnp.where(row > col, 1.0, 0.0).astype(BF)
-        earlier = dot(lower, sum(named).astype(BF))
-        rows = 0.0
+        upper = jnp.where(row < col, 1.0, 0.0).astype(BF)
+        earlier = dot(sum(named).astype(BF), upper)
+        place = lax.broadcasted_iota(jnp.int32, (rows, tokens), 0).astype(F32)
+        block = jnp.floor((place + 0.5) * (1.0 / capacity))
+        owner = jnp.floor((place + 0.5) * (1.0 / (replicas * capacity)))
+        slot_row = (place + capacity * (owner - block)).astype(jnp.int32)
+        picked = jnp.zeros((rows, tokens), F32)
+        weight = jnp.zeros((rows, tokens), F32)
         targets = []
         for k in range(choices):
-            slot = jnp.sum(earlier * named[k], axis=1, keepdims=True).astype(jnp.int32)
-            target = ids[:, k : k + 1] * capacity + slot
-            match = jnp.where(target == row_slot_ref[...], 1.0, 0.0).astype(BF)
-            weighted = (gate[:, k : k + 1] * grad).astype(BF)
-            rows = rows + dot(match, weighted, ((0,), (0,)))
+            slot = jnp.sum(earlier * named[k], axis=0, keepdims=True).astype(jnp.int32)
+            target = ids[k : k + 1] * capacity + slot
+            match = jnp.where(target == slot_row, 1.0, 0.0)
+            picked = picked + match
+            weight = weight + match * gate[k : k + 1]
             earlier = earlier + named[k]
             targets.append(target)
-        out_ref[...] = rows.astype(BF)
-        choice = lax.broadcasted_iota(jnp.int32, (tokens, choices), 1)
-        chosen = targets[0]
+        values = dot(picked.astype(BF), grad_ref[...])
+        out_ref[...] = (values * jnp.sum(weight, axis=1, keepdims=True)).astype(BF)
+        choice = lax.broadcasted_iota(jnp.int32, (choices, tokens), 0)
+        chosen = jnp.broadcast_to(targets[0], (choices, tokens))
         for k in range(1, choices):
             chosen = jnp.where(choice == k, targets[k], chosen)
         target_ref[...] = chosen
 
     out = (
-        jax.ShapeDtypeStruct((row_slot.shape[1], columns), BF),
-        jax.ShapeDtypeStruct((tokens, choices), jnp.int32),
-    )
-    return whole(kernel, out, experts, gates, output_gradient, row_slot)
+        jax.ShapeDtypeStruct((rows, columns), BF),
+        jax.ShapeDtypeStruct((choices, tokens), jnp.int32),
+    )
+    return whole(kernel, out, experts, gates, output_gradient)
+
+
+def build_parcel(frozen, d_mixed, up_map, d_rows, totals):
+    height, columns = frozen.shape
+    devices = totals.shape[0]
+    rank = up_map.shape[0]
+    peers = d_mixed.shape[0]
+    rest = height - LANES
+
+    def kernel(frozen_ref, mixed_ref, up_ref, rows_ref, totals_ref, out_ref):
+        flat = mixed_ref[...].reshape(peers * TILE, LANES)
+        first = dot(rider_rows(peers, ROWS), flat, ((0,), (0,)))
+        second = dot(rider_rows(peers, ROWS + 1), flat, ((0,), (0,)))
+        adapter = jnp.concatenate([first, second[:, :rest]], axis=1).astype(BF)
+        replicas = devices // EXPERT_COUNT
+        share = rank // replicas
+        slots = frozen_ref[...] + (LOWRANK_SCALE / replicas) * dot(
+            adapter, up_ref[...], ((0,), (0,))
+        )
+        row = lax.broadcasted_iota(jnp.int32, (share, rank), 0)
+        col = lax.broadcasted_iota(jnp.int32, (share, rank), 1)
+        chosen = jnp.where(col == row + lax.axis_index("r") * share, 1.0, 0.0).astype(BF)
+        part = dot(chosen, adapter).astype(BF)
+        up = (LOWRANK_SCALE * dot(part, rows_ref[...])).astype(BF)
+        out_ref[:, :share, :] = jnp.broadcast_to(up[None], (devices, share, columns))
+        rows = dot(placement(devices, ROWS), slots.astype(BF))
+        rows += dot(rider_rows(devices, ROWS), totals_ref[...])
+        rows = rows.reshape(devices, TILE, columns)[:, : ROWS + 1]
+        out_ref[:, share:, :] = rows.astype(BF)
+
+    share = rank * EXPERT_COUNT // devices
+    out = jax.ShapeDtypeStruct((devices, share + ROWS + 1, columns), BF)
+    return whole(kernel, out, frozen, d_mixed, up_map, d_rows, totals)
+
+
+def open_parcel(parcel, experts, gates, target, rank):
+    devices, height, columns = parcel.shape
+    choices, tokens = experts.shape
+    replicas = devices // EXPERT_COUNT
+    share = rank // replicas
+
+    def kernel(parcel_ref, experts_ref, gates_ref, target_ref, mixed_ref, up_ref, grad_ref):
+        values = parcel_ref[...].astype(F32)
+        up_ref[...] = values[:, :share].reshape(EXPERT_COUNT, rank, columns)
+        rest = values[:, share:].reshape(EXPERT_COUNT, replicas, ROWS + 1, columns).sum(axis=1)
+        gate = gates_ref[...]
+        target = target_ref[...]
+        slot = target - experts_ref[...] * ROWS
+        c = lax.broadcasted_iota(jnp.int32, (ROWS + 1, tokens), 0)
+        mixed = jnp.zeros((tokens, columns), F32)
+        for e in range(EXPERT_COUNT):
+            mixer = jnp.zeros((ROWS + 1, tokens), F32)
+            for k in range(choices):
+                hit = (target[k : k + 1] == e * ROWS + c) & (c < ROWS)
+                mixer = mixer + jnp.where(hit, gate[k : k + 1], 0.0)
+            mixed = mixed + lax.dot_general(
+                mixer,
+                rest[e],
+                (((0,), (0,)), ((), ())),
+                precision=HIGH_ACCURACY,
+                preferred_element_type=F32,
+            )
+        mixed_ref[...] = mixed.astype(BF)
+        totals = jnp.concatenate(
+            [rest[e, ROWS : ROWS + 1, :LANES] for e in range(EXPERT_COUNT)], axis=0
+        )
+        totals = (totals * (1.0 / replicas)).astype(BF)
+        expert = lax.broadcasted_iota(jnp.int32, (EXPERT_COUNT, tokens), 0)
+        lane = lax.broadcasted_iota(jnp.int32, (LANES, tokens), 0)
+        grads = []
+        for k in range(choices):
+            named = jnp.where(experts_ref[k : k + 1, :] == expert, 1.0, 0.0).astype(BF)
+            by_lane = dot(totals, named, ((0,), (0,)))
+            at = slot[k : k + 1]
+            hit = (lane == at) | (lane == at + ROWS)
+            grads.append(jnp.sum(jnp.where(hit, by_lane, 0.0), axis=0, keepdims=True))
+        grad_ref[...] = jnp.concatenate(grads, axis=0) / gate
+
+    out = (
+        jax.ShapeDtypeStruct((tokens, columns), BF),
+        jax.ShapeDtypeStruct((EXPERT_COUNT, rank, columns), F32),
+        jax.ShapeDtypeStruct((choices, tokens), F32),
+    )
+    return whole(kernel, out, parcel, experts, gates, target)
 
 
 def dequantize(codes, scales, depth, columns):
@@ -292,17 +382,11 @@
     devices = EXPERT_COUNT * replicas
     rank = lowrank_down_map.shape[1]
     expert_position = lax.axis_index("e")
-    replica = lax.axis_index("r")
     capacity = slot_rows // devices
-    tokens_here = experts.shape[0]
     columns = output_gradient.shape[1]
     scaling = 1.0 / math.sqrt(HIDDEN_UNITS)
 
-    row = np.arange(devices * capacity)
-    row_slot = row // (replicas * capacity) * capacity + row % capacity
-    row_slot = jnp.asarray(row_slot[None], jnp.int32)
-    outgoing, target = route(experts, gates, output_gradient, row_slot, capacity)
-    target = target.reshape(tokens_here * 2)
+    outgoing, target = route(experts.T, gates.T, output_gradient, replicas, capacity)
     weights, own, other = dequantize(codes, scales, depth, columns)
     d_rows = exchange(outgoing, EXPERT)
     chunks = to_chunks(hidden, signs)
@@ -339,48 +423,16 @@
     row_total = jnp.concatenate([sums[ROWS + 2], sums[ROWS + 1, rest : 2 * rest]])
     d_mixed = exchange(d_mixed, SLAB)
     hidden_gradient = finish_gradient(d_mixed, signs)
-    adapter_in = jnp.concatenate([d_mixed[:, ROWS], d_mixed[:, ROWS + 1, :rest]], axis=1)
-
-    slot_output = frozen + (LOWRANK_SCALE / replicas) * lax.dot_general(
-        adapter_in, lowrank_local, (((0,), (0,)), ((), ())), preferred_element_type=F32
-    )
-    share = rank // replicas
-    adapter_share = lax.dynamic_slice_in_dim(adapter_in, replica * share, share, 0)
-    up_share = LOWRANK_SCALE * jnp.dot(adapter_share, d_rows, preferred_element_type=F32)
+
     totals = jnp.concatenate(
         [part.astype(BF).reshape(devices, capacity) for part in split(row_total)], axis=1
     )
-    totals = jnp.pad(totals, ((0, 0), (0, columns - 2 * capacity)))[:, None, :]
-    parcel = jnp.concatenate(
-        [
-            slot_output.astype(BF).reshape(devices, capacity, columns),
-            totals,
-            jnp.broadcast_to(up_share.astype(BF)[None], (devices, share, columns)),
-        ],
-        axis=1,
-    )
-    parcel = exchange(parcel, EXPERT)
-    up_map_gradient = (
-        parcel[:, capacity + 1 :].astype(F32).reshape(EXPERT_COUNT, rank, columns)
-    )
-    summed = (
-        parcel[:, :capacity]
-        .astype(F32)
-        .reshape(EXPERT_COUNT, replicas, capacity, columns)
-        .sum(axis=1)
-        .reshape(EXPERT_COUNT * capacity, columns)
-    )
-    totals = parcel.reshape(EXPERT_COUNT, replicas, capacity + 1 + share, columns)[:, 0, capacity]
-    totals = totals[:, : 2 * capacity].astype(F32)
-    totals = (totals[:, :capacity] + totals[:, capacity:]).reshape(EXPERT_COUNT * capacity)
-    slot_id = jnp.arange(EXPERT_COUNT * capacity, dtype=jnp.int32)
-    chosen = target[:, None] == slot_id[None, :]
-    gates_gradient = jnp.sum(jnp.where(chosen, totals[None, :], 0.0), axis=1)
-    gates_gradient = gates_gradient.reshape(tokens_here, 2) / gates
-    chosen = chosen.reshape(tokens_here, 2, EXPERT_COUNT * capacity)
-    mixer = jnp.sum(jnp.where(chosen, gates[:, :, None], 0.0), axis=1)
-    mixed = jnp.dot(mixer, summed, precision=HIGH_ACCURACY).astype(BF)
-    return (mixed, hidden_gradient, down_map_gradient, up_map_gradient, gates_gradient)
+    totals = jnp.pad(totals, ((0, 0), (0, columns - 2 * capacity)))
+    parcel = exchange(build_parcel(frozen, d_mixed, lowrank_local, d_rows, totals), EXPERT)
+    mixed, up_map_gradient, gates_gradient = open_parcel(
+        parcel, experts.T, gates.T, target, rank
+    )
+    return (mixed, hidden_gradient, down_map_gradient, up_map_gradient, gates_gradient.T)
 
 
 def solution(mesh):

time: 164 us -> 160 us (0.976)
  blocking collectives: 36.9 us -> 55.1 us
  waiting for transfers between devices: 39.5 us -> 30 us
  starting transfers between devices: 37 us -> 29.4 us
  other arithmetic: 4.21 us -> 0.78 us
  Pallas kernels: 8.83 us -> 10.9 us
  local copies, waits for them, and re-layouts: 13.4 us -> 11.5 us
    all_to_all x4 -> x3, waiting for transfers between devices: 36.6 us -> 17.1 us  [exchange(): return lax.all_to_all(value, axes, split_axis=0, concat_axis=0, tiled=True)]
    all_to_all x2 -> x3, blocking collectives: 36.9 us -> 55.1 us  [exchange(): return lax.all_to_all(value, axes, split_axis=0, concat_axis=0, tiled=True)]
    reduce_scatter x1, waiting for transfers between devices: 0.03 us -> 9.37 us  [body(): frozen = lax.psum_scatter(pair, 'z', scatter_dimension=0, tiled=False)]
    all_to_all x4 -> x3, starting transfers between devices: 33 us -> 25.4 us  [exchange(): return lax.all_to_all(value, axes, split_axis=0, concat_axis=0, tiled=True)]
    pallas_call x7 -> x9, Pallas kernels: 4.8 us -> 6.8 us  [whole(): pl.pallas_call(kernel, out_shape=out_shape, compiler_params=pltpu.Compile...]
  transfers between devices with their start and end apart: 8 -> 7, of which waited for: 6 -> 5; matrix products, arithmetic and copies ran while one was open for 4% -> 4% of each run, Pallas kernels for 5% -> 5%
where the time goes in v7:
time: 160 us; the launch traced here: 159 us
  blocking collectives  55.1 us (34%)
  waiting for transfers between devices  30 us (19%)
  starting transfers between devices  29.4 us (18%)
  between operations  15.7 us (10%)
  local copies, waits for them, and re-layouts  11.5 us (7%)
  Pallas kernels  10.9 us (7%)
  matrix products  6.1 us (4%)
    all_to_all x3, blocking collectives, exchange(): return lax.all_to_all(value, axes, split_axis=0, concat_axis=0, tiled=True)  55.1 us
    all_to_all x3, starting transfers between devices, exchange(): return lax.all_to_all(value, axes, split_axis=0, concat_axis=0, tiled=True)  25.4 us
    all_to_all x3, waiting for transfers between devices, exchange(): return lax.all_to_all(value, axes, split_axis=0, concat_axis=0, tiled=True)  17.1 us
    unnamed x35, local copies, waits for them, and re-layouts  10.5 us
    reduce_scatter x1, waiting for transfers between devices, body(): frozen = lax.psum_scatter(pair, 'z', scatter_dimension=0, tiled=False)  9.37 us
    pallas_call x9, Pallas kernels, whole(): pl.pallas_call(kernel, out_shape=out_shape, compiler_params=pltpu.Compile...  6.8 us
    dot_general x2, matrix products, dot(): lax.dot_general(left, right, (dims, ((), ())), preferred_element_type=F32)  3.57 us
  transfers between devices with their start and end apart: 7, of which 5 were waited for; matrix products, arithmetic and copies ran while one was open for 4% of the time, Pallas kernels for 5%

profile of v7, /device:TPU:8, one launch (start us, length us, event | category | flops | bytes accessed | tf_op | source)
XLA Modules:
  0.0 159.4 jit_solution(13376093933994080510)
XLA Ops:
  11.2 10.3 %all-to-all-start = ((bf16[32,5,384]{2,1,0:T(8,128)(2,1)}), bf16[32,5,384]{2,1,0:T(8,128)(2,1)S(1)}, u32[]{:S(2)}, u32[]{:S(2)}) async-start(bf16[32,5,384]{2,1,0:T(8,128)(2,1)} %all_to_all.23), calls=%async_computation | async-start | bytes 393216 | tf_op jit(solution)/shard_map/all_to_all | solution.py:34
  23.3 1.9 %copy-done.1 = bf16[256,6144]{1,0:T(8,128)(2,1)S(1)} copy-done((bf16[256,6144]{1,0:T(8,128)(2,1)S(1)}, bf16[256,6144]{1,0:T(8,128)(2,1)}, u32[]{:S(2)}) %copy-start.1) | copy-done | bytes 3145752
  26.1 1.4 shard_map.138
  27.6 1.6 %copy-done.13 = bf16[256,6144]{1,0:T(8,128)(2,1)} copy-done((bf16[256,6144]{1,0:T(8,128)(2,1)}, bf16[256,6144]{1,0:T(8,128)(2,1)S(1)}, u32[]{:S(2)}) %copy-start.13) | copy-done | bytes 3145752
  29.2 1.2 copy-done.15
  30.4 2.1 %all-to-all-done = bf16[32,5,384]{2,1,0:T(8,128)(2,1)S(1)} async-done(((bf16[32,5,384]{2,1,0:T(8,128)(2,1)}), bf16[32,5,384]{2,1,0:T(8,128)(2,1)S(1)}, u32[]{:S(2)}, u32[]{:S(2)}) %all-to-all-start) | async-done | bytes 122912 | tf_op jit(solution)/shard_map/all_to_all | solution.py:34
  33.3 1.9 %collective-permute-start.1 = (bf16[8,256,384]{2,1,0:T(8,128)(2,1)}, bf16[8,256,384]{2,1,0:T(8,128)(2,1)S(1)}, u32[]{:S(2)}, u32[]{:S(2)}) collective-permute-start(bf16[8,256,384]{2,1,0:T(8,128)(2,1)} %copy-done.15), channel_id=1, source_target_pairs={{0,1},{1,0},{2,3},{3,2},{4,5},{5,4},{6,7},{7,6},{8,9},{9,8},{10,11... | collective-permute-start | bytes 4718600 | tf_op jit(solution)/shard_map/ppermute | solution.py:405
  35.2 22.0 %all_to_all.37.chunks_ref = bf16[64,8,128]{2,1,0:T(8,128)(2,1)S(1)} all-to-all(bf16[64,8,128]{2,1,0:T(8,128)(2,1)S(1)} %shard_map.139), channel_id=1, replica_groups=mesh['e'=8,'r'=4,'z'=8,'c'=2] {'r','z','c'}, dimensions={0} | all-to-all | bytes 262144 | tf_op jit(solution)/shard_map/all_to_all | solution.py:34
  57.8 14.8 %all_to_all.38.chunks_ref = bf16[64,8,128]{2,1,0:T(8,128)(2,1)S(1)} all-to-all(bf16[64,8,128]{2,1,0:T(8,128)(2,1)S(1)} %get-tuple-element.26), channel_id=1, replica_groups=mesh['e'=8,'r'=4,'z'=8,'c'=2] {'r','z','c'}, dimensions={0} | all-to-all | bytes 262144 | tf_op jit(solution)/shard_map/all_to_all | solution.py:34
  73.1 2.0 %collective-permute-start = (bf16[160,256]{1,0:T(8,128)(2,1)S(1)}, bf16[160,256]{1,0:T(8,128)(2,1)S(1)}, u32[]{:S(2)}, u32[]{:S(2)}) collective-permute-start(bf16[160,256]{1,0:T(8,128)(2,1)S(1)} %shard_map.141.rotated_ref), channel_id=1, source_target_pairs={{0,1},{1,0},{2,3},{3,2},{4,5},{5,4},{6,7},{7,6},{8,9},{9,8},{10,11... | collective-permute-start | bytes 245768 | tf_op jit(solution)/shard_map/ppermute | solution.py:406
  75.1 1.1 collective-permute-done.neighbour_ref
  76.3 2.6 %shard_map.142 = f32[8,160,384]{2,1,0:T(8,128)} custom-call(bf16[160,256]{1,0:T(8,128)(2,1)S(1)} %shard_map.141.rotated_ref, bf16[160,256]{1,0:T(8,128)(2,1)S(1)} %collective-permute-done.neighbour_ref, bf16[8,256,384]{2,1,0:T(8,128)(2,1)S(1)} %get-tuple-element.27.own_ref, bf16[8,256,384]{2,1,0:T(8,128)(2,1)S(1)} %collective-permute-done.1.other_ref), custom_call_target="tpu_custom_call" | custom-call | flops 503316480 | bytes 5111808 | tf_op jit(solution)/shard_map/pallas_call | solution.py:237
  79.0 2.4 %all-gather.2.cloned.1.call-done = bf16[224,6144]{1,0:T(8,128)(2,1)} async-done(((bf16[224,384]{1,0:T(8,128)(2,1)}), bf16[224,6144]{1,0:T(8,128)(2,1)}) %all-gather.2.cloned.1.call-update) | async-done | bytes 2752528 | tf_op jit(solution)/shard_map/all_gather | solution.py:397
  81.4 2.5 %fusion.7.grad_ref = bf16[160,64]{1,0:T(8,128)(2,1)S(1)} fusion(bf16[224,6144]{1,0:T(8,128)(2,1)} %all-gather.2.cloned.1.call-done), kind=kOutput, calls=%fused_computation.5 | convolution fusion | flops 125849600 | bytes 2772992 | tf_op jit(solution)/shard_map/dot_general | solution.py:412
  84.1 2.7 %fusion.2.main_ref = f32[160,256]{1,0:T(8,128)S(1)} fusion(bf16[256,6144]{1,0:T(8,128)(2,1)S(1)} %copy-done.14, bf16[224,6144]{1,0:T(8,128)(2,1)} %all-gather.2.cloned.1.call-done), kind=kOutput, calls=%fused_computation.2 | convolution fusion | flops 503316480 | bytes 5275648 | tf_op jit(solution)/shard_map/dot_general | solution.py:38
  87.6 18.2 %all_to_all.39.chunks_ref = bf16[64,8,128]{2,1,0:T(8,128)(2,1)S(1)} all-to-all(bf16[64,8,128]{2,1,0:T(8,128)(2,1)S(1)} %shard_map.143), channel_id=1, replica_groups=mesh['e'=8,'r'=4,'z'=8,'c'=2] {'r','z','c'}, dimensions={0} | all-to-all | bytes 262144 | tf_op jit(solution)/shard_map/all_to_all | solution.py:34
  106.6 5.6 %all-to-all-start.4 = ((bf16[64,8,128]{2,1,0:T(8,128)(2,1)}), bf16[64,8,128]{2,1,0:T(8,128)(2,1)S(1)}, u32[]{:S(2)}, u32[]{:S(2)}) async-start(bf16[64,8,128]{2,1,0:T(8,128)(2,1)} %get-tuple-element.31), calls=%async_computation.5 | async-start | bytes 262144 | tf_op jit(solution)/shard_map/all_to_all | solution.py:34
  112.5 9.4 %reduce-scatter.2.cloned.1.call-done = f32[1,160,384]{2,1,0:T(8,128)} async-done(((f32[8,160,384]{2,1,0:T(8,128)}), f32[1,160,384]{2,1,0:T(8,128)}) %reduce-scatter.2.cloned.1.call-update) | async-done | bytes 245776 | tf_op jit(solution)/shard_map/reduce_scatter | solution.py:408
  121.9 0.9 copy-done.3
  122.8 1.5 shard_map.145
  124.3 9.5 %all-to-all-start.5 = ((bf16[32,22,384]{2,1,0:T(8,128)(2,1)}), bf16[32,22,384]{2,1,0:T(8,128)(2,1)S(1)}, u32[]{:S(2)}, u32[]{:S(2)}) async-start(bf16[32,22,384]{2,1,0:T(8,128)(2,1)} %shard_map.145), calls=%async_computation.6 | async-start | bytes 1179648 | tf_op jit(solution)/shard_map/all_to_all | solution.py:34
  134.7 0.9 shard_map.147
  135.6 15.0 %all-to-all-done.5.parcel_ref = bf16[32,22,384]{2,1,0:T(8,128)(2,1)S(1)} async-done(((bf16[32,22,384]{2,1,0:T(8,128)(2,1)}), bf16[32,22,384]{2,1,0:T(8,128)(2,1)S(1)}, u32[]{:S(2)}, u32[]{:S(2)}) %all-to-all-start.5) | async-done | bytes 540704 | tf_op jit(solution)/shard_map/all_to_all | solution.py:34
  150.6 1.4 shard_map.146
  (54 shorter events, 10.5 us)
Async XLA Ops:
  8.0 22.4 %copy-start = (bf16[8,64,384]{2,1,0:T(8,128)(2,1)S(1)}, bf16[8,64,384]{2,1,0:T(8,128)(2,1)}, u32[]{:S(2)}) copy-start(bf16[8,64,384]{2,1,0:T(8,128)(2,1)} %param.15) | copy-start | bytes 1179652
  8.0 0.8 copy-start.6
  8.8 0.7 copy-start.9
  9.5 0.7 copy-start.11
  11.2 61.5 %copy-start.2 = (bf16[256,256]{1,0:T(8,128)(2,1)S(1)}, bf16[256,256]{1,0:T(8,128)(2,1)}, u32[]{:S(2)}) copy-start(bf16[256,256]{1,0:T(8,128)(2,1)} %constant.19.clone.spread_ref) | copy-start | bytes 393220
  11.2 21.3 %all-to-all-start = ((bf16[32,5,384]{2,1,0:T(8,128)(2,1)}), bf16[32,5,384]{2,1,0:T(8,128)(2,1)S(1)}, u32[]{:S(2)}, u32[]{:S(2)}) async-start(bf16[32,5,384]{2,1,0:T(8,128)(2,1)} %all_to_all.23), calls=%async_computation | async-start | bytes 393216 | tf_op jit(solution)/shard_map/all_to_all | solution.py:34
  21.5 60.0 %all-gather.2.cloned.1.call-start = ((), (), s32[]{:S(2)}) async-start(), calls=%async_computation.8 | async-start | bytes 2924544 | tf_op jit(solution)/shard_map/all_gather | solution.py:397
  21.5 0.9 copy-start.5
  22.4 0.7 copy-start.7
  23.3 1.9 %copy-start.1 = (bf16[256,6144]{1,0:T(8,128)(2,1)S(1)}, bf16[256,6144]{1,0:T(8,128)(2,1)}, u32[]{:S(2)}) copy-start(bf16[256,6144]{1,0:T(8,128)(2,1)} %codes_ref.1) | copy-start | bytes 9437188
  25.2 0.9 copy-start.4
  27.6 1.6 %copy-start.13 = (bf16[256,6144]{1,0:T(8,128)(2,1)}, bf16[256,6144]{1,0:T(8,128)(2,1)S(1)}, u32[]{:S(2)}) copy-start(bf16[256,6144]{1,0:T(8,128)(2,1)S(1)} %get-tuple-element.30) | copy-start | bytes 9437188
  29.2 1.2 copy-start.15
  33.2 88.6 %reduce-scatter.2.cloned.1.call-start = ((), (), s32[]{:S(2)}) async-start(), calls=%async_computation.7 | async-start | bytes 2211840 | tf_op jit(solution)/shard_map/reduce_scatter | solution.py:408
  33.3 43.0 %collective-permute-start.1 = (bf16[8,256,384]{2,1,0:T(8,128)(2,1)}, bf16[8,256,384]{2,1,0:T(8,128)(2,1)S(1)}, u32[]{:S(2)}, u32[]{:S(2)}) collective-permute-start(bf16[8,256,384]{2,1,0:T(8,128)(2,1)} %copy-done.15), channel_id=1, source_target_pairs={{0,1},{1,0},{2,3},{3,2},{4,5},{5,4},{6,7},{7,6},{8,9},{9,8},{10,11... | collective-permute-start | bytes 4718600 | tf_op jit(solution)/shard_map/ppermute | solution.py:405
  73.1 5.8 %copy-start.16 = (bf16[256,64]{0,1:T(8,128)(2,1)S(1)}, bf16[256,64]{0,1:T(8,128)(2,1)}, u32[]{:S(2)}) copy-start(bf16[256,64]{0,1:T(8,128)(2,1)} %param.14) | copy-start | bytes 98308
  73.1 3.2 %collective-permute-start = (bf16[160,256]{1,0:T(8,128)(2,1)S(1)}, bf16[160,256]{1,0:T(8,128)(2,1)S(1)}, u32[]{:S(2)}, u32[]{:S(2)}) collective-permute-start(bf16[160,256]{1,0:T(8,128)(2,1)S(1)} %shard_map.141.rotated_ref), channel_id=1, source_target_pairs={{0,1},{1,0},{2,3},{3,2},{4,5},{5,4},{6,7},{7,6},{8,9},{9,8},{10,11... | collective-permute-start | bytes 245768 | tf_op jit(solution)/shard_map/ppermute | solution.py:406
  81.4 2.7 %copy-start.14 = (bf16[256,6144]{1,0:T(8,128)(2,1)S(1)}, bf16[256,6144]{1,0:T(8,128)(2,1)}, u32[]{:S(2)}) copy-start(bf16[256,6144]{1,0:T(8,128)(2,1)} %copy-done.13) | copy-start | bytes 9437188
  86.9 47.8 %copy-start.8 = (s32[256]{0:T(256)S(1)}, s32[256]{0:T(256)}, u32[]{:S(2)}) copy-start(s32[256]{0:T(256)} %param.13) | copy-start | bytes 3076
  86.9 63.7 %copy-start.10 = (s32[16,2]{0,1:T(2,128)S(1)}, s32[16,2]{0,1:T(2,128)}, u32[]{:S(2)}) copy-start(s32[16,2]{0,1:T(2,128)} %param.16) | copy-start | bytes 388
  86.9 63.7 %copy-start.12 = (f32[16,2]{0,1:T(2,128)S(1)}, f32[16,2]{0,1:T(2,128)}, u32[]{:S(2)}) copy-start(f32[16,2]{0,1:T(2,128)} %param.17) | copy-start | bytes 388
  106.6 15.3 %all-to-all-start.4 = ((bf16[64,8,128]{2,1,0:T(8,128)(2,1)}), bf16[64,8,128]{2,1,0:T(8,128)(2,1)S(1)}, u32[]{:S(2)}, u32[]{:S(2)}) async-start(bf16[64,8,128]{2,1,0:T(8,128)(2,1)} %get-tuple-element.31), calls=%async_computation.5 | async-start | bytes 262144 | tf_op jit(solution)/shard_map/all_to_all | solution.py:34
  121.8 0.9 copy-start.3
  124.3 26.2 %all-to-all-start.5 = ((bf16[32,22,384]{2,1,0:T(8,128)(2,1)}), bf16[32,22,384]{2,1,0:T(8,128)(2,1)S(1)}, u32[]{:S(2)}, u32[]{:S(2)}) async-start(bf16[32,22,384]{2,1,0:T(8,128)(2,1)} %shard_map.145), calls=%async_computation.6 | async-start | bytes 1179648 | tf_op jit(solution)/shard_map/all_to_all | solution.py:34
Sparse Core Ops, SparseCore 0:
  33.3 48.0 all-gather.1
Sparse Core Ops, SparseCore 1:
  79.0 42.8 reduce-scatter.1

commit v8 on v7

--- a/solution.py
+++ b/solution.py
@@ -114,9 +114,7 @@
 
     def kernel(frozen_ref, mixed_ref, up_ref, rows_ref, totals_ref, out_ref):
         flat = mixed_ref[...].reshape(peers * TILE, LANES)
-        first = dot(rider_rows(peers, ROWS), flat, ((0,), (0,)))
-        second = dot(rider_rows(peers, ROWS + 1), flat, ((0,), (0,)))
-        adapter = jnp.concatenate([first, second[:, :rest]], axis=1).astype(BF)
+        adapter = read_riders(flat, peers, rest).astype(BF)
         replicas = devices // EXPERT_COUNT
         share = rank // replicas
         slots = frozen_ref[...] + (LOWRANK_SCALE / replicas) * dot(
@@ -249,22 +247,39 @@
     )(rotated, neighbour, own, other)
 
 
-def to_chunks(values, signs):
+def rank_riders(columns, peers):
+    rest = columns.shape[1] - LANES
+    pad = jnp.zeros((peers, LANES - rest), BF)
+    tail = jnp.concatenate([columns[:, LANES:], pad], axis=1)
+    riders = dot(rider_rows(peers, ROWS), columns[:, :LANES])
+    return riders + dot(rider_rows(peers, ROWS + 1), tail)
+
+
+def read_riders(flat, peers, rest):
+    first = dot(rider_rows(peers, ROWS), flat, ((0,), (0,)))
+    second = dot(rider_rows(peers, ROWS + 1), flat, ((0,), (0,)))
+    return jnp.concatenate([first, second[:, :rest]], axis=1)
+
+
+def to_chunks(values, signs, d_rows, up_map):
     height, stride = values.shape
     halves = stride // LANES
     blocks = height // ROWS
-
-    def kernel(values_ref, signs_ref, out_ref):
+    peers = halves * blocks
+
+    def kernel(values_ref, signs_ref, rows_ref, up_ref, out_ref):
         sign = (2 * signs_ref[...] - 1).astype(F32)
         signed = (values_ref[...].astype(F32) * sign).astype(BF)
+        riders = rank_riders(dot(up_ref[...], rows_ref[...], ((1,), (1,))).astype(BF), peers)
         place = placement(blocks, ROWS)
         for half in range(halves):
             part = dot(place, signed[:, half * LANES : (half + 1) * LANES])
+            part += riders[half * blocks * TILE : (half + 1) * blocks * TILE]
             part = part.astype(BF).reshape(blocks, TILE, LANES)
             out_ref[half * blocks : (half + 1) * blocks] = part
 
-    out = jax.ShapeDtypeStruct((halves * blocks, TILE, LANES), BF)
-    return whole(kernel, out, values, signs.reshape(1, stride))
+    out = jax.ShapeDtypeStruct((peers, TILE, LANES), BF)
+    return whole(kernel, out, values, signs.reshape(1, stride), d_rows, up_map)
 
 
 def hadamard(parts):
@@ -302,14 +317,22 @@
     return jnp.concatenate(parts, axis=1)
 
 
-def finish_rotation(chunks, spread, scaling):
-    blocks = chunks.shape[0] * LANES // spread.shape[0]
-
-    def kernel(chunks_ref, spread_ref, out_ref):
-        values = gather_rows(chunks_ref[...], blocks).astype(BF)
+def finish_rotation(chunks, spread, scaling, replicas):
+    peers = chunks.shape[0]
+    blocks = peers * LANES // spread.shape[0]
+    rest = blocks * ROWS - LANES
+
+    def kernel(chunks_ref, spread_ref, out_ref, grad_ref):
+        chunk_values = chunks_ref[...]
+        values = gather_rows(chunk_values, blocks).astype(BF)
         out_ref[...] = (dot(values, spread_ref[...]) * scaling).astype(BF)
-
-    out = jax.ShapeDtypeStruct((blocks * ROWS, spread.shape[0]), BF)
+        grad = read_riders(chunk_values.reshape(peers * TILE, LANES), peers, rest)
+        grad_ref[...] = (grad * (LOWRANK_SCALE / replicas)).astype(BF)
+
+    out = (
+        jax.ShapeDtypeStruct((blocks * ROWS, spread.shape[0]), BF),
+        jax.ShapeDtypeStruct((peers, blocks * ROWS), BF),
+    )
     return whole(kernel, out, chunks, spread)
 
 
@@ -335,7 +358,7 @@
     def kernel(main_ref, grad_ref, down_ref, rotated_ref, spread_ref, out_ref):
         rotated_value = rotated_ref[...]
         down = down_ref[...]
-        d_rotated = main_ref[...] + dot(grad_ref[...], down, ((1,), (1,)))
+        d_rotated = main_ref[...] + dot(grad_ref[...], down, ((0,), (1,)))
         local = dot(d_rotated.astype(BF), spread_ref[...])
         local = (local * scaling).astype(BF)
         product = rotated_value.astype(F32) * d_rotated
@@ -347,10 +370,7 @@
             preferred_element_type=F32,
         )
         adapter = dot(down, rotated_value, ((0,), (1,))).astype(BF)
-        pad = jnp.zeros((peers, LANES - rest), BF)
-        riders = dot(rider_rows(peers, ROWS), adapter[:, :LANES])
-        tail = jnp.concatenate([adapter[:, LANES:], pad], axis=1)
-        riders += dot(rider_rows(peers, ROWS + 1), tail)
+        riders = rank_riders(adapter, peers)
         row_tail = jnp.concatenate(
             [totals[:, LANES:], jnp.zeros((TILE, LANES - rest), F32)], axis=1
         )
@@ -389,32 +409,24 @@
     outgoing, target = route(experts.T, gates.T, output_gradient, replicas, capacity)
     weights, own, other = dequantize(codes, scales, depth, columns)
     d_rows = exchange(outgoing, EXPERT)
-    chunks = to_chunks(hidden, signs)
-    d_rows, weights, own, other, chunks = lax.optimization_barrier(
-        (d_rows, weights, own, other, chunks)
-    )
+    arrived = lax.ppermute(other, "c", [(0, 1), (1, 0)])
+    d_rows, weights, own, _ = lax.optimization_barrier((d_rows, weights, own, other))
     lowrank_local = lax.dynamic_index_in_dim(lowrank_up_map, expert_position, 0, keepdims=False)
-    gathered = lax.all_gather(
-        jnp.concatenate([d_rows, lowrank_local], axis=0), TENSOR, axis=1, tiled=True
-    )
+    d_full = lax.all_gather(d_rows, TENSOR, axis=1, tiled=True)
 
     spread_local = sylvester(stride)
+    chunks = to_chunks(hidden, signs, d_rows, lowrank_local)
     mixed_blocks, _ = mix_blocks(exchange(chunks, SLAB))
-    rotated = finish_rotation(exchange(mixed_blocks, SLAB), spread_local, scaling)
-
-    other = lax.ppermute(other, "c", [(0, 1), (1, 0)])
+    rotated, adapter_grad = finish_rotation(
+        exchange(mixed_blocks, SLAB), spread_local, scaling, replicas
+    )
+
     neighbour = lax.ppermute(rotated, "c", [(0, 1), (1, 0)])
-    pair = pair_products(rotated, neighbour, own, other)
+    pair = pair_products(rotated, neighbour, own, arrived)
     frozen = lax.psum_scatter(pair, "z", scatter_dimension=0, tiled=False)
 
-    d_full = gathered[:slot_rows]
-    lowrank_full = gathered[slot_rows:]
-    adapter_grad = LOWRANK_SCALE * lax.dot_general(
-        d_full, lowrank_full, (((1,), (1,)), ((), ())), preferred_element_type=F32
-    )
-    adapter_grad = adapter_grad.astype(BF)
     main = dot(d_full, weights, ((1,), (1,)))
-    down_map_gradient = dot(rotated, adapter_grad, ((0,), (0,)))
+    down_map_gradient = dot(rotated, adapter_grad, ((0,), (1,)))
     d_chunks = exchange(
         backward_chunks(main, adapter_grad, lowrank_down_map, rotated, spread_local, scaling), SLAB
     )

time: 160 us -> 168 us (1.050)
  local copies, waits for them, and re-layouts: 11.5 us -> 19.3 us
  waiting for transfers between devices: 30 us -> 34.3 us
  blocking collectives: 55.1 us -> 52 us
  matrix products: 6.1 us -> 3.59 us
  Pallas kernels: 10.9 us -> 12.9 us
    all_to_all x3, waiting for transfers between devices: 17.1 us -> 27.9 us  [exchange(): return lax.all_to_all(value, axes, split_axis=0, concat_axis=0, tiled=True)]
    unnamed x35 -> x55, local copies, waits for them, and re-layouts: 10.5 us -> 16.7 us
    reduce_scatter x1, waiting for transfers between devices: 9.37 us -> 5.17 us  [body(): frozen = lax.psum_scatter(pair, 'z', scatter_dimension=0, tiled=False)]
    all_to_all x3, blocking collectives: 55.1 us -> 52 us  [exchange(): return lax.all_to_all(value, axes, split_axis=0, concat_axis=0, tiled=True)]
    dot_general x1 -> x0, matrix products: 2.53 us -> none  [body(): lax.dot_general(d_full, lowrank_full, (((1,), (1,)), ((), ())), preferred...]
    all_gather x1, waiting for transfers between devices: 2.38 us -> 0.01 us  [body(): d_full = lax.all_gather(d_rows, TENSOR, axis=1, tiled=True)]
  transfers between devices with their start and end apart: 7 -> 7, of which waited for: 5 -> 5; matrix products, arithmetic and copies ran while one was open for 4% -> 3% of each run, Pallas kernels for 5% -> 6%
where the time goes in v8:
time: 168 us; the launch traced here: 167 us
  blocking collectives  52 us (31%)
  waiting for transfers between devices  34.3 us (20%)
  starting transfers between devices  29.6 us (18%)
  local copies, waits for them, and re-layouts  19.3 us (11%)
  between operations  15.8 us (9%)
  Pallas kernels  12.9 us (8%)
  matrix products  3.59 us (2%)
    all_to_all x3, blocking collectives, exchange(): return lax.all_to_all(value, axes, split_axis=0, concat_axis=0, tiled=True)  52 us
    all_to_all x3, waiting for transfers between devices, exchange(): return lax.all_to_all(value, axes, split_axis=0, concat_axis=0, tiled=True)  27.9 us
    all_to_all x3, starting transfers between devices, exchange(): return lax.all_to_all(value, axes, split_axis=0, concat_axis=0, tiled=True)  25.6 us
    unnamed x55, local copies, waits for them, and re-layouts  16.7 us
    pallas_call x9, Pallas kernels, whole(): pl.pallas_call(kernel, out_shape=out_shape, compiler_params=pltpu.Compile...  7.18 us
    reduce_scatter x1, waiting for transfers between devices, body(): frozen = lax.psum_scatter(pair, 'z', scatter_dimension=0, tiled=False)  5.17 us
    pallas_call x1, Pallas kernels, pair_products(): pl.pallas_call(kernel, grid=(depth // step,), in_specs=[rows, rows, half,...  4.26 us
    dot_general x2, matrix products, dot(): lax.dot_general(left, right, (dims, ((), ())), preferred_element_type=F32)  3.59 us
  transfers between devices with their start and end apart: 7, of which 5 were waited for; matrix products, arithmetic and copies ran while one was open for 3% of the time, Pallas kernels for 6%

profile of v8, /device:TPU:8, one launch (start us, length us, event | category | flops | bytes accessed | tf_op | source)
XLA Modules:
  0.0 167.5 jit_solution(12058492881353978968)
XLA Ops:
  11.2 10.2 %all-to-all-start = ((bf16[32,5,384]{2,1,0:T(8,128)(2,1)}), bf16[32,5,384]{2,1,0:T(8,128)(2,1)}, u32[]{:S(2)}, u32[]{:S(2)}) async-start(bf16[32,5,384]{2,1,0:T(8,128)(2,1)} %all_to_all.23), calls=%async_computation | async-start | bytes 393216 | tf_op jit(solution)/shard_map/all_to_all | solution.py:34
  21.4 1.9 %copy-done.1 = bf16[256,6144]{1,0:T(8,128)(2,1)S(1)} copy-done((bf16[256,6144]{1,0:T(8,128)(2,1)S(1)}, bf16[256,6144]{1,0:T(8,128)(2,1)}, u32[]{:S(2)}) %copy-start.1) | copy-done | bytes 3145752
  24.2 1.4 shard_map.138
  25.7 1.1 copy-done.4
  26.8 1.2 copy-done.26
  28.0 4.4 %all-to-all-done = bf16[32,5,384]{2,1,0:T(8,128)(2,1)} async-done(((bf16[32,5,384]{2,1,0:T(8,128)(2,1)}), bf16[32,5,384]{2,1,0:T(8,128)(2,1)}, u32[]{:S(2)}, u32[]{:S(2)}) %all-to-all-start) | async-done | bytes 122912 | tf_op jit(solution)/shard_map/all_to_all | solution.py:34
  32.4 1.6 all_to_all.25.rows_ref
  34.1 1.9 %collective-permute-start.1 = (bf16[8,256,384]{2,1,0:T(8,128)(2,1)}, bf16[8,256,384]{2,1,0:T(8,128)(2,1)}, u32[]{:S(2)}, u32[]{:S(2)}) collective-permute-start(bf16[8,256,384]{2,1,0:T(8,128)(2,1)} %copy-done.26), channel_id=1, source_target_pairs={{0,1},{1,0},{2,3},{3,2},{4,5},{5,4},{6,7},{7,6},{8,9},{9,8},{10,11... | collective-permute-start | bytes 4718600 | tf_op jit(solution)/shard_map/ppermute | solution.py:412
  38.5 22.0 %all_to_all.37.chunks_ref = bf16[64,8,128]{2,1,0:T(8,128)(2,1)S(1)} all-to-all(bf16[64,8,128]{2,1,0:T(8,128)(2,1)S(1)} %shard_map.139), channel_id=1, replica_groups=mesh['e'=8,'r'=4,'z'=8,'c'=2] {'r','z','c'}, dimensions={0} | all-to-all | bytes 262144 | tf_op jit(solution)/shard_map/all_to_all | solution.py:34
  61.1 15.0 %all_to_all.38.chunks_ref = bf16[64,8,128]{2,1,0:T(8,128)(2,1)S(1)} all-to-all(bf16[64,8,128]{2,1,0:T(8,128)(2,1)S(1)} %get-tuple-element.26), channel_id=1, replica_groups=mesh['e'=8,'r'=4,'z'=8,'c'=2] {'r','z','c'}, dimensions={0} | all-to-all | bytes 262144 | tf_op jit(solution)/shard_map/all_to_all | solution.py:34
  78.0 2.0 %collective-permute-start = (bf16[160,256]{1,0:T(8,128)(2,1)S(1)}, bf16[160,256]{1,0:T(8,128)(2,1)S(1)}, u32[]{:S(2)}, u32[]{:S(2)}) collective-permute-start(bf16[160,256]{1,0:T(8,128)(2,1)S(1)} %get-tuple-element.27.rotated_ref), channel_id=1, source_target_pairs={{0,1},{1,0},{2,3},{3,2},{4,5},{5,4},{6,7},{7,6},{8,9},{9,8},{10,11... | collective-permute-start | bytes 245768 | tf_op jit(solution)/shard_map/ppermute | solution.py:424
  80.0 1.1 collective-permute-done.neighbour_ref
  81.2 1.4 copy-done.5
  82.6 4.3 %shard_map.142 = f32[8,160,384]{2,1,0:T(8,128)} custom-call(bf16[160,256]{1,0:T(8,128)(2,1)S(1)} %get-tuple-element.27.rotated_ref, bf16[160,256]{1,0:T(8,128)(2,1)S(1)} %collective-permute-done.neighbour_ref, bf16[8,256,384]{2,1,0:T(8,128)(2,1)S(1)} %copy-done.5, bf16[8,256,384]{2,1,0:T(8,128)(2,1)} %collective-permute-done.1.other_ref), custom_call_target="tpu_custom_call" | custom-call | flops 503316480 | bytes 5111808 | tf_op jit(solution)/shard_map/pallas_call | solution.py:235
  87.5 1.5 copy.16.down_ref
  89.0 2.8 %fusion.5.main_ref = f32[160,256]{1,0:T(8,128)S(1)} fusion(bf16[160,6144]{1,0:T(8,128)(2,1)} %all-gather.2.cloned.1.call-done, bf16[256,6144]{1,0:T(8,128)(2,1)S(1)} %get-tuple-element.29), kind=kOutput, calls=%fused_computation.12 | convolution fusion | flops 503316480 | bytes 5275648 | tf_op jit(solution)/shard_map/dot_general | solution.py:38
  92.6 15.0 %all_to_all.39.chunks_ref = bf16[64,8,128]{2,1,0:T(8,128)(2,1)S(1)} all-to-all(bf16[64,8,128]{2,1,0:T(8,128)(2,1)S(1)} %shard_map.143), channel_id=1, replica_groups=mesh['e'=8,'r'=4,'z'=8,'c'=2] {'r','z','c'}, dimensions={0} | all-to-all | bytes 262144 | tf_op jit(solution)/shard_map/all_to_all | solution.py:34
  108.6 5.6 %all-to-all-start.4 = ((bf16[64,8,128]{2,1,0:T(8,128)(2,1)}), bf16[64,8,128]{2,1,0:T(8,128)(2,1)S(1)}, u32[]{:S(2)}, u32[]{:S(2)}) async-start(bf16[64,8,128]{2,1,0:T(8,128)(2,1)} %get-tuple-element.31), calls=%async_computation.5 | async-start | bytes 262144 | tf_op jit(solution)/shard_map/all_to_all | solution.py:34
  114.3 9.4 %all-to-all-done.4.mixed_ref.chunks_ref = bf16[64,8,128]{2,1,0:T(8,128)(2,1)S(1)} async-done(((bf16[64,8,128]{2,1,0:T(8,128)(2,1)}), bf16[64,8,128]{2,1,0:T(8,128)(2,1)S(1)}, u32[]{:S(2)}, u32[]{:S(2)}) %all-to-all-start.4) | async-done | bytes 131104 | tf_op jit(solution)/shard_map/all_to_all | solution.py:34
  123.7 5.2 %reduce-scatter.2.cloned.1.call-done = f32[1,160,384]{2,1,0:T(8,128)} async-done(((f32[8,160,384]{2,1,0:T(8,128)}), f32[1,160,384]{2,1,0:T(8,128)}) %reduce-scatter.2.cloned.1.call-update) | async-done | bytes 245776 | tf_op jit(solution)/shard_map/reduce_scatter | solution.py:426
  131.6 1.5 shard_map.145
  133.1 9.7 %all-to-all-start.5 = ((bf16[32,22,384]{2,1,0:T(8,128)(2,1)}), bf16[32,22,384]{2,1,0:T(8,128)(2,1)S(1)}, u32[]{:S(2)}, u32[]{:S(2)}) async-start(bf16[32,22,384]{2,1,0:T(8,128)(2,1)} %shard_map.145), calls=%async_computation.6 | async-start | bytes 1179648 | tf_op jit(solution)/shard_map/all_to_all | solution.py:34
  144.5 14.1 %all-to-all-done.5.parcel_ref = bf16[32,22,384]{2,1,0:T(8,128)(2,1)S(1)} async-done(((bf16[32,22,384]{2,1,0:T(8,128)(2,1)}), bf16[32,22,384]{2,1,0:T(8,128)(2,1)S(1)}, u32[]{:S(2)}, u32[]{:S(2)}) %all-to-all-start.5) | async-done | bytes 540704 | tf_op jit(solution)/shard_map/all_to_all | solution.py:34
  158.6 1.4 shard_map.146
  (72 shorter events, 15.8 us)
Async XLA Ops:
  8.0 28.1 %copy-start = (bf16[8,64,384]{2,1,0:T(8,128)(2,1)S(1)}, bf16[8,64,384]{2,1,0:T(8,128)(2,1)}, u32[]{:S(2)}) copy-start(bf16[8,64,384]{2,1,0:T(8,128)(2,1)} %param.15) | copy-start | bytes 1179652
  11.2 21.3 %all-to-all-start = ((bf16[32,5,384]{2,1,0:T(8,128)(2,1)}), bf16[32,5,384]{2,1,0:T(8,128)(2,1)}, u32[]{:S(2)}, u32[]{:S(2)}) async-start(bf16[32,5,384]{2,1,0:T(8,128)(2,1)} %all_to_all.23), calls=%async_computation | async-start | bytes 393216 | tf_op jit(solution)/shard_map/all_to_all | solution.py:34
  21.4 67.6 %all-gather.2.cloned.1.call-start = ((), (), s32[]{:S(2)}) async-start(), calls=%async_computation.8 | async-start | bytes 2088960 | tf_op jit(solution)/shard_map/all_gather | solution.py:415
  21.4 1.9 %copy-start.1 = (bf16[256,6144]{1,0:T(8,128)(2,1)S(1)}, bf16[256,6144]{1,0:T(8,128)(2,1)}, u32[]{:S(2)}) copy-start(bf16[256,6144]{1,0:T(8,128)(2,1)} %codes_ref.1) | copy-start | bytes 9437188
  24.2 11.9 %copy-start.21 = (s32[256]{0:T(256)S(1)}, s32[256]{0:T(256)}, u32[]{:S(2)}) copy-start(s32[256]{0:T(256)} %param.13) | copy-start | bytes 3076
  25.7 1.1 copy-start.4
  26.8 1.2 copy-start.26
  34.1 94.8 %reduce-scatter.2.cloned.1.call-start = ((), (), s32[]{:S(2)}) async-start(), calls=%async_computation.7 | async-start | bytes 2211840 | tf_op jit(solution)/shard_map/reduce_scatter | solution.py:426
  34.1 47.0 %collective-permute-start.1 = (bf16[8,256,384]{2,1,0:T(8,128)(2,1)}, bf16[8,256,384]{2,1,0:T(8,128)(2,1)}, u32[]{:S(2)}, u32[]{:S(2)}) collective-permute-start(bf16[8,256,384]{2,1,0:T(8,128)(2,1)} %copy-done.26), channel_id=1, source_target_pairs={{0,1},{1,0},{2,3},{3,2},{4,5},{5,4},{6,7},{7,6},{8,9},{9,8},{10,11... | collective-permute-start | bytes 4718600 | tf_op jit(solution)/shard_map/ppermute | solution.py:412
  36.1 2.4 %copy-start.11 = (bf16[64,384]{1,0:T(8,128)(2,1)}, bf16[64,384]{1,0:T(8,128)(2,1)S(1)}, u32[]{:S(2)}) copy-start(bf16[64,384]{1,0:T(8,128)(2,1)S(1)} %dynamic-slice_bitcast_fusion.up_ref) | copy-start | bytes 147460
  36.1 0.9 copy-start.2
  78.0 3.2 %collective-permute-start = (bf16[160,256]{1,0:T(8,128)(2,1)S(1)}, bf16[160,256]{1,0:T(8,128)(2,1)S(1)}, u32[]{:S(2)}, u32[]{:S(2)}) collective-permute-start(bf16[160,256]{1,0:T(8,128)(2,1)S(1)} %get-tuple-element.27.rotated_ref), channel_id=1, source_target_pairs={{0,1},{1,0},{2,3},{3,2},{4,5},{5,4},{6,7},{7,6},{8,9},{9,8},{10,11... | collective-permute-start | bytes 245768 | tf_op jit(solution)/shard_map/ppermute | solution.py:424
  81.2 1.4 copy-start.5
  89.0 2.9 %copy-start.7 = (bf16[160,256]{1,0:T(8,128)(2,1)S(1)}, bf16[160,256]{1,0:T(8,128)(2,1)}, u32[]{:S(2)}) copy-start(bf16[160,256]{1,0:T(8,128)(2,1)} %copy-done.6) | copy-start | bytes 245764
  89.0 2.9 %copy-start.10 = (bf16[256,256]{1,0:T(8,128)(2,1)S(1)}, bf16[256,256]{1,0:T(8,128)(2,1)}, u32[]{:S(2)}) copy-start(bf16[256,256]{1,0:T(8,128)(2,1)} %constant.17.clone.spread_ref) | copy-start | bytes 393220
  89.0 2.9 %copy-start.13 = (bf16[256,64]{1,0:T(8,128)(2,1)S(1)}, bf16[256,64]{1,0:T(8,128)(2,1)}, u32[]{:S(2)}) copy-start(bf16[256,64]{1,0:T(8,128)(2,1)} %copy.16.down_ref) | copy-start | bytes 98308
  89.0 2.9 %copy-start.16 = (bf16[64,160]{1,0:T(8,128)(2,1)S(1)}, bf16[64,160]{1,0:T(8,128)(2,1)}, u32[]{:S(2)}) copy-start(bf16[64,160]{1,0:T(8,128)(2,1)} %copy-done.15) | copy-start | bytes 61444
  91.8 51.0 %copy-start.8 = (bf16[160,256]{1,0:T(8,128)(2,1)S(1)}, bf16[160,256]{1,0:T(8,128)(2,1)}, u32[]{:S(2)}) copy-start(bf16[160,256]{1,0:T(8,128)(2,1)} %copy-done.6) | copy-start | bytes 245764
  91.8 51.0 %copy-start.17 = (bf16[64,160]{1,0:T(8,128)(2,1)S(1)}, bf16[64,160]{1,0:T(8,128)(2,1)}, u32[]{:S(2)}) copy-start(bf16[64,160]{1,0:T(8,128)(2,1)} %copy-done.15) | copy-start | bytes 61444
  91.9 66.7 %copy-start.23 = (s32[16,2]{0,1:T(2,128)S(1)}, s32[16,2]{0,1:T(2,128)}, u32[]{:S(2)}) copy-start(s32[16,2]{0,1:T(2,128)} %param.16) | copy-start | bytes 388
  91.9 66.7 %copy-start.25 = (f32[16,2]{0,1:T(2,128)S(1)}, f32[16,2]{0,1:T(2,128)}, u32[]{:S(2)}) copy-start(f32[16,2]{0,1:T(2,128)} %param.17) | copy-start | bytes 388
  108.6 15.2 %all-to-all-start.4 = ((bf16[64,8,128]{2,1,0:T(8,128)(2,1)}), bf16[64,8,128]{2,1,0:T(8,128)(2,1)S(1)}, u32[]{:S(2)}, u32[]{:S(2)}) async-start(bf16[64,8,128]{2,1,0:T(8,128)(2,1)} %get-tuple-element.31), calls=%async_computation.5 | async-start | bytes 262144 | tf_op jit(solution)/shard_map/all_to_all | solution.py:34
  130.6 0.9 copy-start.14
  133.1 25.5 %all-to-all-start.5 = ((bf16[32,22,384]{2,1,0:T(8,128)(2,1)}), bf16[32,22,384]{2,1,0:T(8,128)(2,1)S(1)}, u32[]{:S(2)}, u32[]{:S(2)}) async-start(bf16[32,22,384]{2,1,0:T(8,128)(2,1)} %shard_map.145), calls=%async_computation.6 | async-start | bytes 1179648 | tf_op jit(solution)/shard_map/all_to_all | solution.py:34
  (10 other events, 7.7 us)
Sparse Core Ops, SparseCore 0:
  34.2 44.7 all-gather.1
Sparse Core Ops, SparseCore 1:
  87.6 41.3 reduce-scatter.1

commit v9 on v7

--- a/solution.py
+++ b/solution.py
@@ -102,7 +102,7 @@
         jax.ShapeDtypeStruct((rows, columns), BF),
         jax.ShapeDtypeStruct((choices, tokens), jnp.int32),
     )
-    return whole(kernel, out, experts, gates, output_gradient)
+    return pl.pallas_call(kernel, out_shape=out)(experts, gates, output_gradient)
 
 
 def build_parcel(frozen, d_mixed, up_map, d_rows, totals):
@@ -390,8 +390,9 @@
     weights, own, other = dequantize(codes, scales, depth, columns)
     d_rows = exchange(outgoing, EXPERT)
     chunks = to_chunks(hidden, signs)
-    d_rows, weights, own, other, chunks = lax.optimization_barrier(
-        (d_rows, weights, own, other, chunks)
+    arrived = lax.ppermute(other, "c", [(0, 1), (1, 0)])
+    d_rows, weights, own, arrived, chunks = lax.optimization_barrier(
+        (d_rows, weights, own, arrived, chunks)
     )
     lowrank_local = lax.dynamic_index_in_dim(lowrank_up_map, expert_position, 0, keepdims=False)
     gathered = lax.all_gather(
@@ -402,9 +403,8 @@
     mixed_blocks, _ = mix_blocks(exchange(chunks, SLAB))
     rotated = finish_rotation(exchange(mixed_blocks, SLAB), spread_local, scaling)
 
-    other = lax.ppermute(other, "c", [(0, 1), (1, 0)])
     neighbour = lax.ppermute(rotated, "c", [(0, 1), (1, 0)])
-    pair = pair_products(rotated, neighbour, own, other)
+    pair = pair_products(rotated, neighbour, own, arrived)
     frozen = lax.psum_scatter(pair, "z", scatter_dimension=0, tiled=False)
 
     d_full = gathered[:slot_rows]

time: 160 us -> 171 us (1.069)
  waiting for transfers between devices: 30 us -> 34.5 us
  Pallas kernels: 10.9 us -> 14.4 us
  local copies, waits for them, and re-layouts: 11.5 us -> 13.6 us
    all_to_all x3, waiting for transfers between devices: 17.1 us -> 23.7 us  [exchange(): return lax.all_to_all(value, axes, split_axis=0, concat_axis=0, tiled=True)]
    all_to_all x2, local copies, waits for them, and re-layouts: 0.79 us -> 3.26 us  [exchange(): return lax.all_to_all(value, axes, split_axis=0, concat_axis=0, tiled=True)]
    all_gather x1, waiting for transfers between devices: 2.38 us -> 0.02 us  [body(): lax.all_gather(jnp.concatenate([d_rows, lowrank_local], axis=0), TENSOR,...]
    pallas_call x1, Pallas kernels: 1.44 us -> 3.55 us  [dequantize(): pl.pallas_call(kernel, grid=(depth,), in_specs=[pl.BlockSpec((stride, 2 *...]
    unnamed x35 -> x37, local copies, waits for them, and re-layouts: 10.5 us -> 9.56 us
    pallas_call x9 -> x8, Pallas kernels: 6.8 us -> 6.51 us  [whole(): pl.pallas_call(kernel, out_shape=out_shape, compiler_params=pltpu.Compile...]
  transfers between devices with their start and end apart: 7 -> 7, of which waited for: 5 -> 4; matrix products, arithmetic and copies ran while one was open for 4% -> 5% of each run, Pallas kernels for 5% -> 5%
where the time goes in v9:
time: 171 us; the launch traced here: 170 us
  blocking collectives  55.2 us (32%)
  waiting for transfers between devices  34.5 us (20%)
  starting transfers between devices  28.7 us (17%)
  between operations  15.7 us (9%)
  Pallas kernels  14.4 us (8%)
  local copies, waits for them, and re-layouts  13.6 us (8%)
  matrix products  6.15 us (4%)
  other arithmetic  1.71 us (1%)
    all_to_all x3, blocking collectives, exchange(): return lax.all_to_all(value, axes, split_axis=0, concat_axis=0, tiled=True)  55.2 us
    all_to_all x3, starting transfers between devices, exchange(): return lax.all_to_all(value, axes, split_axis=0, concat_axis=0, tiled=True)  24.7 us
    all_to_all x3, waiting for transfers between devices, exchange(): return lax.all_to_all(value, axes, split_axis=0, concat_axis=0, tiled=True)  23.7 us
    reduce_scatter x1, waiting for transfers between devices, body(): frozen = lax.psum_scatter(pair, 'z', scatter_dimension=0, tiled=False)  9.65 us
    unnamed x37, local copies, waits for them, and re-layouts  9.56 us
    pallas_call x8, Pallas kernels, whole(): pl.pallas_call(kernel, out_shape=out_shape, compiler_params=pltpu.Compile...  6.51 us
    dot_general x2, matrix products, dot(): lax.dot_general(left, right, (dims, ((), ())), preferred_element_type=F32)  3.62 us
    pallas_call x1, Pallas kernels, dequantize(): pl.pallas_call(kernel, grid=(depth,), in_specs=[pl.BlockSpec((stride, 2 *...  3.55 us
  transfers between devices with their start and end apart: 7, of which 4 were waited for; matrix products, arithmetic and copies ran while one was open for 5% of the time, Pallas kernels for 5%

profile of v9, /device:TPU:8, one launch (start us, length us, event | category | flops | bytes accessed | tf_op | source)
XLA Modules:
  0.0 170.0 jit_solution(14635534166129264936)
XLA Ops:
  8.0 1.9 %copy-done.1 = bf16[256,6144]{1,0:T(8,128)(2,1)S(1)} copy-done((bf16[256,6144]{1,0:T(8,128)(2,1)S(1)}, bf16[256,6144]{1,0:T(8,128)(2,1)}, u32[]{:S(2)}) %copy-start.1) | copy-done | bytes 3145752
  10.8 3.6 %shard_map.138 = (bf16[256,6144]{1,0:T(8,128)(2,1)S(1)}, bf16[8,256,384]{2,1,0:T(8,128)(2,1)S(1)}, bf16[8,256,384]{2,1,0:T(8,128)(2,1)}) custom-call(bf16[256,6144]{1,0:T(8,128)(2,1)S(1)} %copy-done.1, f32[4,6144]{1,0:T(4,128)S(1)} %copy-done.10), custom_call_target="tpu_custom_call" | custom-call | flops 3145728 | bytes 9437184 | tf_op jit(solution)/shard_map/pallas_call | solution.py:209
  14.4 1.6 copy-done.16
  16.0 1.9 %collective-permute-start = (bf16[8,256,384]{2,1,0:T(8,128)(2,1)}, bf16[8,256,384]{2,1,0:T(8,128)(2,1)S(1)}, u32[]{:S(2)}, u32[]{:S(2)}) collective-permute-start(bf16[8,256,384]{2,1,0:T(8,128)(2,1)} %get-tuple-element.24), channel_id=1, source_target_pairs={{0,1},{1,0},{2,3},{3,2},{4,5},{5,4},{6,7},{7,6},{8,9},{9,8},{10,11... | collective-permute-start | bytes 4718600 | tf_op jit(solution)/shard_map/ppermute | solution.py:393
  17.9 1.7 shard_map.137
  19.6 1.6 all_to_all.23
  21.3 10.2 %all-to-all-start = ((bf16[32,5,384]{2,1,0:T(8,128)(2,1)}), bf16[32,5,384]{2,1,0:T(8,128)(2,1)}, u32[]{:S(2)}, u32[]{:S(2)}) async-start(bf16[32,5,384]{2,1,0:T(8,128)(2,1)} %all_to_all.23), calls=%async_computation | async-start | bytes 393216 | tf_op jit(solution)/shard_map/all_to_all | solution.py:34
  33.9 9.4 %all-to-all-done = bf16[32,5,384]{2,1,0:T(8,128)(2,1)} async-done(((bf16[32,5,384]{2,1,0:T(8,128)(2,1)}), bf16[32,5,384]{2,1,0:T(8,128)(2,1)}, u32[]{:S(2)}, u32[]{:S(2)}) %all-to-all-start) | async-done | bytes 122912 | tf_op jit(solution)/shard_map/all_to_all | solution.py:34
  43.3 1.6 all_to_all.25.rows_ref
  45.0 1.6 pad_maximum_fusion
  46.7 22.0 %all_to_all.37.chunks_ref = bf16[64,8,128]{2,1,0:T(8,128)(2,1)S(1)} all-to-all(bf16[64,8,128]{2,1,0:T(8,128)(2,1)} %copy-done.7), channel_id=1, replica_groups=mesh['e'=8,'r'=4,'z'=8,'c'=2] {'r','z','c'}, dimensions={0} | all-to-all | bytes 262144 | tf_op jit(solution)/shard_map/all_to_all | solution.py:34
  69.3 14.9 %all_to_all.38.chunks_ref = bf16[64,8,128]{2,1,0:T(8,128)(2,1)S(1)} all-to-all(bf16[64,8,128]{2,1,0:T(8,128)(2,1)S(1)} %get-tuple-element.26), channel_id=1, replica_groups=mesh['e'=8,'r'=4,'z'=8,'c'=2] {'r','z','c'}, dimensions={0} | all-to-all | bytes 262144 | tf_op jit(solution)/shard_map/all_to_all | solution.py:34
  85.5 2.0 %collective-permute-start.1 = (bf16[160,256]{1,0:T(8,128)(2,1)S(1)}, bf16[160,256]{1,0:T(8,128)(2,1)S(1)}, u32[]{:S(2)}, u32[]{:S(2)}) collective-permute-start(bf16[160,256]{1,0:T(8,128)(2,1)S(1)} %shard_map.141.rotated_ref), channel_id=1, source_target_pairs={{0,1},{1,0},{2,3},{3,2},{4,5},{5,4},{6,7},{7,6},{8,9},{9,8},{10,11... | collective-permute-start | bytes 245768 | tf_op jit(solution)/shard_map/ppermute | solution.py:406
  87.5 1.2 collective-permute-done.1.neighbour_ref
  88.7 2.6 %shard_map.142 = f32[8,160,384]{2,1,0:T(8,128)} custom-call(bf16[160,256]{1,0:T(8,128)(2,1)S(1)} %shard_map.141.rotated_ref, bf16[160,256]{1,0:T(8,128)(2,1)S(1)} %collective-permute-done.1.neighbour_ref, bf16[8,256,384]{2,1,0:T(8,128)(2,1)S(1)} %get-tuple-element.27.own_ref, bf16[8,256,384]{2,1,0:T(8,128)(2,1)S(1)} %collective-permute-done.other_ref), custom_call_target="tpu_custom_call" | custom-call | flops 503316480 | bytes 5111808 | tf_op jit(solution)/shard_map/pallas_call | solution.py:237
  92.9 2.5 %fusion.7.grad_ref = bf16[160,64]{1,0:T(8,128)(2,1)S(1)} fusion(bf16[224,6144]{1,0:T(8,128)(2,1)} %all-gather.2.cloned.1.call-done), kind=kOutput, calls=%fused_computation.5 | convolution fusion | flops 125849600 | bytes 2772992 | tf_op jit(solution)/shard_map/dot_general | solution.py:412
  95.6 2.8 %fusion.2.main_ref = f32[160,256]{1,0:T(8,128)S(1)} fusion(bf16[256,6144]{1,0:T(8,128)(2,1)S(1)} %copy-done.17, bf16[224,6144]{1,0:T(8,128)(2,1)} %all-gather.2.cloned.1.call-done), kind=kOutput, calls=%fused_computation.2 | convolution fusion | flops 503316480 | bytes 5275648 | tf_op jit(solution)/shard_map/dot_general | solution.py:38
  99.1 18.3 %all_to_all.39.chunks_ref = bf16[64,8,128]{2,1,0:T(8,128)(2,1)S(1)} all-to-all(bf16[64,8,128]{2,1,0:T(8,128)(2,1)S(1)} %shard_map.143), channel_id=1, replica_groups=mesh['e'=8,'r'=4,'z'=8,'c'=2] {'r','z','c'}, dimensions={0} | all-to-all | bytes 262144 | tf_op jit(solution)/shard_map/all_to_all | solution.py:34
  118.2 5.6 %all-to-all-start.4 = ((bf16[64,8,128]{2,1,0:T(8,128)(2,1)}), bf16[64,8,128]{2,1,0:T(8,128)(2,1)S(1)}, u32[]{:S(2)}, u32[]{:S(2)}) async-start(bf16[64,8,128]{2,1,0:T(8,128)(2,1)} %get-tuple-element.31), calls=%async_computation.5 | async-start | bytes 262144 | tf_op jit(solution)/shard_map/all_to_all | solution.py:34
  124.1 9.6 %reduce-scatter.2.cloned.1.call-done = f32[1,160,384]{2,1,0:T(8,128)} async-done(((f32[8,160,384]{2,1,0:T(8,128)}), f32[1,160,384]{2,1,0:T(8,128)}) %reduce-scatter.2.cloned.1.call-update) | async-done | bytes 245776 | tf_op jit(solution)/shard_map/reduce_scatter | solution.py:408
  134.7 1.5 shard_map.145
  136.2 8.9 %all-to-all-start.5 = ((bf16[32,22,384]{2,1,0:T(8,128)(2,1)}), bf16[32,22,384]{2,1,0:T(8,128)(2,1)S(1)}, u32[]{:S(2)}, u32[]{:S(2)}) async-start(bf16[32,22,384]{2,1,0:T(8,128)(2,1)} %shard_map.145), calls=%async_computation.6 | async-start | bytes 1179648 | tf_op jit(solution)/shard_map/all_to_all | solution.py:34
  146.9 14.3 %all-to-all-done.5.parcel_ref = bf16[32,22,384]{2,1,0:T(8,128)(2,1)S(1)} async-done(((bf16[32,22,384]{2,1,0:T(8,128)(2,1)}), bf16[32,22,384]{2,1,0:T(8,128)(2,1)S(1)}, u32[]{:S(2)}, u32[]{:S(2)}) %all-to-all-start.5) | async-done | bytes 540704 | tf_op jit(solution)/shard_map/all_to_all | solution.py:34
  161.1 1.4 shard_map.146
  (56 shorter events, 11.4 us)
Async XLA Ops:
  8.0 25.3 %copy-start = (bf16[8,64,384]{2,1,0:T(8,128)(2,1)S(1)}, bf16[8,64,384]{2,1,0:T(8,128)(2,1)}, u32[]{:S(2)}) copy-start(bf16[8,64,384]{2,1,0:T(8,128)(2,1)} %param.15) | copy-start | bytes 1179652
  8.0 1.9 %copy-start.1 = (bf16[256,6144]{1,0:T(8,128)(2,1)S(1)}, bf16[256,6144]{1,0:T(8,128)(2,1)}, u32[]{:S(2)}) copy-start(bf16[256,6144]{1,0:T(8,128)(2,1)} %codes_ref.1) | copy-start | bytes 9437188
  10.0 0.9 copy-start.10
  10.8 20.7 %copy-start.12 = (s32[256]{0:T(256)S(1)}, s32[256]{0:T(256)}, u32[]{:S(2)}) copy-start(s32[256]{0:T(256)} %param.13) | copy-start | bytes 3076
  14.4 1.6 copy-start.16
  16.0 28.9 %collective-permute-start = (bf16[8,256,384]{2,1,0:T(8,128)(2,1)}, bf16[8,256,384]{2,1,0:T(8,128)(2,1)S(1)}, u32[]{:S(2)}, u32[]{:S(2)}) collective-permute-start(bf16[8,256,384]{2,1,0:T(8,128)(2,1)} %get-tuple-element.24), channel_id=1, source_target_pairs={{0,1},{1,0},{2,3},{3,2},{4,5},{5,4},{6,7},{7,6},{8,9},{9,8},{10,11... | collective-permute-start | bytes 4718600 | tf_op jit(solution)/shard_map/ppermute | solution.py:393
  21.3 22.1 %all-to-all-start = ((bf16[32,5,384]{2,1,0:T(8,128)(2,1)}), bf16[32,5,384]{2,1,0:T(8,128)(2,1)}, u32[]{:S(2)}, u32[]{:S(2)}) async-start(bf16[32,5,384]{2,1,0:T(8,128)(2,1)} %all_to_all.23), calls=%async_computation | async-start | bytes 393216 | tf_op jit(solution)/shard_map/all_to_all | solution.py:34
  31.5 61.4 %all-gather.2.cloned.1.call-start = ((), (), s32[]{:S(2)}) async-start(), calls=%async_computation.8 | async-start | bytes 2924544 | tf_op jit(solution)/shard_map/all_gather | solution.py:398
  31.5 0.9 copy-start.11
  32.7 0.6 copy-start.7
  46.6 87.1 %reduce-scatter.2.cloned.1.call-start = ((), (), s32[]{:S(2)}) async-start(), calls=%async_computation.7 | async-start | bytes 2211840 | tf_op jit(solution)/shard_map/reduce_scatter | solution.py:408
  84.2 0.9 copy-start.5
  85.5 3.2 %collective-permute-start.1 = (bf16[160,256]{1,0:T(8,128)(2,1)S(1)}, bf16[160,256]{1,0:T(8,128)(2,1)S(1)}, u32[]{:S(2)}, u32[]{:S(2)}) collective-permute-start(bf16[160,256]{1,0:T(8,128)(2,1)S(1)} %shard_map.141.rotated_ref), channel_id=1, source_target_pairs={{0,1},{1,0},{2,3},{3,2},{4,5},{5,4},{6,7},{7,6},{8,9},{9,8},{10,11... | collective-permute-start | bytes 245768 | tf_op jit(solution)/shard_map/ppermute | solution.py:406
  92.9 2.7 %copy-start.17 = (bf16[256,6144]{1,0:T(8,128)(2,1)S(1)}, bf16[256,6144]{1,0:T(8,128)(2,1)}, u32[]{:S(2)}) copy-start(bf16[256,6144]{1,0:T(8,128)(2,1)} %copy-done.16) | copy-start | bytes 9437188
  95.6 2.8 %copy-start.3 = (bf16[160,256]{1,0:T(8,128)(2,1)S(1)}, bf16[160,256]{1,0:T(8,128)(2,1)}, u32[]{:S(2)}) copy-start(bf16[160,256]{1,0:T(8,128)(2,1)} %copy-done.2) | copy-start | bytes 245764
  95.6 2.8 %copy-start.6 = (bf16[256,256]{1,0:T(8,128)(2,1)S(1)}, bf16[256,256]{1,0:T(8,128)(2,1)}, u32[]{:S(2)}) copy-start(bf16[256,256]{1,0:T(8,128)(2,1)} %constant.19.clone.spread_ref) | copy-start | bytes 393220
  95.6 38.1 %copy-start.4 = (bf16[160,384]{1,0:T(8,128)(2,1)S(1)}, bf16[160,384]{1,0:T(8,128)(2,1)}, u32[]{:S(2)}) copy-start(bf16[160,384]{1,0:T(8,128)(2,1)} %all_to_all.25.rows_ref) | copy-start | bytes 368644
  95.6 38.1 %copy-start.8 = (bf16[64,384]{1,0:T(8,128)(2,1)S(1)}, bf16[64,384]{1,0:T(8,128)(2,1)}, u32[]{:S(2)}) copy-start(bf16[64,384]{1,0:T(8,128)(2,1)} %dynamic-slice_bitcast_fusion.up_ref) | copy-start | bytes 147460
  98.4 62.7 %copy-start.13 = (s32[16,2]{0,1:T(2,128)S(1)}, s32[16,2]{0,1:T(2,128)}, u32[]{:S(2)}) copy-start(s32[16,2]{0,1:T(2,128)} %param.16) | copy-start | bytes 388
  98.4 62.7 %copy-start.14 = (f32[16,2]{0,1:T(2,128)S(1)}, f32[16,2]{0,1:T(2,128)}, u32[]{:S(2)}) copy-start(f32[16,2]{0,1:T(2,128)} %param.17) | copy-start | bytes 388
  98.4 62.7 %copy-start.15 = (s32[2,16]{1,0:T(2,128)S(1)}, s32[2,16]{1,0:T(2,128)}, u32[]{:S(2)}) copy-start(s32[2,16]{1,0:T(2,128)} %get-tuple-element.33.target_ref) | copy-start | bytes 388
  118.2 15.5 %all-to-all-start.4 = ((bf16[64,8,128]{2,1,0:T(8,128)(2,1)}), bf16[64,8,128]{2,1,0:T(8,128)(2,1)S(1)}, u32[]{:S(2)}, u32[]{:S(2)}) async-start(bf16[64,8,128]{2,1,0:T(8,128)(2,1)} %get-tuple-element.31), calls=%async_computation.5 | async-start | bytes 262144 | tf_op jit(solution)/shard_map/all_to_all | solution.py:34
  133.7 0.9 copy-start.9
  136.2 24.9 %all-to-all-start.5 = ((bf16[32,22,384]{2,1,0:T(8,128)(2,1)}), bf16[32,22,384]{2,1,0:T(8,128)(2,1)S(1)}, u32[]{:S(2)}, u32[]{:S(2)}) async-start(bf16[32,22,384]{2,1,0:T(8,128)(2,1)} %shard_map.145), calls=%async_computation.6 | async-start | bytes 1179648 | tf_op jit(solution)/shard_map/all_to_all | solution.py:34
  (1 other events, 0.6 us)
Sparse Core Ops, SparseCore 0:
  46.7 46.0 all-gather.1
Sparse Core Ops, SparseCore 1:
  92.0 41.6 reduce-scatter.1

commit v10 on v7

--- a/solution.py
+++ b/solution.py
@@ -230,7 +230,7 @@
     def kernel(rotated_ref, neighbour_ref, own_ref, other_ref, out_ref):
         for z in range(step):
             total = dot(rotated_ref[...], own_ref[z]) + dot(neighbour_ref[...], other_ref[z])
-            out_ref[z] = total
+            out_ref[z] = total.astype(BF)
 
     rows = pl.BlockSpec((height, stride), lambda z: (0, 0))
     half = pl.BlockSpec((step, stride, columns), lambda z: (z, 0, 0))
@@ -239,7 +239,7 @@
         grid=(depth // step,),
         in_specs=[rows, rows, half, half],
         out_specs=pl.BlockSpec((step, height, columns), lambda z: (z, 0, 0)),
-        out_shape=jax.ShapeDtypeStruct((depth, height, columns), F32),
+        out_shape=jax.ShapeDtypeStruct((depth, height, columns), BF),
         cost_estimate=pl.CostEstimate(
             flops=4 * height * stride * depth * columns,
             bytes_accessed=4 * depth * columns * (stride + height),
@@ -386,6 +386,9 @@
     columns = output_gradient.shape[1]
     scaling = 1.0 / math.sqrt(HIDDEN_UNITS)
 
+    lowrank_local = lax.dynamic_index_in_dim(lowrank_up_map, expert_position, 0, keepdims=False)
+    padded = jnp.pad(lowrank_local, ((0, rank // 2), (0, 0)))
+    lowrank_full = lax.all_gather(padded, TENSOR, axis=1, tiled=True)[:rank]
     outgoing, target = route(experts.T, gates.T, output_gradient, replicas, capacity)
     weights, own, other = dequantize(codes, scales, depth, columns)
     d_rows = exchange(outgoing, EXPERT)
@@ -393,10 +396,7 @@
     d_rows, weights, own, other, chunks = lax.optimization_barrier(
         (d_rows, weights, own, other, chunks)
     )
-    lowrank_local = lax.dynamic_index_in_dim(lowrank_up_map, expert_position, 0, keepdims=False)
-    gathered = lax.all_gather(
-        jnp.concatenate([d_rows, lowrank_local], axis=0), TENSOR, axis=1, tiled=True
-    )
+    d_full = lax.all_gather(d_rows, TENSOR, axis=1, tiled=True)
 
     spread_local = sylvester(stride)
     mixed_blocks, _ = mix_blocks(exchange(chunks, SLAB))
@@ -405,10 +405,8 @@
     other = lax.ppermute(other, "c", [(0, 1), (1, 0)])
     neighbour = lax.ppermute(rotated, "c", [(0, 1), (1, 0)])
     pair = pair_products(rotated, neighbour, own, other)
-    frozen = lax.psum_scatter(pair, "z", scatter_dimension=0, tiled=False)
-
-    d_full = gathered[:slot_rows]
-    lowrank_full = gathered[slot_rows:]
+    frozen = lax.psum_scatter(pair, "z", scatter_dimension=0, tiled=False).astype(F32)
+
     adapter_grad = LOWRANK_SCALE * lax.dot_general(
         d_full, lowrank_full, (((1,), (1,)), ((), ())), preferred_element_type=F32
     )

time: 160 us -> 182 us (1.14)
  waiting for transfers between devices: 30 us -> 53.6 us
  blocking collectives: 55.1 us -> 36.9 us
  local copies, waits for them, and re-layouts: 11.5 us -> 20.3 us
  starting transfers between devices: 29.4 us -> 37.9 us
    all_to_all x3 -> x2, blocking collectives: 55.1 us -> 36.9 us  [exchange(): return lax.all_to_all(value, axes, split_axis=0, concat_axis=0, tiled=True)]
    all_gather x1 -> x2, waiting for transfers between devices: 2.38 us -> 15.6 us  [the longest x1 15.6 us: body(): d_full = lax.all_gather(d_rows, TENSOR, axis=1, tiled=True)]
    all_to_all x3 -> x4, waiting for transfers between devices: 17.1 us -> 29.4 us  [exchange(): return lax.all_to_all(value, axes, split_axis=0, concat_axis=0, tiled=True)]
    all_to_all x3 -> x4, starting transfers between devices: 25.4 us -> 33.8 us  [exchange(): return lax.all_to_all(value, axes, split_axis=0, concat_axis=0, tiled=True)]
    unnamed x35 -> x55, local copies, waits for them, and re-layouts: 10.5 us -> 17.1 us
    reduce_scatter x1, waiting for transfers between devices: 9.37 us -> 7.43 us  [body(): lax.psum_scatter(pair, 'z', scatter_dimension=0, tiled=False).astype(F32)]
  transfers between devices with their start and end apart: 7 -> 9, of which waited for: 5 -> 7; matrix products, arithmetic and copies ran while one was open for 4% -> 4% of each run, Pallas kernels for 5% -> 4%
where the time goes in v10:
time: 182 us; the launch traced here: 181 us
  waiting for transfers between devices  53.6 us (29%)
  starting transfers between devices  37.9 us (21%)
  blocking collectives  36.9 us (20%)
  local copies, waits for them, and re-layouts  20.3 us (11%)
  between operations  15.8 us (9%)
  Pallas kernels  11.3 us (6%)
  matrix products  4.57 us (3%)
    all_to_all x2, blocking collectives, exchange(): return lax.all_to_all(value, axes, split_axis=0, concat_axis=0, tiled=True)  36.9 us
    all_to_all x4, starting transfers between devices, exchange(): return lax.all_to_all(value, axes, split_axis=0, concat_axis=0, tiled=True)  33.8 us
    all_to_all x4, waiting for transfers between devices, exchange(): return lax.all_to_all(value, axes, split_axis=0, concat_axis=0, tiled=True)  29.4 us
    unnamed x55, local copies, waits for them, and re-layouts  17.1 us
    all_gather x1, waiting for transfers between devices, body(): d_full = lax.all_gather(d_rows, TENSOR, axis=1, tiled=True)  15.6 us
    pallas_call x9, Pallas kernels, whole(): pl.pallas_call(kernel, out_shape=out_shape, compiler_params=pltpu.Compile...  7.45 us
    reduce_scatter x1, waiting for transfers between devices, body(): lax.psum_scatter(pair, 'z', scatter_dimension=0, tiled=False).astype(F32)  7.43 us
  transfers between devices with their start and end apart: 9, of which 7 were waited for; matrix products, arithmetic and copies ran while one was open for 4% of the time, Pallas kernels for 4%

profile of v10, /device:TPU:8, one launch (start us, length us, event | category | flops | bytes accessed | tf_op | source)
XLA Modules:
  0.0 181.4 jit_solution(13118091527082035847)
XLA Ops:
  13.4 10.2 %all-to-all-start = ((bf16[32,5,384]{2,1,0:T(8,128)(2,1)}), bf16[32,5,384]{2,1,0:T(8,128)(2,1)}, u32[]{:S(2)}, u32[]{:S(2)}) async-start(bf16[32,5,384]{2,1,0:T(8,128)(2,1)} %all_to_all.23), calls=%async_computation | async-start | bytes 393216 | tf_op jit(solution)/shard_map/all_to_all | solution.py:34
  26.1 1.9 %copy-done.1 = bf16[256,6144]{1,0:T(8,128)(2,1)S(1)} copy-done((bf16[256,6144]{1,0:T(8,128)(2,1)S(1)}, bf16[256,6144]{1,0:T(8,128)(2,1)}, u32[]{:S(2)}) %copy-start.1) | copy-done | bytes 3145752
  28.9 1.4 shard_map.138
  32.7 2.0 %all-to-all-done = bf16[32,5,384]{2,1,0:T(8,128)(2,1)} async-done(((bf16[32,5,384]{2,1,0:T(8,128)(2,1)}), bf16[32,5,384]{2,1,0:T(8,128)(2,1)}, u32[]{:S(2)}, u32[]{:S(2)}) %all-to-all-start) | async-done | bytes 122912 | tf_op jit(solution)/shard_map/all_to_all | solution.py:34
  34.6 1.6 all_to_all.25.rows_ref
  36.4 1.9 %collective-permute-start.1 = (bf16[8,256,384]{2,1,0:T(8,128)(2,1)}, bf16[8,256,384]{2,1,0:T(8,128)(2,1)S(1)}, u32[]{:S(2)}, u32[]{:S(2)}) collective-permute-start(bf16[8,256,384]{2,1,0:T(8,128)(2,1)} %copy-done.25), channel_id=1, source_target_pairs={{0,1},{1,0},{2,3},{3,2},{4,5},{5,4},{6,7},{7,6},{8,9},{9,8},{10,11... | collective-permute-start | bytes 4718600 | tf_op jit(solution)/shard_map/ppermute | solution.py:405
  38.3 22.2 %all_to_all.37.chunks_ref = bf16[64,8,128]{2,1,0:T(8,128)(2,1)S(1)} all-to-all(bf16[64,8,128]{2,1,0:T(8,128)(2,1)} %copy-done.10), channel_id=1, replica_groups=mesh['e'=8,'r'=4,'z'=8,'c'=2] {'r','z','c'}, dimensions={0} | all-to-all | bytes 262144 | tf_op jit(solution)/shard_map/all_to_all | solution.py:34
  61.1 14.7 %all_to_all.38.chunks_ref = bf16[64,8,128]{2,1,0:T(8,128)(2,1)S(1)} all-to-all(bf16[64,8,128]{2,1,0:T(8,128)(2,1)S(1)} %get-tuple-element.26), channel_id=1, replica_groups=mesh['e'=8,'r'=4,'z'=8,'c'=2] {'r','z','c'}, dimensions={0} | all-to-all | bytes 262144 | tf_op jit(solution)/shard_map/all_to_all | solution.py:34
  77.1 2.0 %collective-permute-start = (bf16[160,256]{1,0:T(8,128)(2,1)S(1)}, bf16[160,256]{1,0:T(8,128)(2,1)S(1)}, u32[]{:S(2)}, u32[]{:S(2)}) collective-permute-start(bf16[160,256]{1,0:T(8,128)(2,1)S(1)} %shard_map.141.rotated_ref), channel_id=1, source_target_pairs={{0,1},{1,0},{2,3},{3,2},{4,5},{5,4},{6,7},{7,6},{8,9},{9,8},{10,11... | collective-permute-start | bytes 245768 | tf_op jit(solution)/shard_map/ppermute | solution.py:406
  80.3 1.4 copy-done.3
  81.7 2.4 %shard_map.142 = bf16[8,160,384]{2,1,0:T(8,128)(2,1)} custom-call(bf16[160,256]{1,0:T(8,128)(2,1)S(1)} %shard_map.141.rotated_ref, bf16[160,256]{1,0:T(8,128)(2,1)S(1)} %collective-permute-done.neighbour_ref, bf16[8,256,384]{2,1,0:T(8,128)(2,1)S(1)} %copy-done.3, bf16[8,256,384]{2,1,0:T(8,128)(2,1)S(1)} %collective-permute-done.1.other_ref), custom_call_target="tpu_custom_call" | custom-call | flops 503316480 | bytes 5111808 | tf_op jit(solution)/shard_map/pallas_call | solution.py:237
  84.8 1.5 copy.18.down_ref
  86.3 15.6 %all-gather.3.cloned.1.call-done = bf16[160,6144]{1,0:T(8,128)(2,1)} async-done(((bf16[160,384]{1,0:T(8,128)(2,1)}), bf16[160,6144]{1,0:T(8,128)(2,1)}) %all-gather.3.cloned.1.call-update) | async-done | bytes 1966096 | tf_op jit(solution)/shard_map/all_gather | solution.py:399
  101.9 2.5 %fusion.grad_ref = bf16[160,64]{1,0:T(8,128)(2,1)S(1)} fusion(bf16[160,6144]{1,0:T(8,128)(2,1)} %all-gather.3.cloned.1.call-done, bf16[96,6144]{1,0:T(8,128)(2,1)} %all-gather.5.cloned.1.call-done), kind=kOutput, calls=%fused_computation.1 | convolution fusion | flops 125849600 | bytes 2772992 | tf_op jit(solution)/shard_map/dot_general | solution.py:410
  104.5 1.2 fusion.7.main_ref
  105.7 1.3 shard_map.143
  107.1 7.4 %all-to-all-start.3 = ((bf16[64,8,128]{2,1,0:T(8,128)(2,1)}), bf16[64,8,128]{2,1,0:T(8,128)(2,1)S(1)}, u32[]{:S(2)}, u32[]{:S(2)}) async-start(bf16[64,8,128]{2,1,0:T(8,128)(2,1)} %shard_map.143), calls=%async_computation.4 | async-start | bytes 262144 | tf_op jit(solution)/shard_map/all_to_all | solution.py:34
  114.5 7.4 %reduce-scatter.2.cloned.1.call-done = bf16[1,160,384]{2,1,0:T(8,128)(2,1)} async-done(((bf16[8,160,384]{2,1,0:T(8,128)(2,1)}), bf16[1,160,384]{2,1,0:T(8,128)(2,1)}) %reduce-scatter.2.cloned.1.call-update) | async-done | bytes 122896 | tf_op jit(solution)/shard_map/reduce_scatter | solution.py:408
  124.8 8.1 %all-to-all-start.4 = ((bf16[64,8,128]{2,1,0:T(8,128)(2,1)}), bf16[64,8,128]{2,1,0:T(8,128)(2,1)S(1)}, u32[]{:S(2)}, u32[]{:S(2)}) async-start(bf16[64,8,128]{2,1,0:T(8,128)(2,1)} %get-tuple-element.31), calls=%async_computation.5 | async-start | bytes 262144 | tf_op jit(solution)/shard_map/all_to_all | solution.py:34
  133.1 9.3 %all-to-all-done.4.mixed_ref.chunks_ref = bf16[64,8,128]{2,1,0:T(8,128)(2,1)S(1)} async-done(((bf16[64,8,128]{2,1,0:T(8,128)(2,1)}), bf16[64,8,128]{2,1,0:T(8,128)(2,1)S(1)}, u32[]{:S(2)}, u32[]{:S(2)}) %all-to-all-start.4) | async-done | bytes 131104 | tf_op jit(solution)/shard_map/all_to_all | solution.py:34
  144.1 1.5 shard_map.145
  145.7 8.1 %all-to-all-start.5 = ((bf16[32,22,384]{2,1,0:T(8,128)(2,1)}), bf16[32,22,384]{2,1,0:T(8,128)(2,1)S(1)}, u32[]{:S(2)}, u32[]{:S(2)}) async-start(bf16[32,22,384]{2,1,0:T(8,128)(2,1)} %shard_map.145), calls=%async_computation.6 | async-start | bytes 1179648 | tf_op jit(solution)/shard_map/all_to_all | solution.py:34
  155.6 17.0 %all-to-all-done.5.parcel_ref = bf16[32,22,384]{2,1,0:T(8,128)(2,1)S(1)} async-done(((bf16[32,22,384]{2,1,0:T(8,128)(2,1)}), bf16[32,22,384]{2,1,0:T(8,128)(2,1)S(1)}, u32[]{:S(2)}, u32[]{:S(2)}) %all-to-all-start.5) | async-done | bytes 540704 | tf_op jit(solution)/shard_map/all_to_all | solution.py:34
  172.6 1.4 shard_map.146
  (79 shorter events, 21.4 us)
Async XLA Ops:
  8.0 1.0 copy-start
  8.0 78.3 %all-gather.5.cloned.1.call-start = ((), (), s32[]{:S(2)}) async-start(), calls=%async_computation.9 | async-start | bytes 1253376 | tf_op jit(solution)/shard_map/all_gather | solution.py:391
  13.4 21.3 %all-to-all-start = ((bf16[32,5,384]{2,1,0:T(8,128)(2,1)}), bf16[32,5,384]{2,1,0:T(8,128)(2,1)}, u32[]{:S(2)}, u32[]{:S(2)}) async-start(bf16[32,5,384]{2,1,0:T(8,128)(2,1)} %all_to_all.23), calls=%async_computation | async-start | bytes 393216 | tf_op jit(solution)/shard_map/all_to_all | solution.py:34
  23.6 78.3 %all-gather.3.cloned.1.call-start = ((), (), s32[]{:S(2)}) async-start(), calls=%async_computation.8 | async-start | bytes 2088960 | tf_op jit(solution)/shard_map/all_gather | solution.py:399
  26.1 1.9 %copy-start.1 = (bf16[256,6144]{1,0:T(8,128)(2,1)S(1)}, bf16[256,6144]{1,0:T(8,128)(2,1)}, u32[]{:S(2)}) copy-start(bf16[256,6144]{1,0:T(8,128)(2,1)} %codes_ref.1) | copy-start | bytes 9437188
  30.3 1.2 copy-start.2
  31.5 1.2 copy-start.25
  36.3 85.6 %reduce-scatter.2.cloned.1.call-start = ((), (), s32[]{:S(2)}) async-start(), calls=%async_computation.7 | async-start | bytes 1105920 | tf_op jit(solution)/shard_map/reduce_scatter | solution.py:408
  36.4 43.9 %collective-permute-start.1 = (bf16[8,256,384]{2,1,0:T(8,128)(2,1)}, bf16[8,256,384]{2,1,0:T(8,128)(2,1)S(1)}, u32[]{:S(2)}, u32[]{:S(2)}) collective-permute-start(bf16[8,256,384]{2,1,0:T(8,128)(2,1)} %copy-done.25), channel_id=1, source_target_pairs={{0,1},{1,0},{2,3},{3,2},{4,5},{5,4},{6,7},{7,6},{8,9},{9,8},{10,11... | collective-permute-start | bytes 4718600 | tf_op jit(solution)/shard_map/ppermute | solution.py:405
  77.1 3.2 %collective-permute-start = (bf16[160,256]{1,0:T(8,128)(2,1)S(1)}, bf16[160,256]{1,0:T(8,128)(2,1)S(1)}, u32[]{:S(2)}, u32[]{:S(2)}) collective-permute-start(bf16[160,256]{1,0:T(8,128)(2,1)S(1)} %shard_map.141.rotated_ref), channel_id=1, source_target_pairs={{0,1},{1,0},{2,3},{3,2},{4,5},{5,4},{6,7},{7,6},{8,9},{9,8},{10,11... | collective-permute-start | bytes 245768 | tf_op jit(solution)/shard_map/ppermute | solution.py:406
  80.3 1.4 copy-start.3
  101.9 2.6 %copy-start.26 = (bf16[160,6144]{1,0:T(8,128)(2,1)S(1)}, bf16[160,6144]{1,0:T(8,128)(2,1)}, u32[]{:S(2)}) copy-start(bf16[160,6144]{1,0:T(8,128)(2,1)} %all-gather.3.cloned.1.call-done) | copy-start | bytes 5898244
  104.4 1.2 copy-start.14
  104.4 1.2 copy-start.5
  104.4 1.2 copy-start.9
  104.5 1.2 copy-start.13
  105.7 48.1 %copy-start.6 = (bf16[160,256]{1,0:T(8,128)(2,1)S(1)}, bf16[160,256]{1,0:T(8,128)(2,1)}, u32[]{:S(2)}) copy-start(bf16[160,256]{1,0:T(8,128)(2,1)} %copy-done.4) | copy-start | bytes 245764
  107.1 46.8 %copy-start.15 = (bf16[160,64]{1,0:T(8,128)(2,1)S(1)}, bf16[160,64]{1,0:T(8,128)(2,1)}, u32[]{:S(2)}) copy-start(bf16[160,64]{1,0:T(8,128)(2,1)} %copy-done.14) | copy-start | bytes 61444
  107.1 47.6 %copy-start.20 = (s32[256]{0:T(256)S(1)}, s32[256]{0:T(256)}, u32[]{:S(2)}) copy-start(s32[256]{0:T(256)} %param.13) | copy-start | bytes 3076
  107.1 65.5 %copy-start.22 = (s32[16,2]{0,1:T(2,128)S(1)}, s32[16,2]{0,1:T(2,128)}, u32[]{:S(2)}) copy-start(s32[16,2]{0,1:T(2,128)} %param.16) | copy-start | bytes 388
  107.1 65.5 %copy-start.24 = (f32[16,2]{0,1:T(2,128)S(1)}, f32[16,2]{0,1:T(2,128)}, u32[]{:S(2)}) copy-start(f32[16,2]{0,1:T(2,128)} %param.17) | copy-start | bytes 388
  107.1 16.9 %all-to-all-start.3 = ((bf16[64,8,128]{2,1,0:T(8,128)(2,1)}), bf16[64,8,128]{2,1,0:T(8,128)(2,1)S(1)}, u32[]{:S(2)}, u32[]{:S(2)}) async-start(bf16[64,8,128]{2,1,0:T(8,128)(2,1)} %shard_map.143), calls=%async_computation.4 | async-start | bytes 262144 | tf_op jit(solution)/shard_map/all_to_all | solution.py:34
  124.8 17.6 %all-to-all-start.4 = ((bf16[64,8,128]{2,1,0:T(8,128)(2,1)}), bf16[64,8,128]{2,1,0:T(8,128)(2,1)S(1)}, u32[]{:S(2)}, u32[]{:S(2)}) async-start(bf16[64,8,128]{2,1,0:T(8,128)(2,1)} %get-tuple-element.31), calls=%async_computation.5 | async-start | bytes 262144 | tf_op jit(solution)/shard_map/all_to_all | solution.py:34
  145.7 26.9 %all-to-all-start.5 = ((bf16[32,22,384]{2,1,0:T(8,128)(2,1)}), bf16[32,22,384]{2,1,0:T(8,128)(2,1)S(1)}, u32[]{:S(2)}, u32[]{:S(2)}) async-start(bf16[32,22,384]{2,1,0:T(8,128)(2,1)} %shard_map.145), calls=%async_computation.6 | async-start | bytes 1179648 | tf_op jit(solution)/shard_map/all_to_all | solution.py:34
  (12 other events, 9.0 us)
Sparse Core Ops, SparseCore 0:
  11.1 46.5 all-gather.4
  60.0 41.8 all-gather.2
Sparse Core Ops, SparseCore 1:
  84.9 37.0 reduce-scatter.1
